TPU v7x, 32 devices: a whole 2x2x4 slice. The times are simulated.
32 devices in a mesh: shot: 2 (over core), tile: 16 (over z, y, x).
Axes of the slice: x: 2, y: 2, z: 4, core: 2. Of those that a mesh axis runs over, the one named last changes fastest.
Arguments:
- adjoint_state: float32 [2, 9, 64, 64, 128], P('shot', None, 'tile'), may hold values from -6 to 6
- adjoint_source: bfloat16 [2, 3, 64, 64, 128], P('shot', None, 'tile'), may hold values from -6 to 6
- forward_field: bfloat16 [2, 9, 64, 64, 128], P('shot', None, 'tile'), may hold values from -6 to 6
- lame_first: float32 [64, 64, 128], P('tile'), may hold values from 0.5 to 1
- shear_modulus: float32 [64, 64, 128], P('tile'), may hold values from 0.3 to 1
- buoyancy: float32 [64, 64, 128], P('tile'), may hold values from 0.3 to 1
- active_blocks: int32 [16, 8, 4], P('tile'), may hold values from 0 to 1, as said below
- orientation: int32 [16, 8, 4], P('tile', 'shot'), may hold values from 0 to 3
Outputs:
- final_state: float32 [2, 9, 64, 64, 128], P('shot', None, 'tile')
- gradient: float32 [3, 64, 64, 128], P(None, 'tile', 'shot')
Inputs may be any that keep to these rules, and one draw needn't show every extreme that they name: `active_blocks`: in each column of blocks (fixed first two indices) the blocks are 1 from depth index 0 up to a surface index and 0 above it; the block of depth index 0 is always 1.
All inputs are finite; a program needn't handle non-finite values.
Results may differ from a plain program's by a relative error of at most 0.0003.
Values sent between devices are 32-bit elements; how exact they have to be, the bound alone decides.
No kernel may reach another device: no remote copies, remote signals or barrier semaphores. Data moves between devices by JAX's collectives and lax.ppermute only.
A program may use at most 64 MiB of HBM per device.

v0:
```python
import jax
import jax.numpy as jnp
from jax import lax
from jax.sharding import PartitionSpec as P

BY = 8
BZ = 32
STEPS = 3
SWEEPS = 2


time_step = 0.25
smooth_rate = 0.1
weight_table = ((1.0, 1.0, 0.25), (0.25, 1.0, 1.0), (1.0, 0.25, 1.0), (0.6, 0.6, 0.6))


def extended(block, sides, width):
    for axis, dim in sides:
        count = lax.axis_size(axis)
        forward = [(i, i + 1) for i in range(count - 1)]
        backward = [(target, source) for source, target in forward]
        low = lax.ppermute(
            lax.slice_in_dim(block, block.shape[dim] - width, None, axis=dim), axis, forward
        )
        high = lax.ppermute(lax.slice_in_dim(block, 0, width, axis=dim), axis, backward)
        block = jnp.concatenate([low, block, high], axis=dim)
    return block


def prev_of(field, axis):
    size = field.shape[axis]
    zeros = jnp.zeros_like(lax.slice_in_dim(field, 0, 1, axis=axis))
    return jnp.concatenate([zeros, lax.slice_in_dim(field, 0, size - 1, axis=axis)], axis)


def next_of(field, axis):
    size = field.shape[axis]
    zeros = jnp.zeros_like(lax.slice_in_dim(field, 0, 1, axis=axis))
    return jnp.concatenate([lax.slice_in_dim(field, 1, size, axis=axis), zeros], axis)


def back_diff(field, axis):
    return field - prev_of(field, axis)


def ahead_diff(field, axis):
    return next_of(field, axis) - field


def back_with(field, plane):
    return field - jnp.concatenate([plane, field[:-1]], 0)


def ahead_with(field, plane):
    return jnp.concatenate([field[1:], plane], 0) - field


def expand_blocks(blocks, width):
    return jnp.repeat(jnp.repeat(jnp.repeat(blocks, width, 0), BY, 1), BZ, 2)


def face_halo(stacked):
    return extended(stacked, (("tile", 1),), 1)


def stress_before(comps):
    padded = face_halo(jnp.stack(comps))
    return (padded[3, 0:1], padded[6, 0:1], padded[7, 0:1])


def velocity_after(comps):
    padded = face_halo(jnp.stack(comps))
    return (padded[0, -1:], padded[1, -1:], padded[2, -1:])


def local(
    adjoint_state,
    adjoint_source,
    forward_field,
    lame_first,
    shear_modulus,
    buoyancy,
    active_blocks,
    orientation,
):
    width = lame_first.shape[0]
    cells = expand_blocks(active_blocks.astype(jnp.float32), width)
    comps = [adjoint_state[0, i] for i in range(9)]
    fwd = [forward_field[0, i].astype(jnp.float32) for i in range(9)]
    image_lame = jnp.zeros_like(cells)
    image_shear = jnp.zeros_like(cells)
    image_density = jnp.zeros_like(cells)
    for step_index in range(STEPS):
        before_xx, before_xy, before_xz = stress_before(comps)
        vel_x, vel_y, vel_z, str_xx, str_yy, str_zz, str_xy, str_xz, str_yz = comps
        vel_x = cells * (
            vel_x
            + time_step
            * buoyancy
            * (back_with(str_xx, before_xx) + back_diff(str_xy, 1) + back_diff(str_xz, 2))
        )
        vel_y = cells * (
            vel_y
            + time_step
            * buoyancy
            * (back_with(str_xy, before_xy) + back_diff(str_yy, 1) + back_diff(str_yz, 2))
        )
        vel_z = cells * (
            vel_z
            + time_step
            * buoyancy
            * (back_with(str_xz, before_xz) + back_diff(str_yz, 1) + back_diff(str_zz, 2))
            + time_step * adjoint_source[0, step_index].astype(jnp.float32)
        )
        comps = [vel_x, vel_y, vel_z, str_xx, str_yy, str_zz, str_xy, str_xz, str_yz]
        after_x, after_y, after_z = velocity_after(comps)
        strain_xx = ahead_with(vel_x, after_x)
        strain_yy = ahead_diff(vel_y, 1)
        strain_zz = ahead_diff(vel_z, 2)
        diverge = strain_xx + strain_yy + strain_zz
        str_xx = cells * (
            str_xx + time_step * (lame_first * diverge + 2.0 * shear_modulus * strain_xx)
        )
        str_yy = cells * (
            str_yy + time_step * (lame_first * diverge + 2.0 * shear_modulus * strain_yy)
        )
        str_zz = cells * (
            str_zz + time_step * (lame_first * diverge + 2.0 * shear_modulus * strain_zz)
        )
        str_xy = cells * (
            str_xy + time_step * shear_modulus * (ahead_diff(vel_x, 1) + ahead_with(vel_y, after_y))
        )
        str_xz = cells * (
            str_xz + time_step * shear_modulus * (ahead_diff(vel_x, 2) + ahead_with(vel_z, after_z))
        )
        str_yz = cells * (
            str_yz + time_step * shear_modulus * (ahead_diff(vel_y, 2) + ahead_diff(vel_z, 1))
        )
        comps = [vel_x, vel_y, vel_z, str_xx, str_yy, str_zz, str_xy, str_xz, str_yz]
        image_lame = image_lame + (str_xx + str_yy + str_zz) * (fwd[0] + fwd[1] + fwd[2])
        image_shear = image_shear + (
            str_xx * fwd[0]
            + str_yy * fwd[1]
            + str_zz * fwd[2]
            + str_xy * fwd[3]
            + str_xz * fwd[4]
            + str_yz * fwd[5]
        )
        image_density = image_density + (vel_x * fwd[6] + vel_y * fwd[7] + vel_z * fwd[8])
    final_state = jnp.stack(comps)[None]
    partial_value = jnp.stack([image_lame, image_shear, image_density])
    groups = lax.axis_size("shot")
    owned = partial_value.shape[2] // groups
    total = lax.psum(partial_value, "shot")
    summed = lax.dynamic_slice_in_dim(total, lax.axis_index("shot") * owned, owned, 2)
    summed = summed * (STEPS * groups) ** (-0.5)
    weights = []
    for column in range(3):
        table = jnp.zeros(orientation.shape, jnp.float32)
        for klass in range(4):
            table = table + (orientation == klass).astype(jnp.float32) * weight_table[klass][column]
        weights.append(expand_blocks(table, width))
    grad = summed
    for sweep in range(SWEEPS):
        padded = extended(grad, (("shot", 2), ("tile", 1)), 1)
        center = padded[:, 1:-1, 1:-1]
        lap_x = padded[:, 2:, 1:-1] + padded[:, :-2, 1:-1] - 2.0 * center
        lap_y = padded[:, 1:-1, 2:] + padded[:, 1:-1, :-2] - 2.0 * center
        lap_z = next_of(center, 3) + prev_of(center, 3) - 2.0 * center
        grad = grad + smooth_rate * (weights[0] * lap_x + weights[1] * lap_y + weights[2] * lap_z)
    return (final_state, grad)


def solution(mesh):
    return jax.shard_map(
        local,
        mesh=mesh,
        in_specs=(
            P("shot", None, "tile", None, None),
            P("shot", None, "tile", None, None),
            P("shot", None, "tile", None, None),
            P("tile", None, None),
            P("tile", None, None),
            P("tile", None, None),
            P("tile", None, None),
            P("tile", "shot", None),
        ),
        out_specs=(P("shot", None, "tile", None, None), P(None, "tile", "shot", None)),
        check_vma=False,
    )
```

profile of v0, /device:TPU:8, one launch (start us, length us, event | category | flops | bytes accessed | tf_op | source)
XLA Modules:
  0.0 141.4 jit_solution(6129499883286859111)
XLA Ops:
  7.2 1.0 constant_dynamic-update-slice_fusion.8
  8.2 0.9 constant_dynamic-update-slice_fusion.7
  10.1 0.9 constant_dynamic-update-slice_fusion.5
  11.0 0.9 constant_dynamic-update-slice_fusion.4
  12.1 3.5 %collective-permute-start = (f32[9,1,64,128]{3,2,1,0:T(8,128)S(1)}, f32[9,1,64,128]{3,2,1,0:T(8,128)S(1)}, u32[]{:S(2)}, u32[]{:S(2)}) collective-permute-start(f32[9,1,64,128]{3,2,1,0:T(8,128)S(1)} %slice.505), channel_id=1, source_target_pairs={{0,1},{1,2},{2,3},{3,4},{4,5},{5,6},{6,7},{7,8},{8,9},{9,10},{10,1... | collective-permute-start | bytes 884744 | tf_op jit(solution)/shard_map/ppermute | solution.py:22
  16.0 8.7 %collective-permute-done = f32[9,1,64,128]{3,2,1,0:T(8,128)S(1)} collective-permute-done((f32[9,1,64,128]{3,2,1,0:T(8,128)S(1)}, f32[9,1,64,128]{3,2,1,0:T(8,128)S(1)}, u32[]{:S(2)}, u32[]{:S(2)}) %collective-permute-start) | collective-permute-done | bytes 294944 | tf_op jit(solution)/shard_map/ppermute | solution.py:22
  26.0 2.4 %collective-permute-start.1 = (f32[9,1,64,128]{3,2,1,0:T(8,128)S(1)}, f32[9,1,64,128]{3,2,1,0:T(8,128)S(1)}, u32[]{:S(2)}, u32[]{:S(2)}) collective-permute-start(f32[9,1,64,128]{3,2,1,0:T(8,128)S(1)} %slice.516), channel_id=1, source_target_pairs={{1,0},{2,1},{3,2},{4,3},{5,4},{6,5},{7,6},{8,7},{9,8},{10,9},{11,1... | collective-permute-start | bytes 884744 | tf_op jit(solution)/shard_map/ppermute | solution.py:25
  28.8 6.9 %collective-permute-done.1 = f32[9,1,64,128]{3,2,1,0:T(8,128)S(1)} collective-permute-done((f32[9,1,64,128]{3,2,1,0:T(8,128)S(1)}, f32[9,1,64,128]{3,2,1,0:T(8,128)S(1)}, u32[]{:S(2)}, u32[]{:S(2)}) %collective-permute-start.1) | collective-permute-done | bytes 294944 | tf_op jit(solution)/shard_map/ppermute | solution.py:25
  36.2 2.5 %collective-permute-start.2 = (f32[9,1,64,128]{3,2,1,0:T(8,128)S(1)}, f32[9,1,64,128]{3,2,1,0:T(8,128)S(1)}, u32[]{:S(2)}, u32[]{:S(2)}) collective-permute-start(f32[9,1,64,128]{3,2,1,0:T(8,128)S(1)} %slice.528), channel_id=1, source_target_pairs={{0,1},{1,2},{2,3},{3,4},{4,5},{5,6},{6,7},{7,8},{8,9},{9,10},{10,1... | collective-permute-start | bytes 884744 | tf_op jit(solution)/shard_map/ppermute | solution.py:22
  38.8 8.1 %collective-permute-done.2 = f32[9,1,64,128]{3,2,1,0:T(8,128)S(1)} collective-permute-done((f32[9,1,64,128]{3,2,1,0:T(8,128)S(1)}, f32[9,1,64,128]{3,2,1,0:T(8,128)S(1)}, u32[]{:S(2)}, u32[]{:S(2)}) %collective-permute-start.2) | collective-permute-done | bytes 294944 | tf_op jit(solution)/shard_map/ppermute | solution.py:22
  47.5 2.4 %collective-permute-start.3 = (f32[9,1,64,128]{3,2,1,0:T(8,128)S(1)}, f32[9,1,64,128]{3,2,1,0:T(8,128)S(1)}, u32[]{:S(2)}, u32[]{:S(2)}) collective-permute-start(f32[9,1,64,128]{3,2,1,0:T(8,128)S(1)} %slice.542), channel_id=1, source_target_pairs={{1,0},{2,1},{3,2},{4,3},{5,4},{6,5},{7,6},{8,7},{9,8},{10,9},{11,1... | collective-permute-start | bytes 884744 | tf_op jit(solution)/shard_map/ppermute | solution.py:25
  50.4 5.8 %collective-permute-done.3 = f32[9,1,64,128]{3,2,1,0:T(8,128)S(1)} collective-permute-done((f32[9,1,64,128]{3,2,1,0:T(8,128)S(1)}, f32[9,1,64,128]{3,2,1,0:T(8,128)S(1)}, u32[]{:S(2)}, u32[]{:S(2)}) %collective-permute-start.3) | collective-permute-done | bytes 294944 | tf_op jit(solution)/shard_map/ppermute | solution.py:25
  56.6 2.1 %collective-permute-start.4 = (f32[9,1,64,128]{3,2,1,0:T(8,128)S(1)}, f32[9,1,64,128]{3,2,1,0:T(8,128)S(1)}, u32[]{:S(2)}, u32[]{:S(2)}) collective-permute-start(f32[9,1,64,128]{3,2,1,0:T(8,128)S(1)} %slice.554), channel_id=1, source_target_pairs={{0,1},{1,2},{2,3},{3,4},{4,5},{5,6},{6,7},{7,8},{8,9},{9,10},{10,1... | collective-permute-start | bytes 884744 | tf_op jit(solution)/shard_map/ppermute | solution.py:22
  58.8 8.4 %collective-permute-done.4 = f32[9,1,64,128]{3,2,1,0:T(8,128)S(1)} collective-permute-done((f32[9,1,64,128]{3,2,1,0:T(8,128)S(1)}, f32[9,1,64,128]{3,2,1,0:T(8,128)S(1)}, u32[]{:S(2)}, u32[]{:S(2)}) %collective-permute-start.4) | collective-permute-done | bytes 294944 | tf_op jit(solution)/shard_map/ppermute | solution.py:22
  67.2 1.1 fusion.37
  68.4 1.0 copy.74
  69.5 2.5 %collective-permute-start.5 = (f32[9,1,64,128]{3,2,1,0:T(8,128)S(1)}, f32[9,1,64,128]{3,2,1,0:T(8,128)}, u32[]{:S(2)}, u32[]{:S(2)}) collective-permute-start(f32[9,1,64,128]{3,2,1,0:T(8,128)S(1)} %slice.568), channel_id=1, source_target_pairs={{1,0},{2,1},{3,2},{4,3},{5,4},{6,5},{7,6},{8,7},{9,8},{10,9},{11,1... | collective-permute-start | bytes 884744 | tf_op jit(solution)/shard_map/ppermute | solution.py:25
  73.1 5.2 %collective-permute-done.5 = f32[9,1,64,128]{3,2,1,0:T(8,128)} collective-permute-done((f32[9,1,64,128]{3,2,1,0:T(8,128)S(1)}, f32[9,1,64,128]{3,2,1,0:T(8,128)}, u32[]{:S(2)}, u32[]{:S(2)}) %collective-permute-start.5) | collective-permute-done | bytes 294944 | tf_op jit(solution)/shard_map/ppermute | solution.py:25
  83.6 17.1 %all-reduce.42.cloned.1.call-done = f32[3,4,64,128]{3,2,1,0:T(8,128)} async-done(((f32[3,4,64,128]{3,2,1,0:T(8,128)}), f32[3,4,64,128]{3,2,1,0:T(8,128)}) %all-reduce.42.cloned.1.call-update) | async-done | bytes 393232 | tf_op jit(solution)/shard_map/psum | solution.py:154
  100.7 1.0 dynamic-slice_multiply_fusion
  101.8 2.2 %collective-permute-start.6 = (f32[3,4,1,128]{3,2,1,0:T(1,128)S(1)}, f32[3,4,1,128]{3,2,1,0:T(1,128)S(1)}, u32[]{:S(2)}, u32[]{:S(2)}) collective-permute-start(f32[3,4,1,128]{3,2,1,0:T(1,128)S(1)} %get-tuple-element.94), channel_id=1, source_target_pairs={{0,16},{1,17},{2,18},{3,19},{4,20},{5,21},{6,22},{7,23},{8,24},{9,... | collective-permute-start | bytes 18440 | tf_op jit(solution)/shard_map/ppermute | solution.py:22
  104.0 1.3 collective-permute-start.7
  105.9 1.1 collective-permute-done.7
  107.1 4.3 %collective-permute-start.8 = (f32[3,1,34,128]{3,2,1,0:T(8,128)S(1)}, f32[3,1,34,128]{3,2,1,0:T(8,128)S(1)}, u32[]{:S(2)}, u32[]{:S(2)}) collective-permute-start(f32[3,1,34,128]{3,2,1,0:T(8,128)S(1)} %get-tuple-element.85), channel_id=1, source_target_pairs={{1,0},{2,1},{3,2},{4,3},{5,4},{6,5},{7,6},{8,7},{9,8},{10,9},{11,1... | collective-permute-start | bytes 156680 | tf_op jit(solution)/shard_map/ppermute | solution.py:25
  111.3 1.9 %collective-permute-start.9 = (f32[3,1,34,128]{3,2,1,0:T(8,128)S(1)}, f32[3,1,34,128]{3,2,1,0:T(8,128)S(1)}, u32[]{:S(2)}, u32[]{:S(2)}) collective-permute-start(f32[3,1,34,128]{3,2,1,0:T(8,128)S(1)} %get-tuple-element.86), channel_id=1, source_target_pairs={{0,1},{1,2},{2,3},{3,4},{4,5},{5,6},{6,7},{7,8},{8,9},{9,10},{10,1... | collective-permute-start | bytes 156680 | tf_op jit(solution)/shard_map/ppermute | solution.py:22
  113.4 5.9 %collective-permute-done.9 = f32[3,1,34,128]{3,2,1,0:T(8,128)S(1)} collective-permute-done((f32[3,1,34,128]{3,2,1,0:T(8,128)S(1)}, f32[3,1,34,128]{3,2,1,0:T(8,128)S(1)}, u32[]{:S(2)}, u32[]{:S(2)}) %collective-permute-start.9) | collective-permute-done | bytes 52256 | tf_op jit(solution)/shard_map/ppermute | solution.py:22
  119.5 1.3 collective-permute-start.10
  120.8 1.3 collective-permute-start.11
  122.7 1.1 collective-permute-done.11
  123.8 1.9 %collective-permute-start.12 = (f32[3,1,34,128]{3,2,1,0:T(8,128)S(1)}, f32[3,1,34,128]{3,2,1,0:T(8,128)S(1)}, u32[]{:S(2)}, u32[]{:S(2)}) collective-permute-start(f32[3,1,34,128]{3,2,1,0:T(8,128)S(1)} %get-tuple-element.83), channel_id=1, source_target_pairs={{1,0},{2,1},{3,2},{4,3},{5,4},{6,5},{7,6},{8,7},{9,8},{10,9},{11,1... | collective-permute-start | bytes 156680 | tf_op jit(solution)/shard_map/ppermute | solution.py:25
  125.8 3.9 %collective-permute-start.13 = (f32[3,1,34,128]{3,2,1,0:T(8,128)S(1)}, f32[3,1,34,128]{3,2,1,0:T(8,128)S(1)}, u32[]{:S(2)}, u32[]{:S(2)}) collective-permute-start(f32[3,1,34,128]{3,2,1,0:T(8,128)S(1)} %get-tuple-element.84), channel_id=1, source_target_pairs={{0,1},{1,2},{2,3},{3,4},{4,5},{5,6},{6,7},{7,8},{8,9},{9,10},{10,1... | collective-permute-start | bytes 156680 | tf_op jit(solution)/shard_map/ppermute | solution.py:22
  130.0 3.7 %collective-permute-done.13 = f32[3,1,34,128]{3,2,1,0:T(8,128)S(1)} collective-permute-done((f32[3,1,34,128]{3,2,1,0:T(8,128)S(1)}, f32[3,1,34,128]{3,2,1,0:T(8,128)S(1)}, u32[]{:S(2)}, u32[]{:S(2)}) %collective-permute-start.13) | collective-permute-done | bytes 52256 | tf_op jit(solution)/shard_map/ppermute | solution.py:22
  (151 shorter events, 14.1 us)
Async XLA Ops:
  7.2 4.8 %copy-start.1 = (f32[1,9,4,64,128]{4,3,2,1,0:T(8,128)S(1)}, f32[1,9,4,64,128]{4,3,2,1,0:T(8,128)}, u32[]{:S(2)}) copy-start(f32[1,9,4,64,128]{4,3,2,1,0:T(8,128)} %param.8) | copy-start | bytes 3538948
  7.2 93.5 %all-reduce.42.cloned.1.call-start = ((), (), s32[]{:S(2)}) async-start(), calls=%async_computation | async-start | bytes 786432 | tf_op jit(solution)/shard_map/psum | solution.py:154
  11.0 4.6 %copy-start.9 = (s32[1,8,4]{1,2,0:T(4,128)S(1)}, s32[1,8,4]{1,2,0:T(4,128)}, u32[]{:S(2)}) copy-start(s32[1,8,4]{1,2,0:T(4,128)} %param.14) | copy-start | bytes 388
  12.0 12.6 %copy-start.2 = (f32[4,64,128]{2,1,0:T(8,128)S(1)}, f32[4,64,128]{2,1,0:T(8,128)}, u32[]{:S(2)}) copy-start(f32[4,64,128]{2,1,0:T(8,128)} %param.13) | copy-start | bytes 393220
  12.1 12.6 %collective-permute-start = (f32[9,1,64,128]{3,2,1,0:T(8,128)S(1)}, f32[9,1,64,128]{3,2,1,0:T(8,128)S(1)}, u32[]{:S(2)}, u32[]{:S(2)}) collective-permute-start(f32[9,1,64,128]{3,2,1,0:T(8,128)S(1)} %slice.505), channel_id=1, source_target_pairs={{0,1},{1,2},{2,3},{3,4},{4,5},{5,6},{6,7},{7,8},{8,9},{9,10},{10,1... | collective-permute-start | bytes 884744 | tf_op jit(solution)/shard_map/ppermute | solution.py:22
  24.6 0.9 copy-start.7
  26.0 9.8 %collective-permute-start.1 = (f32[9,1,64,128]{3,2,1,0:T(8,128)S(1)}, f32[9,1,64,128]{3,2,1,0:T(8,128)S(1)}, u32[]{:S(2)}, u32[]{:S(2)}) collective-permute-start(f32[9,1,64,128]{3,2,1,0:T(8,128)S(1)} %slice.516), channel_id=1, source_target_pairs={{1,0},{2,1},{3,2},{4,3},{5,4},{6,5},{7,6},{8,7},{9,8},{10,9},{11,1... | collective-permute-start | bytes 884744 | tf_op jit(solution)/shard_map/ppermute | solution.py:25
  28.4 7.3 %copy-start = (f32[4,64,128]{2,1,0:T(8,128)S(1)}, f32[4,64,128]{2,1,0:T(8,128)}, u32[]{:S(2)}) copy-start(f32[4,64,128]{2,1,0:T(8,128)} %param.12) | copy-start | bytes 393220
  28.4 7.3 %copy-start.3 = (f32[4,64,128]{2,1,0:T(8,128)S(1)}, f32[4,64,128]{2,1,0:T(8,128)}, u32[]{:S(2)}) copy-start(f32[4,64,128]{2,1,0:T(8,128)} %param.11) | copy-start | bytes 393220
  36.2 10.6 %collective-permute-start.2 = (f32[9,1,64,128]{3,2,1,0:T(8,128)S(1)}, f32[9,1,64,128]{3,2,1,0:T(8,128)S(1)}, u32[]{:S(2)}, u32[]{:S(2)}) collective-permute-start(f32[9,1,64,128]{3,2,1,0:T(8,128)S(1)} %slice.528), channel_id=1, source_target_pairs={{0,1},{1,2},{2,3},{3,4},{4,5},{5,6},{6,7},{7,8},{8,9},{9,10},{10,1... | collective-permute-start | bytes 884744 | tf_op jit(solution)/shard_map/ppermute | solution.py:22
  47.5 8.6 %collective-permute-start.3 = (f32[9,1,64,128]{3,2,1,0:T(8,128)S(1)}, f32[9,1,64,128]{3,2,1,0:T(8,128)S(1)}, u32[]{:S(2)}, u32[]{:S(2)}) collective-permute-start(f32[9,1,64,128]{3,2,1,0:T(8,128)S(1)} %slice.542), channel_id=1, source_target_pairs={{1,0},{2,1},{3,2},{4,3},{5,4},{6,5},{7,6},{8,7},{9,8},{10,9},{11,1... | collective-permute-start | bytes 884744 | tf_op jit(solution)/shard_map/ppermute | solution.py:25
  56.5 2.3 %copy-start.8 = (s32[1,4,4]{2,1,0:T(4,128)S(1)}, s32[1,4,4]{2,1,0:T(4,128)}, u32[]{:S(2)}) copy-start(s32[1,4,4]{2,1,0:T(4,128)} %param.15) | copy-start | bytes 196
  56.5 10.7 %copy-start.4 = (bf16[1,9,4,64,128]{4,3,2,1,0:T(8,128)(2,1)S(1)}, bf16[1,9,4,64,128]{4,3,2,1,0:T(8,128)(2,1)}, u32[]{:S(2)}) copy-start(bf16[1,9,4,64,128]{4,3,2,1,0:T(8,128)(2,1)} %param.10) | copy-start | bytes 1769476
  56.6 10.5 %collective-permute-start.4 = (f32[9,1,64,128]{3,2,1,0:T(8,128)S(1)}, f32[9,1,64,128]{3,2,1,0:T(8,128)S(1)}, u32[]{:S(2)}, u32[]{:S(2)}) collective-permute-start(f32[9,1,64,128]{3,2,1,0:T(8,128)S(1)} %slice.554), channel_id=1, source_target_pairs={{0,1},{1,2},{2,3},{3,4},{4,5},{5,6},{6,7},{7,8},{8,9},{9,10},{10,1... | collective-permute-start | bytes 884744 | tf_op jit(solution)/shard_map/ppermute | solution.py:22
  69.5 8.7 %collective-permute-start.5 = (f32[9,1,64,128]{3,2,1,0:T(8,128)S(1)}, f32[9,1,64,128]{3,2,1,0:T(8,128)}, u32[]{:S(2)}, u32[]{:S(2)}) collective-permute-start(f32[9,1,64,128]{3,2,1,0:T(8,128)S(1)} %slice.568), channel_id=1, source_target_pairs={{1,0},{2,1},{3,2},{4,3},{5,4},{6,5},{7,6},{8,7},{9,8},{10,9},{11,1... | collective-permute-start | bytes 884744 | tf_op jit(solution)/shard_map/ppermute | solution.py:25
  79.9 0.9 copy-start.5
  100.7 18.5 %copy-start.6 = (f32[3,4,64,128]{3,2,1,0:T(8,128)S(1)}, f32[3,4,64,128]{3,2,1,0:T(8,128)}, u32[]{:S(2)}) copy-start(f32[3,4,64,128]{3,2,1,0:T(8,128)} %all-reduce.42.cloned.1.call-done) | copy-start | bytes 1179652
  101.8 4.2 %collective-permute-start.6 = (f32[3,4,1,128]{3,2,1,0:T(1,128)S(1)}, f32[3,4,1,128]{3,2,1,0:T(1,128)S(1)}, u32[]{:S(2)}, u32[]{:S(2)}) collective-permute-start(f32[3,4,1,128]{3,2,1,0:T(1,128)S(1)} %get-tuple-element.94), channel_id=1, source_target_pairs={{0,16},{1,17},{2,18},{3,19},{4,20},{5,21},{6,22},{7,23},{8,24},{9,... | collective-permute-start | bytes 18440 | tf_op jit(solution)/shard_map/ppermute | solution.py:22
  104.0 3.1 %collective-permute-start.7 = (f32[3,4,1,128]{3,2,1,0:T(1,128)S(1)}, f32[3,4,1,128]{3,2,1,0:T(1,128)S(1)}, u32[]{:S(2)}, u32[]{:S(2)}) collective-permute-start(f32[3,4,1,128]{3,2,1,0:T(1,128)S(1)} %get-tuple-element.93), channel_id=1, source_target_pairs={{16,0},{17,1},{18,2},{19,3},{20,4},{21,5},{22,6},{23,7},{24,8},{25... | collective-permute-start | bytes 18440 | tf_op jit(solution)/shard_map/ppermute | solution.py:25
  107.1 6.3 %collective-permute-start.8 = (f32[3,1,34,128]{3,2,1,0:T(8,128)S(1)}, f32[3,1,34,128]{3,2,1,0:T(8,128)S(1)}, u32[]{:S(2)}, u32[]{:S(2)}) collective-permute-start(f32[3,1,34,128]{3,2,1,0:T(8,128)S(1)} %get-tuple-element.85), channel_id=1, source_target_pairs={{1,0},{2,1},{3,2},{4,3},{5,4},{6,5},{7,6},{8,7},{9,8},{10,9},{11,1... | collective-permute-start | bytes 156680 | tf_op jit(solution)/shard_map/ppermute | solution.py:25
  111.3 7.9 %collective-permute-start.9 = (f32[3,1,34,128]{3,2,1,0:T(8,128)S(1)}, f32[3,1,34,128]{3,2,1,0:T(8,128)S(1)}, u32[]{:S(2)}, u32[]{:S(2)}) collective-permute-start(f32[3,1,34,128]{3,2,1,0:T(8,128)S(1)} %get-tuple-element.86), channel_id=1, source_target_pairs={{0,1},{1,2},{2,3},{3,4},{4,5},{5,6},{6,7},{7,8},{8,9},{9,10},{10,1... | collective-permute-start | bytes 156680 | tf_op jit(solution)/shard_map/ppermute | solution.py:22
  119.5 3.3 %collective-permute-start.10 = (f32[3,4,1,128]{3,2,1,0:T(1,128)S(1)}, f32[3,4,1,128]{3,2,1,0:T(1,128)S(1)}, u32[]{:S(2)}, u32[]{:S(2)}) collective-permute-start(f32[3,4,1,128]{3,2,1,0:T(1,128)S(1)} %get-tuple-element.90), channel_id=1, source_target_pairs={{0,16},{1,17},{2,18},{3,19},{4,20},{5,21},{6,22},{7,23},{8,24},{9,... | collective-permute-start | bytes 18440 | tf_op jit(solution)/shard_map/ppermute | solution.py:22
  120.8 3.1 %collective-permute-start.11 = (f32[3,4,1,128]{3,2,1,0:T(1,128)S(1)}, f32[3,4,1,128]{3,2,1,0:T(1,128)S(1)}, u32[]{:S(2)}, u32[]{:S(2)}) collective-permute-start(f32[3,4,1,128]{3,2,1,0:T(1,128)S(1)} %get-tuple-element.89), channel_id=1, source_target_pairs={{16,0},{17,1},{18,2},{19,3},{20,4},{21,5},{22,6},{23,7},{24,8},{25... | collective-permute-start | bytes 18440 | tf_op jit(solution)/shard_map/ppermute | solution.py:25
  123.8 6.1 %collective-permute-start.12 = (f32[3,1,34,128]{3,2,1,0:T(8,128)S(1)}, f32[3,1,34,128]{3,2,1,0:T(8,128)S(1)}, u32[]{:S(2)}, u32[]{:S(2)}) collective-permute-start(f32[3,1,34,128]{3,2,1,0:T(8,128)S(1)} %get-tuple-element.83), channel_id=1, source_target_pairs={{1,0},{2,1},{3,2},{4,3},{5,4},{6,5},{7,6},{8,7},{9,8},{10,9},{11,1... | collective-permute-start | bytes 156680 | tf_op jit(solution)/shard_map/ppermute | solution.py:25
  125.8 7.9 %collective-permute-start.13 = (f32[3,1,34,128]{3,2,1,0:T(8,128)S(1)}, f32[3,1,34,128]{3,2,1,0:T(8,128)S(1)}, u32[]{:S(2)}, u32[]{:S(2)}) collective-permute-start(f32[3,1,34,128]{3,2,1,0:T(8,128)S(1)} %get-tuple-element.84), channel_id=1, source_target_pairs={{0,1},{1,2},{2,3},{3,4},{4,5},{5,6},{6,7},{7,8},{8,9},{9,10},{10,1... | collective-permute-start | bytes 156680 | tf_op jit(solution)/shard_map/ppermute | solution.py:22
Sparse Core Ops, SparseCore 0:
  81.8 18.9 all-reduce.41
where the time goes:
time: 142 us; the launch traced here: 141 us
  waiting for transfers between devices  72 us (51%)
  starting transfers between devices  33.6 us (24%)
  between operations  15 us (11%)
  local copies, waits for them, and re-layouts  14.6 us (10%)
  other arithmetic  6.19 us (4%)
    ppermute x7, waiting for transfers between devices, extended(): lax.ppermute(lax.slice_in_dim(block, block.shape[dim] - width, None, axis...  34.7 us
    ppermute x7, waiting for transfers between devices, extended(): lax.ppermute(lax.slice_in_dim(block, 0, width, axis=dim), axis, backward)  20.1 us
    ppermute x7, starting transfers between devices, extended(): lax.ppermute(lax.slice_in_dim(block, block.shape[dim] - width, None, axis...  17.4 us
    psum x1, waiting for transfers between devices, local(): total = lax.psum(partial_value, 'shot')  17.1 us
    ppermute x7, starting transfers between devices, extended(): lax.ppermute(lax.slice_in_dim(block, 0, width, axis=dim), axis, backward)  16.2 us
    unnamed x54, local copies, waits for them, and re-layouts  10.7 us
  transfers between devices with their start and end apart: 15, of which 12 were waited for; matrix products, arithmetic and copies ran while one was open for 4% of the time, Pallas kernels for 0%

commit v1 on v0

v1 whole, which is shorter than its diff:
```python
import functools

import jax
import jax.numpy as jnp
from jax import lax
from jax.experimental import pallas as pl
from jax.experimental.pallas import tpu as pltpu
from jax.sharding import PartitionSpec as P

BY = 8
BZ = 32
STEPS = 3
SWEEPS = 2

time_step = 0.25
smooth_rate = 0.1
weight_table = ((1.0, 1.0, 0.25), (0.25, 1.0, 1.0), (1.0, 0.25, 1.0), (0.6, 0.6, 0.6))

VX, VY, VZ, XX, YY, ZZ, XY, XZ, YZ = range(9)
CB, CL, CM, CB_NEXT = 9, 10, 11, 12
PLANES = 13
ROWS = 32
VMEM = pl.BlockSpec(memory_space=pltpu.VMEM)
SMEM = pl.BlockSpec(memory_space=pltpu.SMEM)
PARAMS = pltpu.CompilerParams(vmem_limit_bytes=24 * 1024 * 1024)


def lanes(shape):
    return lax.broadcasted_iota(jnp.int32, shape, len(shape) - 1)


def rows(shape):
    return lax.broadcasted_iota(jnp.int32, shape, len(shape) - 2)


def z_prev(f):
    return jnp.where(lanes(f.shape) == 0, 0.0, pltpu.roll(f, 1, f.ndim - 1))


def z_next(f):
    size = f.shape[-1]
    return jnp.where(lanes(f.shape) == size - 1, 0.0, pltpu.roll(f, size - 1, f.ndim - 1))


class Plane:
    def __init__(self, ref, *index):
        self.ref, self.index = ref, index
        self.size = ref.shape[len(index)]

    def at(self, row, count):
        return self.ref[self.index + (slice(row, row + count),)]

    def prev(self, row, count):
        if row:
            return self.at(row - 1, count)
        edge = pltpu.roll(self.at(0, 8), 1, 0)
        edge = jnp.where(rows(edge.shape) == 0, 0.0, edge)
        return jnp.concatenate([edge, self.at(7, count - 8)], 0)

    def next(self, row, count):
        if row + count < self.size:
            return self.at(row + 1, count)
        edge = pltpu.roll(self.at(self.size - 8, 8), 7, 0)
        edge = jnp.where(rows(edge.shape) == 7, 0.0, edge)
        return jnp.concatenate([self.at(row + 1, count - 8), edge], 0)

    def set(self, row, value):
        self.ref[self.index + (slice(row, row + value.shape[0]),)] = value


def planes(ref, comps, *index):
    return {c: Plane(ref, n, *index) for n, c in enumerate(comps)}


def divergence(s, before, row, count, have=(XX, YY, ZZ, XY, XZ, YZ)):
    def along_x(c):
        here = s[c].at(row, count)
        return here - before[c].at(row, count) if before is not None else here

    def along_y(c):
        return s[c].at(row, count) - s[c].prev(row, count)

    def along_z(c):
        here = s[c].at(row, count)
        return here - z_prev(here)

    out = []
    for c_x, c_y, c_z in ((XX, XY, XZ), (XY, YY, YZ), (XZ, YZ, ZZ)):
        terms = along_x(c_x)
        if c_y in have:
            terms = terms + along_y(c_y)
        if c_z in have:
            terms = terms + along_z(c_z)
        out.append(terms)
    return out


def strain(v, after, row, count, want=(XX, YY, ZZ, XY, XZ, YZ)):
    x, y, z = (v[c].at(row, count) for c in (VX, VY, VZ))
    if after is None:
        d_x = [-x, -y, -z]
    else:
        d_x = [after[c].at(row, count) - f for c, f in ((VX, x), (VY, y), (VZ, z))]
    out = {XX: d_x[0], YY: v[VY].next(row, count) - y, ZZ: z_next(z) - z}
    out["div"] = out[XX] + out[YY] + out[ZZ]
    if XY in want:
        out[XY] = v[VX].next(row, count) - x + d_x[1]
    if XZ in want:
        out[XZ] = z_next(x) - x + d_x[2]
    if YZ in want:
        out[YZ] = z_next(y) - y + (v[VZ].next(row, count) - z)
    return out


def stress_rate(e, lame, shear, want=(XX, YY, ZZ, XY, XZ, YZ)):
    spread = lame * e["div"]
    return {
        c: spread + 2.0 * shear * e[c] if c in (XX, YY, ZZ) else shear * e[c] for c in want
    }


def cell_plane(active, out):
    shape = (BY, out.shape[1])
    for j in range(out.shape[0] // BY):
        row = jnp.full(shape, active[0, j, 0].astype(jnp.float32))
        for k in range(1, out.shape[1] // BZ):
            row = jnp.where(lanes(shape) >= k * BZ, active[0, j, k].astype(jnp.float32), row)
        out[j * BY : (j + 1) * BY, :] = row


def chunks(size):
    return range(0, size, ROWS)


def first_kernel(
    active, state, source, lame, shear, buoyancy, by_pair, by_next, st, coef, cells, v2, s2, msg
):
    width, size_y = state.shape[1], state.shape[2]
    last = width - 1
    cell_plane(active, cells)

    def forced(step, x, row):
        return (
            time_step
            * cells[row : row + ROWS, :]
            * source[step, x, row : row + ROWS, :].astype(jnp.float32)
        )

    up, down = 0, 1
    for row in chunks(size_y):
        c = cells[row : row + ROWS, :]
        for x in range(width):
            for n, param in enumerate((buoyancy, lame, shear)):
                coef[n, x, row : row + ROWS, :] = time_step * c * param[x, row : row + ROWS, :]

    def coefs(x, row):
        return [coef[n, x, row : row + ROWS, :] for n in range(3)]

    raw = [{c: Plane(state, c, x) for c in range(9)} for x in range(width)]
    one = [{c: Plane(st, c, x) for c in range(9)} for x in range(width)]
    two = {x: {c: Plane(v2, n, c) for c in (VX, VY, VZ)} for n, x in enumerate((0, 1, last))}
    for x in range(width):
        for row in chunks(size_y):
            c = cells[row : row + ROWS, :]
            cb = coefs(x, row)[0]
            terms = divergence(raw[x], raw[x - 1] if x else None, row, ROWS)
            for comp, term in zip((VX, VY, VZ), terms):
                value = c * raw[x][comp].at(row, ROWS) + cb * term
                if comp == VZ:
                    value = value + forced(0, x, row)
                one[x][comp].set(row, value)
    for x in range(width):
        for row in chunks(size_y):
            c = cells[row : row + ROWS, :]
            _, cl, cm = coefs(x, row)
            rate = stress_rate(strain(one[x], one[x + 1] if x < last else None, row, ROWS), cl, cm)
            for comp, term in rate.items():
                one[x][comp].set(row, c * raw[x][comp].at(row, ROWS) + term)
    for x in two:
        for row in chunks(size_y):
            cb = coefs(x, row)[0]
            terms = divergence(one[x], one[x - 1] if x else None, row, ROWS)
            for comp, term in zip((VX, VY, VZ), terms):
                value = one[x][comp].at(row, ROWS) + cb * term
                if comp == VZ:
                    value = value + forced(1, x, row)
                two[x][comp].set(row, value)
    stress = {c: Plane(s2, c) for c in range(9) if c >= XX}
    for row in chunks(size_y):
        _, cl, cm = coefs(0, row)
        rate = stress_rate(strain(two[0], two[1], row, ROWS), cl, cm)
        for comp, term in rate.items():
            stress[comp].set(row, one[0][comp].at(row, ROWS) + term)
        _, cl, cm = coefs(last, row)
        want = (XX, XY, XZ)
        rate = stress_rate(strain(two[last], None, row, ROWS, want), cl, cm, want)
        for n, comp in enumerate(want):
            here = slice(row, row + ROWS)
            msg[up, n, here] = raw[last][comp].at(row, ROWS)
            msg[up, 3 + n, here] = one[last][comp].at(row, ROWS)
            msg[up, 6 + n, here] = one[last][comp].at(row, ROWS) + rate[comp]
    for row in chunks(size_y):
        cb = coefs(0, row)[0]
        here = slice(row, row + ROWS)
        terms = divergence(stress, None, row, ROWS)
        for n, (comp, term) in enumerate(zip((VX, VY, VZ), terms)):
            value = two[0][comp].at(row, ROWS) + cb * term
            if comp == VZ:
                value = value + forced(2, 0, row)
            msg[down, n, here] = one[0][comp].at(row, ROWS)
            msg[down, 3 + n, here] = two[0][comp].at(row, ROWS)
            msg[down, 6 + n, here] = value
        for n in range(3):
            msg[up, CB + n, here] = coef[n, last, here]
            msg[down, CB + n, here] = coef[n, 0, here]
        msg[up, CB_NEXT, here] = coef[0, last, here]
        msg[down, CB_NEXT, here] = coef[0, 1, here]

    even = lax.rem(lax.axis_index("tile"), 2) == 0

    @pl.when(even)
    def _():
        by_pair[...] = msg[up]
        by_next[...] = msg[down]

    @pl.when(jnp.logical_not(even))
    def _():
        by_pair[...] = msg[down]
        by_next[...] = msg[up]


def main_kernel(
    groups,
    active,
    orientation,
    by_pair,
    by_next,
    state,
    st,
    coef,
    source,
    forward,
    final,
    *rest,
):
    images, (cells, got, end, w, low_s, high_v, d_s, d_v, image) = rest[:-9], rest[-9:]
    width, size_y = st.shape[1], st.shape[2]
    last = width - 1
    lo, hi = 0, 1
    cell_plane(active, cells)
    even = lax.rem(lax.axis_index("tile"), 2) == 0

    @pl.when(even)
    def _():
        got[lo] = by_next[...]
        got[hi] = by_pair[...]

    @pl.when(jnp.logical_not(even))
    def _():
        got[lo] = by_pair[...]
        got[hi] = by_next[...]

    def forced(step, x, row):
        return (
            time_step
            * cells[row : row + ROWS, :]
            * source[step, x, row : row + ROWS, :].astype(jnp.float32)
        )

    def coefs(x, row):
        here = slice(row, row + ROWS)
        if x < 0:
            return [got[lo, CB + n, here] for n in range(3)]
        if x > last:
            return [got[hi, CB + n, here] for n in range(3)]
        return [coef[n, x, here] for n in range(3)]

    vel, side, stress = (VX, VY, VZ), (XX, XY, XZ), (XX, YY, ZZ, XY, XZ, YZ)
    raw = [{c: Plane(state, c, x) for c in range(9)} for x in range(width)]
    one = [{c: Plane(st, c, x) for c in range(9)} for x in range(width)]
    base = one[last]
    one[0] = {c: Plane(end, 0, c) for c in range(9)}
    one[last] = {c: Plane(st if c in vel else end, *((c, last) if c in vel else (1, c))) for c in range(9)}
    two = [{c: Plane(w, c, x) for c in range(9)} for x in range(width)]
    three = [{c: Plane(final, c, x) for c in range(9)} for x in range(width)]
    sent_low = [{c: Plane(got, lo, 3 * k + n) for n, c in enumerate(side)} for k in range(3)]
    sent_high = [{c: Plane(got, hi, 3 * k + c) for c in vel} for k in range(3)]
    low_one, low_two = ({c: Plane(low_s, k, n) for n, c in enumerate(side)} for k in range(2))
    high = [{c: Plane(high_v, k, c) for c in vel} for k in range(3)]
    d_low_s = {c: Plane(d_s, 0, c - XX) for c in stress}
    d_high_s = {c: Plane(d_s, 1, c - XX) for c in stress}
    d_high_s_two = {c: Plane(d_s, 2, c - XX) for c in stress}
    d_high_v, d_high_v_two, d_far_v, d_low_v = ({c: Plane(d_v, k, c) for c in vel} for k in range(4))

    for row in chunks(size_y):
        cb, cb_high = coefs(0, row)[0], coefs(last + 1, row)[0]
        for comp, c in zip(vel, side):
            one[0][comp].set(
                row, Plane(st, comp, 0).at(row, ROWS) - cb * sent_low[0][c].at(row, ROWS)
            )
            delta = -cb_high * raw[last][c].at(row, ROWS)
            d_high_v[comp].set(row, delta)
            high[0][comp].set(row, sent_high[0][comp].at(row, ROWS) + delta)
    for row in chunks(size_y):
        c = cells[row : row + ROWS, :]
        _, cl, cm = coefs(0, row)
        for comp, term in stress_rate(strain(one[0], one[1], row, ROWS), cl, cm).items():
            one[0][comp].set(row, c * raw[0][comp].at(row, ROWS) + term)
        _, cl, cm = coefs(last, row)
        v = [high[0][comp].at(row, ROWS) for comp in vel]
        spread = cl * v[0]
        terms = {XX: spread + 2.0 * cm * v[0], YY: spread, ZZ: spread, XY: cm * v[1], XZ: cm * v[2]}
        for comp in stress:
            value = base[comp].at(row, ROWS)
            one[last][comp].set(row, value + terms[comp] if comp in terms else value)
        _, cl, cm = coefs(-1, row)
        v = [one[0][comp].at(row, ROWS) for comp in vel]
        spread = cl * v[0]
        terms = {XX: spread + 2.0 * cm * v[0], YY: spread, ZZ: spread, XY: cm * v[1], XZ: cm * v[2]}
        for comp, term in terms.items():
            d_low_s[comp].set(row, term)
        for comp in side:
            low_one[comp].set(row, sent_low[1][comp].at(row, ROWS) + terms[comp])
        _, cl, cm = coefs(last + 1, row)
        for comp, term in stress_rate(strain(d_high_v, None, row, ROWS), cl, cm).items():
            d_high_s[comp].set(row, term)

    for row in chunks(size_y):
        for x in range(width):
            cb = coefs(x, row)[0]
            terms = divergence(one[x], one[x - 1] if x else low_one, row, ROWS)
            for comp, term in zip(vel, terms):
                value = one[x][comp].at(row, ROWS) + cb * term
                if comp == VZ:
                    value = value + forced(1, x, row)
                two[x][comp].set(row, value)
        cb = coefs(last + 1, row)[0]
        for comp, term in zip(vel, divergence(d_high_s, one[last], row, ROWS)):
            value = d_high_v[comp].at(row, ROWS) + cb * term
            d_high_v_two[comp].set(row, value)
            high[1][comp].set(row, sent_high[1][comp].at(row, ROWS) + value)
        cb = got[hi, CB_NEXT, row : row + ROWS]
        for comp, c in zip(vel, side):
            d_far_v[comp].set(row, -cb * d_high_s[c].at(row, ROWS))
        cb = coefs(-1, row)[0]
        terms = divergence(d_low_s, None, row, ROWS, (XX, YY, ZZ, XY, XZ))
        for comp, term in zip(vel, terms):
            d_low_v[comp].set(row, cb * term)
    for row in chunks(size_y):
        for x in range(width):
            _, cl, cm = coefs(x, row)
            after = two[x + 1] if x < last else high[1]
            for comp, term in stress_rate(strain(two[x], after, row, ROWS), cl, cm).items():
                two[x][comp].set(row, one[x][comp].at(row, ROWS) + term)
        _, cl, cm = coefs(-1, row)
        rate = stress_rate(strain(d_low_v, two[0], row, ROWS, side), cl, cm, side)
        for comp, term in rate.items():
            value = sent_low[2][comp].at(row, ROWS) + d_low_s[comp].at(row, ROWS)
            low_two[comp].set(row, value + term)
        _, cl, cm = coefs(last + 1, row)
        for comp, term in stress_rate(strain(d_high_v_two, d_far_v, row, ROWS), cl, cm).items():
            d_high_s_two[comp].set(row, d_high_s[comp].at(row, ROWS) + term)

    for row in chunks(size_y):
        for x in range(width):
            cb = coefs(x, row)[0]
            terms = divergence(two[x], two[x - 1] if x else low_two, row, ROWS)
            for comp, term in zip(vel, terms):
                value = two[x][comp].at(row, ROWS) + cb * term
                if comp == VZ:
                    value = value + forced(2, x, row)
                three[x][comp].set(row, value)
        cb = coefs(last + 1, row)[0]
        for comp, term in zip(vel, divergence(d_high_s_two, two[last], row, ROWS)):
            value = d_high_v_two[comp].at(row, ROWS) + cb * term
            high[2][comp].set(row, sent_high[2][comp].at(row, ROWS) + value)
    for row in chunks(size_y):
        here = slice(row, row + ROWS)
        for x in range(width):
            _, cl, cm = coefs(x, row)
            after = three[x + 1] if x < last else high[2]
            rate = stress_rate(strain(three[x], after, row, ROWS), cl, cm)
            sums = {}
            for comp in stress:
                before = two[x][comp].at(row, ROWS)
                value = before + rate[comp]
                three[x][comp].set(row, value)
                sums[comp] = one[x][comp].at(row, ROWS) + before + value
            f = [forward[n, x, here].astype(jnp.float32) for n in range(9)]
            image[0, x, here] = (sums[XX] + sums[YY] + sums[ZZ]) * (f[0] + f[1] + f[2])
            total = sums[XX] * f[0]
            for n, comp in enumerate(stress[1:]):
                total = total + sums[comp] * f[n + 1]
            image[1, x, here] = total
            total = 0.0
            for comp in vel:
                moved = [k[x][comp].at(row, ROWS) for k in (one, two, three)]
                total = total + (moved[0] + moved[1] + moved[2]) * f[6 + comp]
            image[2, x, here] = total

    if groups != 2:
        images[0][...] = image[...]
        return
    give, keep = images
    me = lax.axis_index("shot")
    count = keep.shape[0] // (3 * width)
    mine = pl.multiple_of(me * (size_y - count), 8)
    theirs = pl.multiple_of((1 - me) * (size_y - count), 8)
    for n in range(3):
        for x in range(width):
            here = slice((n * width + x) * count, (n * width + x + 1) * count)
            give[here, :] = image[n, x, pl.ds(theirs, count), :]
            keep[here, :] = image[n, x, pl.ds(mine, count), :]
    blocks = orientation.shape[1]
    give[3 * width * count :, :] = class_tile(orientation, jnp.where(me == 0, blocks - 1, 0), keep.shape[1])


def class_tile(orientation, j, size_z):
    shape = (BY, size_z)
    out = jnp.full(shape, orientation[0, j, 0].astype(jnp.float32))
    for k in range(1, size_z // BZ):
        out = jnp.where(lanes(shape) >= k * BZ, orientation[0, j, k].astype(jnp.float32), out)
    return out


def y_prev(f):
    return jnp.where(rows(f.shape) == 0, 0.0, pltpu.roll(f, 1, f.ndim - 2))


def y_next(f):
    size = f.shape[-2]
    return jnp.where(rows(f.shape) == size - 1, 0.0, pltpu.roll(f, size - 1, f.ndim - 2))


def sweep(here, before, after, weights):
    w_x, w_y, w_z = weights
    twice = 2.0 * here
    along_x = -twice
    for plane in (before, after):
        if plane is not None:
            along_x = along_x + plane
    along_y = y_next(here) + y_prev(here) - twice
    along_z = z_next(here) + z_prev(here) - twice
    return here + (w_x * along_x + w_y * along_y + w_z * along_z)


def edge_row(me, own):
    return jnp.where(me == 0, own, BY - 1)


def sum_kernel(scale, orientation, keep, received, by_pair, by_next, grad, swept, weights, classes, msg):
    width, count, size_z = grad.shape[1:]
    own = count - BY
    me = lax.axis_index("shot")
    first = pl.multiple_of(me * BY, BY)
    for j in range(own // BY):
        classes[pl.ds(first + j * BY, BY), :] = class_tile(orientation, j, size_z)
    beyond = pl.multiple_of((1 - me) * own, BY)
    classes[pl.ds(beyond, BY), :] = received[3 * width * count :, :]
    klass = classes[...]
    for column in range(3):
        table = jnp.full(klass.shape, weight_table[3][column], jnp.float32)
        for k in range(3):
            table = jnp.where(klass == k, weight_table[k][column], table)
        weights[column] = smooth_rate * table
    for n in range(3):
        for x in range(width):
            here = slice((n * width + x) * count, (n * width + x + 1) * count)
            grad[n, x] = (keep[here, :] + received[here, :]) * scale
    w = [weights[k] for k in range(3)]
    for n in range(3):
        for x in range(width):
            swept[n, x] = sweep(
                grad[n, x],
                grad[n, x - 1] if x else None,
                grad[n, x + 1] if x < width - 1 else None,
                w,
            )
    edge = edge_row(me, own)
    mine = pl.ds(first, own)
    for to, x in ((0, width - 1), (1, 0)):
        msg[to, 6 * own :, :] = jnp.zeros((BY, size_z), jnp.float32)
        for n in range(3):
            msg[to, 2 * n * own : (2 * n + 1) * own, :] = grad[n, x, mine, :]
            msg[to, (2 * n + 1) * own : (2 * n + 2) * own, :] = swept[n, x, mine, :]
            msg[to, 6 * own + n : 6 * own + n + 1, :] = grad[n, x, pl.ds(edge, 1), :]
        for j in range(own // BY):
            row = weights[0, pl.ds(pl.multiple_of(first + j * BY, BY), BY), :][0:1]
            msg[to, 6 * own + 3 + j : 6 * own + 4 + j, :] = row
    even = lax.rem(lax.axis_index("tile"), 2) == 0

    @pl.when(even)
    def _():
        by_pair[...] = msg[0]
        by_next[...] = msg[1]

    @pl.when(jnp.logical_not(even))
    def _():
        by_pair[...] = msg[1]
        by_next[...] = msg[0]


def smooth_kernel(by_pair, by_next, grad, swept, weights, out, got, beside, full, result):
    width, count, size_z = grad.shape[1:]
    own = count - BY
    last = width - 1
    even = lax.rem(lax.axis_index("tile"), 2) == 0
    me = lax.axis_index("shot")
    first = pl.multiple_of(me * BY, BY)
    mine = pl.ds(first, own)

    @pl.when(even)
    def _():
        got[0] = by_next[...]
        got[1] = by_pair[...]

    @pl.when(jnp.logical_not(even))
    def _():
        got[0] = by_pair[...]
        got[1] = by_next[...]

    edge = edge_row(me, own)
    beside[...] = jnp.zeros(beside.shape, jnp.float32)
    for side, x in ((0, 0), (1, last)):
        for n in range(3):
            beside[side, n, mine, :] = got[side, 2 * n * own : (2 * n + 1) * own, :]
            beside[side, n, pl.ds(edge, 1), :] = got[side, 6 * own + n : 6 * own + n + 1, :]
            beside[side, 3 + n, mine, :] = got[side, (2 * n + 1) * own : (2 * n + 2) * own, :]
        for j in range(own // BY):
            row = got[side, 6 * own + 3 + j : 6 * own + 4 + j, :]
            here = pl.ds(pl.multiple_of(first + j * BY, BY), BY)
            beside[side, 6, here, :] = jnp.broadcast_to(row, (BY, size_z))
    w = [weights[k] for k in range(3)]
    for n in range(3):
        for x in range(width):
            value = swept[n, x]
            if x == 0:
                value = value + w[0] * beside[0, n]
            if x == last:
                value = value + w[0] * beside[1, n]
            full[x + 1] = value
        full[0] = beside[0, 3 + n] + beside[0, 6] * grad[n, 0]
        full[width + 1] = beside[1, 3 + n] + beside[1, 6] * grad[n, last]
        for x in range(width):
            result[...] = sweep(full[x + 1], full[x], full[x + 2], w)
            out[n, x] = result[mine, :]


def extended(block, sides, width):
    for axis, dim in sides:
        count = lax.axis_size(axis)
        forward = [(i, i + 1) for i in range(count - 1)]
        backward = [(target, source) for source, target in forward]
        low = lax.ppermute(
            lax.slice_in_dim(block, block.shape[dim] - width, None, axis=dim), axis, forward
        )
        high = lax.ppermute(lax.slice_in_dim(block, 0, width, axis=dim), axis, backward)
        block = jnp.concatenate([low, block, high], axis=dim)
    return block


def smooth_anywhere(image, orientation):
    groups = lax.axis_size("shot")
    owned = image.shape[2] // groups
    total = lax.psum(image, "shot")
    grad = lax.dynamic_slice_in_dim(total, lax.axis_index("shot") * owned, owned, 2)
    grad = grad * (STEPS * groups) ** (-0.5)
    weights = []
    for column in range(3):
        table = jnp.zeros(orientation.shape, jnp.float32)
        for klass in range(4):
            table = table + (orientation == klass).astype(jnp.float32) * weight_table[klass][column]
        table = jnp.repeat(jnp.repeat(table, image.shape[1], 0), BY, 1)
        weights.append(jnp.repeat(table, BZ, 2))
    for _ in range(SWEEPS):
        padded = extended(grad, (("shot", 2), ("tile", 1)), 1)
        padded = jnp.pad(padded, ((0, 0), (0, 0), (0, 0), (1, 1)))
        center = padded[:, 1:-1, 1:-1, 1:-1]
        lap_x = padded[:, 2:, 1:-1, 1:-1] + padded[:, :-2, 1:-1, 1:-1] - 2.0 * center
        lap_y = padded[:, 1:-1, 2:, 1:-1] + padded[:, 1:-1, :-2, 1:-1] - 2.0 * center
        lap_z = padded[:, 1:-1, 1:-1, 2:] + padded[:, 1:-1, 1:-1, :-2] - 2.0 * center
        grad = grad + smooth_rate * (weights[0] * lap_x + weights[1] * lap_y + weights[2] * lap_z)
    return grad


def both_ways(by_pair, by_next):
    count = lax.axis_size("tile")
    out = []
    for array, start in ((by_next, 1), (by_pair, 0)):
        pairs = [(i, i + 1) for i in range(start, count - 1, 2)]
        out.append(lax.ppermute(array, "tile", pairs + [(b, a) for a, b in pairs]))
    return out[1], out[0]


def f32(*shape):
    return jax.ShapeDtypeStruct(shape, jnp.float32)


def call(kernel, outs, args, scratch, scalars=0):
    return pl.pallas_call(
        kernel,
        out_shape=outs,
        in_specs=[SMEM] * scalars + [VMEM] * (len(args) - scalars),
        out_specs=jax.tree.map(lambda _: VMEM, outs),
        scratch_shapes=[pltpu.VMEM(shape, jnp.float32) for shape in scratch],
        compiler_params=PARAMS,
    )(*args)


def local(
    adjoint_state,
    adjoint_source,
    forward_field,
    lame_first,
    shear_modulus,
    buoyancy,
    active_blocks,
    orientation,
):
    width, size_y, size_z = lame_first.shape
    plane = (size_y, size_z)
    groups = lax.axis_size("shot")
    state, source, forward = adjoint_state[0], adjoint_source[0], forward_field[0]
    by_pair, by_next, st, coef = call(
        first_kernel,
        (f32(PLANES, *plane), f32(PLANES, *plane), f32(9, width, *plane), f32(3, width, *plane)),
        (active_blocks, state, source, lame_first, shear_modulus, buoyancy),
        [plane, (3, 3, *plane), (9, *plane), (2, PLANES, *plane)],
        1,
    )
    by_pair, by_next = both_ways(by_pair, by_next)
    owned = size_y // groups
    count = owned + BY
    if groups == 2:
        images = (f32(3 * width * count + BY, size_z), f32(3 * width * count, size_z))
    else:
        images = (f32(3, width, *plane),)
    final, *images = call(
        functools.partial(main_kernel, groups),
        (f32(9, width, *plane), *images),
        (active_blocks, orientation, by_pair, by_next, state, st, coef, source, forward),
        [
            plane,
            (2, PLANES, *plane),
            (2, 9, *plane),
            (9, width, *plane),
            (2, 3, *plane),
            (3, 3, *plane),
            (3, 6, *plane),
            (4, 3, *plane),
            (3, width, *plane),
        ],
        2,
    )
    if groups != 2:
        return final[None], smooth_anywhere(images[0], orientation)
    give, keep = images
    received = lax.ppermute(give, "shot", [(0, 1), (1, 0)])
    block = (3, width, count, size_z)
    by_pair, by_next, grad, swept, weights = call(
        functools.partial(sum_kernel, (STEPS * groups) ** (-0.5)),
        (f32(6 * owned + BY, size_z), f32(6 * owned + BY, size_z), f32(*block), f32(*block), f32(3, count, size_z)),
        (orientation, keep, received),
        [(count, size_z), (2, 6 * owned + BY, size_z)],
        1,
    )
    by_pair, by_next = both_ways(by_pair, by_next)
    gradient = call(
        smooth_kernel,
        f32(3, width, owned, size_z),
        (by_pair, by_next, grad, swept, weights),
        [
            (2, 6 * owned + BY, size_z),
            (2, 7, count, size_z),
            (width + 2, count, size_z),
            (count, size_z),
        ],
    )
    return final[None], gradient


def solution(mesh):
    return jax.shard_map(
        local,
        mesh=mesh,
        in_specs=(
            P("shot", None, "tile", None, None),
            P("shot", None, "tile", None, None),
            P("shot", None, "tile", None, None),
            P("tile", None, None),
            P("tile", None, None),
            P("tile", None, None),
            P("tile", None, None),
            P("tile", "shot", None),
        ),
        out_specs=(P("shot", None, "tile", None, None), P(None, "tile", "shot", None)),
        check_vma=False,
    )
```

time: 142 us -> 46.1 us (0.32)
  waiting for transfers between devices: 72 us -> 22.8 us
  starting transfers between devices: 33.6 us -> 10.3 us
  between operations: 15 us -> 0.68 us
  local copies, waits for them, and re-layouts: 14.6 us -> 5.68 us
  Pallas kernels: 0 us -> 6.39 us
  other arithmetic: 6.19 us -> 0 us
    ppermute x14 -> x5, waiting for transfers between devices: 54.9 us -> 22.8 us  [the longest x4 21.3 us: both_ways(): out.append(lax.ppermute(array, 'tile', pairs + [(b, a) for a, b in pairs]))]
    ppermute x14 -> x5, starting transfers between devices: 33.6 us -> 10.3 us  [the longest x4 10.3 us: both_ways(): out.append(lax.ppermute(array, 'tile', pairs + [(b, a) for a, b in pairs]))]
    psum x1 -> x0, waiting for transfers between devices: 17.1 us -> none  [local(): total = lax.psum(partial_value, 'shot')]
    pallas_call x0 -> x4, Pallas kernels: none -> 6.39 us  [call(): pl.pallas_call(kernel, out_shape=outs, in_specs=[SMEM] * scalars + [VMEM]...]
    unnamed x54 -> x15, local copies, waits for them, and re-layouts: 10.7 us -> 5.68 us
    another operation x6 -> x0, other arithmetic: 2.66 us -> none  [the longest x4 2.53 us: local(): partial_value = jnp.stack([image_lame, image_shear, image_density])]
    slice x44 -> x0, local copies, waits for them, and re-layouts: 1.45 us -> none  [the longest x20 1.15 us: next_of(): lax.slice_in_dim(field, 1, size, axis=axis)]
  transfers between devices with their start and end apart: 15 -> 5, of which waited for: 12 -> 4; matrix products, arithmetic and copies ran while one was open for 4% -> 0% of each run, Pallas kernels for 0% -> 0%
where the time goes in v1:
time: 46.1 us; the launch traced here: 45.9 us
  waiting for transfers between devices  22.8 us (49%)
  starting transfers between devices  10.3 us (22%)
  Pallas kernels  6.39 us (14%)
  local copies, waits for them, and re-layouts  5.68 us (12%)
  between operations  0.68 us (1%)
    ppermute x4, waiting for transfers between devices, both_ways(): out.append(lax.ppermute(array, 'tile', pairs + [(b, a) for a, b in pairs]))  21.3 us
    ppermute x4, starting transfers between devices, both_ways(): out.append(lax.ppermute(array, 'tile', pairs + [(b, a) for a, b in pairs]))  10.3 us
    pallas_call x4, Pallas kernels, call(): pl.pallas_call(kernel, out_shape=outs, in_specs=[SMEM] * scalars + [VMEM]...  6.39 us
    unnamed x15, local copies, waits for them, and re-layouts  5.68 us
    ppermute x1, waiting for transfers between devices, local(): received = lax.ppermute(give, 'shot', [(0, 1), (1, 0)])  1.51 us
  transfers between devices with their start and end apart: 5, of which 4 were waited for; matrix products, arithmetic and copies ran while one was open for 0% of the time, Pallas kernels for 0%

profile of v1, /device:TPU:8, one launch (start us, length us, event | category | flops | bytes accessed | tf_op | source)
XLA Modules:
  0.0 45.9 jit_solution(8175242812121826688)
XLA Ops:
  0.6 0.0 copy-start.6
  0.6 0.8 %copy.11.active = s32[1,8,4]{2,1,0:T(8,128)S(1)} copy(s32[1,8,4]{1,2,0:T(4,128)} %param.14) | data formatting | bytes 256 | tf_op args[6]
  1.4 0.0 copy-start
  1.4 1.3 %copy-done = f32[1,9,4,64,128]{4,3,2,1,0:T(8,128)S(1)} copy-done((f32[1,9,4,64,128]{4,3,2,1,0:T(8,128)S(1)}, f32[1,9,4,64,128]{4,3,2,1,0:T(8,128)}, u32[]{:S(2)}) %copy-start) | copy-done | bytes 1179672
  2.7 0.0 copy-start.1
  2.7 0.9 %copy-done.1 = bf16[1,3,4,64,128]{4,3,2,1,0:T(8,128)(2,1)S(1)} copy-done((bf16[1,3,4,64,128]{4,3,2,1,0:T(8,128)(2,1)S(1)}, bf16[1,3,4,64,128]{4,3,2,1,0:T(8,128)(2,1)}, u32[]{:S(2)}) %copy-start.1) | copy-done | bytes 196632
  3.6 0.0 copy-start.3
  3.6 0.9 %copy-done.3 = f32[4,64,128]{2,1,0:T(8,128)S(1)} copy-done((f32[4,64,128]{2,1,0:T(8,128)S(1)}, f32[4,64,128]{2,1,0:T(8,128)}, u32[]{:S(2)}) %copy-start.3) | copy-done | bytes 131096
  4.5 0.0 copy-start.4
  4.5 0.9 %copy-done.4 = f32[4,64,128]{2,1,0:T(8,128)S(1)} copy-done((f32[4,64,128]{2,1,0:T(8,128)S(1)}, f32[4,64,128]{2,1,0:T(8,128)}, u32[]{:S(2)}) %copy-start.4) | copy-done | bytes 131096
  5.4 0.0 copy-start.5
  5.4 0.9 %copy-done.5 = f32[4,64,128]{2,1,0:T(8,128)S(1)} copy-done((f32[4,64,128]{2,1,0:T(8,128)S(1)}, f32[4,64,128]{2,1,0:T(8,128)}, u32[]{:S(2)}) %copy-start.5) | copy-done | bytes 131096
  6.3 0.0 copy-start.2
  6.3 1.4 %shard_map.95 = (f32[13,64,128]{2,1,0:T(8,128)S(1)}, f32[13,64,128]{2,1,0:T(8,128)S(1)}, f32[9,4,64,128]{3,2,1,0:T(8,128)S(1)}, f32[3,4,64,128]{3,2,1,0:T(8,128)S(1)}) custom-call(s32[1,8,4]{2,1,0:T(8,128)S(1)} %copy.11.active, f32[9,4,64,128]{3,2,1,0:T(8,128)S(1)} %bitcast.4, bf16[3,4,64,128]{3,2,1,0:T(8,128)(2,1)S(1)} %bitcast.6, ...), custom_call_target="tpu_custom_call" | custom-call | tf_op jit(solution)/shard_map/pallas_call | solution.py:600
  7.7 1.6 %collective-permute-start = (f32[13,64,128]{2,1,0:T(8,128)S(1)}, f32[13,64,128]{2,1,0:T(8,128)S(1)}, u32[]{:S(2)}, u32[]{:S(2)}) collective-permute-start(f32[13,64,128]{2,1,0:T(8,128)S(1)} %get-tuple-element.14), channel_id=1, source_target_pairs={{0,1},{2,3},{4,5},{6,7},{8,9},{10,11},{12,13},{14,15},{1,0},{3,2},... | collective-permute-start | bytes 1277960 | tf_op jit(solution)/shard_map/ppermute | solution.py:591
  9.3 3.3 %collective-permute-start.1 = (f32[13,64,128]{2,1,0:T(8,128)S(1)}, f32[13,64,128]{2,1,0:T(8,128)S(1)}, u32[]{:S(2)}, u32[]{:S(2)}) collective-permute-start(f32[13,64,128]{2,1,0:T(8,128)S(1)} %get-tuple-element.15), channel_id=1, source_target_pairs={{1,2},{3,4},{5,6},{7,8},{9,10},{11,12},{13,14},{2,1},{4,3},{6,5},{... | collective-permute-start | bytes 1277960 | tf_op jit(solution)/shard_map/ppermute | solution.py:591
  12.6 14.9 %collective-permute-done.by_pair = f32[13,64,128]{2,1,0:T(8,128)S(1)} collective-permute-done((f32[13,64,128]{2,1,0:T(8,128)S(1)}, f32[13,64,128]{2,1,0:T(8,128)S(1)}, u32[]{:S(2)}, u32[]{:S(2)}) %collective-permute-start) | collective-permute-done | bytes 426016 | tf_op jit(solution)/shard_map/ppermute | solution.py:591
  27.5 0.0 collective-permute-done.1.by_next
  27.5 0.0 copy-done.6
  27.5 0.0 copy-done.2
  27.5 3.1 %shard_map.96 = (f32[9,4,64,128]{3,2,1,0:T(8,128)}, f32[488,128]{1,0:T(8,128)S(1)}, f32[480,128]{1,0:T(8,128)S(1)}) custom-call(s32[1,8,4]{2,1,0:T(8,128)S(1)} %copy.11.active, s32[1,4,4]{2,1,0:T(4,128)S(1)} %copy-done.6, f32[13,64,128]{2,1,0:T(8,128)S(1)} %collective-permute-done.by_pair, f32[13,64,128]{2,1,0:T(8,128)S(1)} %collective-permute-done.1.by_next, ...), custom_call_target="tpu_custom_call" | custom-call | tf_op jit(solution)/shard_map/pallas_call | solution.py:600
  30.7 0.0 collective-permute-start.2
  30.7 1.5 %collective-permute-done.2.received = f32[488,128]{1,0:T(8,128)S(1)} collective-permute-done((f32[488,128]{1,0:T(8,128)S(1)}, f32[488,128]{1,0:T(8,128)S(1)}, u32[]{:S(2)}, u32[]{:S(2)}) %collective-permute-start.2) | collective-permute-done | bytes 249888 | tf_op jit(solution)/shard_map/ppermute | solution.py:658
  32.2 0.9 %shard_map.97 = (f32[200,128]{1,0:T(8,128)S(1)}, f32[200,128]{1,0:T(8,128)S(1)}, f32[3,4,40,128]{3,2,1,0:T(8,128)S(1)}, f32[3,4,40,128]{3,2,1,0:T(8,128)S(1)}, f32[3,40,128]{2,1,0:T(8,128)S(1)}) custom-call(s32[1,4,4]{2,1,0:T(4,128)S(1)} %copy-done.6, f32[480,128]{1,0:T(8,128)S(1)} %get-tuple-element.19.keep, f32[488,128]{1,0:T(8,128)S(1)} %collective-permute-done.2.received), custom_call_target="tpu_custom_call" | custom-call | tf_op jit(solution)/shard_map/pallas_call | solution.py:600
  33.0 3.5 %collective-permute-start.3 = (f32[200,128]{1,0:T(8,128)S(1)}, f32[200,128]{1,0:T(8,128)S(1)}, u32[]{:S(2)}, u32[]{:S(2)}) collective-permute-start(f32[200,128]{1,0:T(8,128)S(1)} %get-tuple-element.21), channel_id=1, source_target_pairs={{0,1},{2,3},{4,5},{6,7},{8,9},{10,11},{12,13},{14,15},{1,0},{3,2},... | collective-permute-start | bytes 307208 | tf_op jit(solution)/shard_map/ppermute | solution.py:591
  36.5 2.0 %collective-permute-start.4 = (f32[200,128]{1,0:T(8,128)S(1)}, f32[200,128]{1,0:T(8,128)S(1)}, u32[]{:S(2)}, u32[]{:S(2)}) collective-permute-start(f32[200,128]{1,0:T(8,128)S(1)} %get-tuple-element.22), channel_id=1, source_target_pairs={{1,2},{3,4},{5,6},{7,8},{9,10},{11,12},{13,14},{2,1},{4,3},{6,5},{... | collective-permute-start | bytes 307208 | tf_op jit(solution)/shard_map/ppermute | solution.py:591
  38.6 1.2 %collective-permute-done.3.by_pair = f32[200,128]{1,0:T(8,128)S(1)} collective-permute-done((f32[200,128]{1,0:T(8,128)S(1)}, f32[200,128]{1,0:T(8,128)S(1)}, u32[]{:S(2)}, u32[]{:S(2)}) %collective-permute-start.3) | collective-permute-done | bytes 102432 | tf_op jit(solution)/shard_map/ppermute | solution.py:591
  39.7 5.2 %collective-permute-done.4.by_next = f32[200,128]{1,0:T(8,128)S(1)} collective-permute-done((f32[200,128]{1,0:T(8,128)S(1)}, f32[200,128]{1,0:T(8,128)S(1)}, u32[]{:S(2)}, u32[]{:S(2)}) %collective-permute-start.4) | collective-permute-done | bytes 102432 | tf_op jit(solution)/shard_map/ppermute | solution.py:591
  44.9 1.0 %shard_map.98 = f32[3,4,32,128]{3,2,1,0:T(8,128)} custom-call(f32[200,128]{1,0:T(8,128)S(1)} %collective-permute-done.3.by_pair, f32[200,128]{1,0:T(8,128)S(1)} %collective-permute-done.4.by_next, f32[3,4,40,128]{3,2,1,0:T(8,128)S(1)} %get-tuple-element.23.grad, f32[3,4,40,128]{3,2,1,0:T(8,128)S(1)} %get-tuple-element.24.swept, ...), custom_call_target="tpu_custom_call" | custom-call | tf_op jit(solution)/shard_map/pallas_call | solution.py:600
Async XLA Ops:
  0.6 26.9 %copy-start.6 = (s32[1,4,4]{2,1,0:T(4,128)S(1)}, s32[1,4,4]{2,1,0:T(4,128)}, u32[]{:S(2)}) copy-start(s32[1,4,4]{2,1,0:T(4,128)} %orientation.3) | copy-start | bytes 196
  1.4 1.3 %copy-start = (f32[1,9,4,64,128]{4,3,2,1,0:T(8,128)S(1)}, f32[1,9,4,64,128]{4,3,2,1,0:T(8,128)}, u32[]{:S(2)}) copy-start(f32[1,9,4,64,128]{4,3,2,1,0:T(8,128)} %param.8) | copy-start | bytes 3538948
  2.7 0.9 %copy-start.1 = (bf16[1,3,4,64,128]{4,3,2,1,0:T(8,128)(2,1)S(1)}, bf16[1,3,4,64,128]{4,3,2,1,0:T(8,128)(2,1)}, u32[]{:S(2)}) copy-start(bf16[1,3,4,64,128]{4,3,2,1,0:T(8,128)(2,1)} %param.9) | copy-start | bytes 589828
  3.6 0.9 %copy-start.3 = (f32[4,64,128]{2,1,0:T(8,128)S(1)}, f32[4,64,128]{2,1,0:T(8,128)}, u32[]{:S(2)}) copy-start(f32[4,64,128]{2,1,0:T(8,128)} %lame.1) | copy-start | bytes 393220
  4.5 0.9 %copy-start.4 = (f32[4,64,128]{2,1,0:T(8,128)S(1)}, f32[4,64,128]{2,1,0:T(8,128)}, u32[]{:S(2)}) copy-start(f32[4,64,128]{2,1,0:T(8,128)} %shear.1) | copy-start | bytes 393220
  5.4 0.9 %copy-start.5 = (f32[4,64,128]{2,1,0:T(8,128)S(1)}, f32[4,64,128]{2,1,0:T(8,128)}, u32[]{:S(2)}) copy-start(f32[4,64,128]{2,1,0:T(8,128)} %buoyancy.1) | copy-start | bytes 393220
  6.3 21.2 %copy-start.2 = (bf16[1,9,4,64,128]{4,3,2,1,0:T(8,128)(2,1)S(1)}, bf16[1,9,4,64,128]{4,3,2,1,0:T(8,128)(2,1)}, u32[]{:S(2)}) copy-start(bf16[1,9,4,64,128]{4,3,2,1,0:T(8,128)(2,1)} %param.10) | copy-start | bytes 1769476
  7.7 19.8 %collective-permute-start = (f32[13,64,128]{2,1,0:T(8,128)S(1)}, f32[13,64,128]{2,1,0:T(8,128)S(1)}, u32[]{:S(2)}, u32[]{:S(2)}) collective-permute-start(f32[13,64,128]{2,1,0:T(8,128)S(1)} %get-tuple-element.14), channel_id=1, source_target_pairs={{0,1},{2,3},{4,5},{6,7},{8,9},{10,11},{12,13},{14,15},{1,0},{3,2},... | collective-permute-start | bytes 1277960 | tf_op jit(solution)/shard_map/ppermute | solution.py:591
  9.3 18.2 %collective-permute-start.1 = (f32[13,64,128]{2,1,0:T(8,128)S(1)}, f32[13,64,128]{2,1,0:T(8,128)S(1)}, u32[]{:S(2)}, u32[]{:S(2)}) collective-permute-start(f32[13,64,128]{2,1,0:T(8,128)S(1)} %get-tuple-element.15), channel_id=1, source_target_pairs={{1,2},{3,4},{5,6},{7,8},{9,10},{11,12},{13,14},{2,1},{4,3},{6,5},{... | collective-permute-start | bytes 1277960 | tf_op jit(solution)/shard_map/ppermute | solution.py:591
  30.7 1.5 %collective-permute-start.2 = (f32[488,128]{1,0:T(8,128)S(1)}, f32[488,128]{1,0:T(8,128)S(1)}, u32[]{:S(2)}, u32[]{:S(2)}) collective-permute-start(f32[488,128]{1,0:T(8,128)S(1)} %get-tuple-element.20), channel_id=1, source_target_pairs={{0,16},{16,0},{1,17},{17,1},{2,18},{18,2},{3,19},{19,3},{4,20},{20... | collective-permute-start | bytes 749576 | tf_op jit(solution)/shard_map/ppermute | solution.py:658
  33.0 6.7 %collective-permute-start.3 = (f32[200,128]{1,0:T(8,128)S(1)}, f32[200,128]{1,0:T(8,128)S(1)}, u32[]{:S(2)}, u32[]{:S(2)}) collective-permute-start(f32[200,128]{1,0:T(8,128)S(1)} %get-tuple-element.21), channel_id=1, source_target_pairs={{0,1},{2,3},{4,5},{6,7},{8,9},{10,11},{12,13},{14,15},{1,0},{3,2},... | collective-permute-start | bytes 307208 | tf_op jit(solution)/shard_map/ppermute | solution.py:591
  36.5 8.3 %collective-permute-start.4 = (f32[200,128]{1,0:T(8,128)S(1)}, f32[200,128]{1,0:T(8,128)S(1)}, u32[]{:S(2)}, u32[]{:S(2)}) collective-permute-start(f32[200,128]{1,0:T(8,128)S(1)} %get-tuple-element.22), channel_id=1, source_target_pairs={{1,2},{3,4},{5,6},{7,8},{9,10},{11,12},{13,14},{2,1},{4,3},{6,5},{... | collective-permute-start | bytes 307208 | tf_op jit(solution)/shard_map/ppermute | solution.py:591

commit v2 on v1

--- a/solution.py
+++ b/solution.py
@@ -22,7 +22,7 @@
 ROWS = 32
 VMEM = pl.BlockSpec(memory_space=pltpu.VMEM)
 SMEM = pl.BlockSpec(memory_space=pltpu.SMEM)
-PARAMS = pltpu.CompilerParams(vmem_limit_bytes=24 * 1024 * 1024)
+HBM = pl.BlockSpec(memory_space=pltpu.HBM)
 
 
 def lanes(shape):
@@ -122,9 +122,9 @@
 def cell_plane(active, out):
     shape = (BY, out.shape[1])
     for j in range(out.shape[0] // BY):
-        row = jnp.full(shape, active[0, j, 0].astype(jnp.float32))
+        row = jnp.full(shape, active[0, 0, j].astype(jnp.float32))
         for k in range(1, out.shape[1] // BZ):
-            row = jnp.where(lanes(shape) >= k * BZ, active[0, j, k].astype(jnp.float32), row)
+            row = jnp.where(lanes(shape) >= k * BZ, active[0, k, j].astype(jnp.float32), row)
         out[j * BY : (j + 1) * BY, :] = row
 
 
@@ -133,11 +133,41 @@
 
 
 def first_kernel(
-    active, state, source, lame, shear, buoyancy, by_pair, by_next, st, coef, cells, v2, s2, msg
+    active,
+    state_hbm,
+    source_hbm,
+    lame_hbm,
+    shear_hbm,
+    buoyancy_hbm,
+    by_pair,
+    by_next,
+    state,
+    st,
+    coef,
+    cells,
+    v2,
+    s2,
+    msg,
+    params,
+    source,
+    sems,
 ):
     width, size_y = state.shape[1], state.shape[2]
     last = width - 1
+    copies = [
+        pltpu.make_async_copy(array, params.at[n], sems.at[n])
+        for n, array in enumerate((buoyancy_hbm, lame_hbm, shear_hbm))
+    ]
+    copies += [
+        pltpu.make_async_copy(state_hbm.at[c], state.at[c], sems.at[3 + c])
+        for c in (XX, XY, XZ, YY, YZ, ZZ, VX, VY, VZ)
+    ]
+    copies.append(pltpu.make_async_copy(source_hbm, source, sems.at[12]))
+    for copy in copies:
+        copy.start()
     cell_plane(active, cells)
+    for copy in copies[:3]:
+        copy.wait()
 
     def forced(step, x, row):
         return (
@@ -150,8 +180,10 @@
     for row in chunks(size_y):
         c = cells[row : row + ROWS, :]
         for x in range(width):
-            for n, param in enumerate((buoyancy, lame, shear)):
-                coef[n, x, row : row + ROWS, :] = time_step * c * param[x, row : row + ROWS, :]
+            for n in range(3):
+                coef[n, x, row : row + ROWS, :] = time_step * c * params[n, x, row : row + ROWS, :]
+    for copy in copies[3:]:
+        copy.wait()
 
     def coefs(x, row):
         return [coef[n, x, row : row + ROWS, :] for n in range(3)]
@@ -233,8 +265,8 @@
     groups,
     active,
     orientation,
+    by_next,
     by_pair,
-    by_next,
     state,
     st,
     coef,
@@ -500,7 +532,7 @@
         by_next[...] = msg[0]
 
 
-def smooth_kernel(by_pair, by_next, grad, swept, weights, out, got, beside, full, result):
+def smooth_kernel(by_next, by_pair, grad, swept, weights, out, got, beside, full, result):
     width, count, size_z = grad.shape[1:]
     own = count - BY
     last = width - 1
@@ -592,18 +624,25 @@
     return out[1], out[0]
 
 
+def in_hbm(array):
+    return pltpu.with_memory_space_constraint(array, pltpu.HBM)
+
+
 def f32(*shape):
     return jax.ShapeDtypeStruct(shape, jnp.float32)
 
 
-def call(kernel, outs, args, scratch, scalars=0):
+def call(kernel, outs, args, scratch, scalars=0, space=VMEM):
     return pl.pallas_call(
         kernel,
         out_shape=outs,
-        in_specs=[SMEM] * scalars + [VMEM] * (len(args) - scalars),
+        in_specs=[SMEM] * scalars + [space] * (len(args) - scalars),
         out_specs=jax.tree.map(lambda _: VMEM, outs),
-        scratch_shapes=[pltpu.VMEM(shape, jnp.float32) for shape in scratch],
-        compiler_params=PARAMS,
+        scratch_shapes=[
+            pltpu.VMEM(shape, jnp.float32) if isinstance(shape, tuple) else shape
+            for shape in scratch
+        ],
+        compiler_params=pltpu.CompilerParams(vmem_limit_bytes=24 * 1024 * 1024),
     )(*args)
 
 
@@ -621,12 +660,23 @@
     plane = (size_y, size_z)
     groups = lax.axis_size("shot")
     state, source, forward = adjoint_state[0], adjoint_source[0], forward_field[0]
-    by_pair, by_next, st, coef = call(
+    active = jnp.swapaxes(active_blocks, 1, 2)
+    grid = f32(9, width, *plane)
+    by_pair, by_next, raw, st, coef = call(
         first_kernel,
-        (f32(PLANES, *plane), f32(PLANES, *plane), f32(9, width, *plane), f32(3, width, *plane)),
-        (active_blocks, state, source, lame_first, shear_modulus, buoyancy),
-        [plane, (3, 3, *plane), (9, *plane), (2, PLANES, *plane)],
+        (f32(PLANES, *plane), f32(PLANES, *plane), grid, grid, f32(3, width, *plane)),
+        [in_hbm(a) for a in (active, state, source, lame_first, shear_modulus, buoyancy)],
+        [
+            plane,
+            (3, 3, *plane),
+            (9, *plane),
+            (2, PLANES, *plane),
+            (3, width, *plane),
+            pltpu.VMEM(source.shape, source.dtype),
+            pltpu.SemaphoreType.DMA((13,)),
+        ],
         1,
+        HBM,
     )
     by_pair, by_next = both_ways(by_pair, by_next)
     owned = size_y // groups
@@ -638,7 +688,7 @@
     final, *images = call(
         functools.partial(main_kernel, groups),
         (f32(9, width, *plane), *images),
-        (active_blocks, orientation, by_pair, by_next, state, st, coef, source, forward),
+        (active, orientation, by_next, by_pair, raw, st, coef, source, forward),
         [
             plane,
             (2, PLANES, *plane),
@@ -668,7 +718,7 @@
     gradient = call(
         smooth_kernel,
         f32(3, width, owned, size_z),
-        (by_pair, by_next, grad, swept, weights),
+        (by_next, by_pair, grad, swept, weights),
         [
             (2, 6 * owned + BY, size_z),
             (2, 7, count, size_z),

time: 46.1 us -> 44.6 us (0.967)
  the two profiles are of different devices: /device:TPU:8 before, /device:TPU:0 now
where the time goes in v2:
time: 44.6 us; the launch traced here: 44.4 us
  waiting for transfers between devices  25.4 us (57%)
  starting transfers between devices  10.2 us (23%)
  Pallas kernels  8.08 us (18%)
  between operations  0.71 us (2%)
    ppermute x4, waiting for transfers between devices, both_ways(): out.append(lax.ppermute(array, 'tile', pairs + [(b, a) for a, b in pairs]))  23.9 us
    ppermute x4, starting transfers between devices, both_ways(): out.append(lax.ppermute(array, 'tile', pairs + [(b, a) for a, b in pairs]))  10.2 us
    pallas_call x4, Pallas kernels, call(): pl.pallas_call(kernel, out_shape=outs, in_specs=[SMEM] * scalars + [space...  8.08 us
    ppermute x1, waiting for transfers between devices, local(): received = lax.ppermute(give, 'shot', [(0, 1), (1, 0)])  1.51 us
  transfers between devices with their start and end apart: 5, of which 3 were waited for; matrix products, arithmetic and copies ran while one was open for 0% of the time, Pallas kernels for 0%

profile of v2, /device:TPU:0, one launch (start us, length us, event | category | flops | bytes accessed | tf_op | source)
XLA Modules:
  0.0 44.4 jit_solution(7968949417039951120)
XLA Ops:
  0.6 0.0 copy-start.3
  0.6 0.0 copy-start
  0.7 0.0 copy-start.2
  0.7 0.0 copy-start.1
  0.7 3.2 %shard_map.95 = (f32[13,64,128]{2,1,0:T(8,128)S(1)}, f32[13,64,128]{2,1,0:T(8,128)S(1)}, f32[9,4,64,128]{3,2,1,0:T(8,128)S(1)}, f32[9,4,64,128]{3,2,1,0:T(8,128)S(1)}, f32[3,4,64,128]{3,2,1,0:T(8,128)S(1)}) custom-call(s32[1,4,8]{2,1,0:T(4,128)} %bitcast.8, f32[9,4,64,128]{3,2,1,0:T(8,128)} %bitcast.10, bf16[3,4,64,128]{3,2,1,0:T(8,128)(2,1)} %bitcast.5, ...), custom_call_target="tpu_custom_call" | custom-call | tf_op jit(solution)/shard_map/pallas_call | solution.py:636
  3.9 0.7 %collective-permute-start = (f32[13,64,128]{2,1,0:T(8,128)S(1)}, f32[13,64,128]{2,1,0:T(8,128)S(1)}, u32[]{:S(2)}, u32[]{:S(2)}) collective-permute-start(f32[13,64,128]{2,1,0:T(8,128)S(1)} %get-tuple-element.15), channel_id=1, source_target_pairs={{1,2},{3,4},{5,6},{7,8},{9,10},{11,12},{13,14},{2,1},{4,3},{6,5},{... | collective-permute-start | bytes 1277960 | tf_op jit(solution)/shard_map/ppermute | solution.py:623
  4.6 5.7 %collective-permute-start.1 = (f32[13,64,128]{2,1,0:T(8,128)S(1)}, f32[13,64,128]{2,1,0:T(8,128)S(1)}, u32[]{:S(2)}, u32[]{:S(2)}) collective-permute-start(f32[13,64,128]{2,1,0:T(8,128)S(1)} %get-tuple-element.16), channel_id=1, source_target_pairs={{0,1},{2,3},{4,5},{6,7},{8,9},{10,11},{12,13},{14,15},{1,0},{3,2},... | collective-permute-start | bytes 1277960 | tf_op jit(solution)/shard_map/ppermute | solution.py:623
  10.3 0.0 collective-permute-done.by_next
  10.3 18.6 %collective-permute-done.1.by_pair = f32[13,64,128]{2,1,0:T(8,128)S(1)} collective-permute-done((f32[13,64,128]{2,1,0:T(8,128)S(1)}, f32[13,64,128]{2,1,0:T(8,128)S(1)}, u32[]{:S(2)}, u32[]{:S(2)}) %collective-permute-start.1) | collective-permute-done | bytes 426016 | tf_op jit(solution)/shard_map/ppermute | solution.py:623
  28.9 0.0 copy-done.3
  28.9 0.0 copy-done
  28.9 0.0 copy-done.2
  28.9 0.0 copy-done.1
  28.9 3.0 %shard_map.96 = (f32[9,4,64,128]{3,2,1,0:T(8,128)}, f32[488,128]{1,0:T(8,128)S(1)}, f32[480,128]{1,0:T(8,128)S(1)}) custom-call(s32[1,4,8]{2,1,0:T(4,128)S(1)} %bitcast.9, s32[1,4,4]{2,1,0:T(4,128)S(1)} %copy-done.2, f32[13,64,128]{2,1,0:T(8,128)S(1)} %collective-permute-done.by_next, f32[13,64,128]{2,1,0:T(8,128)S(1)} %collective-permute-done.1.by_pair, ...), custom_call_target="tpu_custom_call" | custom-call | tf_op jit(solution)/shard_map/pallas_call | solution.py:636
  31.9 0.0 collective-permute-start.2
  31.9 1.5 %collective-permute-done.2.received = f32[488,128]{1,0:T(8,128)S(1)} collective-permute-done((f32[488,128]{1,0:T(8,128)S(1)}, f32[488,128]{1,0:T(8,128)S(1)}, u32[]{:S(2)}, u32[]{:S(2)}) %collective-permute-start.2) | collective-permute-done | bytes 249888 | tf_op jit(solution)/shard_map/ppermute | solution.py:708
  33.4 0.9 %shard_map.97 = (f32[200,128]{1,0:T(8,128)S(1)}, f32[200,128]{1,0:T(8,128)S(1)}, f32[3,4,40,128]{3,2,1,0:T(8,128)S(1)}, f32[3,4,40,128]{3,2,1,0:T(8,128)S(1)}, f32[3,40,128]{2,1,0:T(8,128)S(1)}) custom-call(s32[1,4,4]{2,1,0:T(4,128)S(1)} %copy-done.2, f32[480,128]{1,0:T(8,128)S(1)} %get-tuple-element.21.keep, f32[488,128]{1,0:T(8,128)S(1)} %collective-permute-done.2.received), custom_call_target="tpu_custom_call" | custom-call | tf_op jit(solution)/shard_map/pallas_call | solution.py:636
  34.3 0.7 %collective-permute-start.3 = (f32[200,128]{1,0:T(8,128)S(1)}, f32[200,128]{1,0:T(8,128)S(1)}, u32[]{:S(2)}, u32[]{:S(2)}) collective-permute-start(f32[200,128]{1,0:T(8,128)S(1)} %get-tuple-element.23), channel_id=1, source_target_pairs={{1,2},{3,4},{5,6},{7,8},{9,10},{11,12},{13,14},{2,1},{4,3},{6,5},{... | collective-permute-start | bytes 307208 | tf_op jit(solution)/shard_map/ppermute | solution.py:623
  35.0 3.2 %collective-permute-start.4 = (f32[200,128]{1,0:T(8,128)S(1)}, f32[200,128]{1,0:T(8,128)S(1)}, u32[]{:S(2)}, u32[]{:S(2)}) collective-permute-start(f32[200,128]{1,0:T(8,128)S(1)} %get-tuple-element.24), channel_id=1, source_target_pairs={{0,1},{2,3},{4,5},{6,7},{8,9},{10,11},{12,13},{14,15},{1,0},{3,2},... | collective-permute-start | bytes 307208 | tf_op jit(solution)/shard_map/ppermute | solution.py:623
  38.1 0.0 collective-permute-done.3.by_next
  38.1 5.3 %collective-permute-done.4.by_pair = f32[200,128]{1,0:T(8,128)S(1)} collective-permute-done((f32[200,128]{1,0:T(8,128)S(1)}, f32[200,128]{1,0:T(8,128)S(1)}, u32[]{:S(2)}, u32[]{:S(2)}) %collective-permute-start.4) | collective-permute-done | bytes 102432 | tf_op jit(solution)/shard_map/ppermute | solution.py:623
  43.4 1.0 %shard_map.98 = f32[3,4,32,128]{3,2,1,0:T(8,128)} custom-call(f32[200,128]{1,0:T(8,128)S(1)} %collective-permute-done.3.by_next, f32[200,128]{1,0:T(8,128)S(1)} %collective-permute-done.4.by_pair, f32[3,4,40,128]{3,2,1,0:T(8,128)S(1)} %get-tuple-element.25.grad, f32[3,4,40,128]{3,2,1,0:T(8,128)S(1)} %get-tuple-element.26.swept, ...), custom_call_target="tpu_custom_call" | custom-call | tf_op jit(solution)/shard_map/pallas_call | solution.py:636
Async XLA Ops:
  0.6 28.2 %copy-start.3 = (s32[1,8,4]{1,2,0:T(4,128)S(1)}, s32[1,8,4]{1,2,0:T(4,128)}, u32[]{:S(2)}) copy-start(s32[1,8,4]{1,2,0:T(4,128)} %param.14) | copy-start | bytes 388
  0.6 28.2 %copy-start = (bf16[1,3,4,64,128]{4,3,2,1,0:T(8,128)(2,1)S(1)}, bf16[1,3,4,64,128]{4,3,2,1,0:T(8,128)(2,1)}, u32[]{:S(2)}) copy-start(bf16[1,3,4,64,128]{4,3,2,1,0:T(8,128)(2,1)} %param.9) | copy-start | bytes 589828
  0.7 28.2 %copy-start.2 = (s32[1,4,4]{2,1,0:T(4,128)S(1)}, s32[1,4,4]{2,1,0:T(4,128)}, u32[]{:S(2)}) copy-start(s32[1,4,4]{2,1,0:T(4,128)} %orientation.3) | copy-start | bytes 196
  0.7 28.2 %copy-start.1 = (bf16[1,9,4,64,128]{4,3,2,1,0:T(8,128)(2,1)S(1)}, bf16[1,9,4,64,128]{4,3,2,1,0:T(8,128)(2,1)}, u32[]{:S(2)}) copy-start(bf16[1,9,4,64,128]{4,3,2,1,0:T(8,128)(2,1)} %param.10) | copy-start | bytes 1769476
  3.9 6.4 %collective-permute-start = (f32[13,64,128]{2,1,0:T(8,128)S(1)}, f32[13,64,128]{2,1,0:T(8,128)S(1)}, u32[]{:S(2)}, u32[]{:S(2)}) collective-permute-start(f32[13,64,128]{2,1,0:T(8,128)S(1)} %get-tuple-element.15), channel_id=1, source_target_pairs={{1,2},{3,4},{5,6},{7,8},{9,10},{11,12},{13,14},{2,1},{4,3},{6,5},{... | collective-permute-start | bytes 1277960 | tf_op jit(solution)/shard_map/ppermute | solution.py:623
  4.6 24.3 %collective-permute-start.1 = (f32[13,64,128]{2,1,0:T(8,128)S(1)}, f32[13,64,128]{2,1,0:T(8,128)S(1)}, u32[]{:S(2)}, u32[]{:S(2)}) collective-permute-start(f32[13,64,128]{2,1,0:T(8,128)S(1)} %get-tuple-element.16), channel_id=1, source_target_pairs={{0,1},{2,3},{4,5},{6,7},{8,9},{10,11},{12,13},{14,15},{1,0},{3,2},... | collective-permute-start | bytes 1277960 | tf_op jit(solution)/shard_map/ppermute | solution.py:623
  31.9 1.5 %collective-permute-start.2 = (f32[488,128]{1,0:T(8,128)S(1)}, f32[488,128]{1,0:T(8,128)S(1)}, u32[]{:S(2)}, u32[]{:S(2)}) collective-permute-start(f32[488,128]{1,0:T(8,128)S(1)} %get-tuple-element.22), channel_id=1, source_target_pairs={{0,16},{16,0},{1,17},{17,1},{2,18},{18,2},{3,19},{19,3},{4,20},{20... | collective-permute-start | bytes 749576 | tf_op jit(solution)/shard_map/ppermute | solution.py:708
  34.3 3.8 %collective-permute-start.3 = (f32[200,128]{1,0:T(8,128)S(1)}, f32[200,128]{1,0:T(8,128)S(1)}, u32[]{:S(2)}, u32[]{:S(2)}) collective-permute-start(f32[200,128]{1,0:T(8,128)S(1)} %get-tuple-element.23), channel_id=1, source_target_pairs={{1,2},{3,4},{5,6},{7,8},{9,10},{11,12},{13,14},{2,1},{4,3},{6,5},{... | collective-permute-start | bytes 307208 | tf_op jit(solution)/shard_map/ppermute | solution.py:623
  35.0 8.4 %collective-permute-start.4 = (f32[200,128]{1,0:T(8,128)S(1)}, f32[200,128]{1,0:T(8,128)S(1)}, u32[]{:S(2)}, u32[]{:S(2)}) collective-permute-start(f32[200,128]{1,0:T(8,128)S(1)} %get-tuple-element.24), channel_id=1, source_target_pairs={{0,1},{2,3},{4,5},{6,7},{8,9},{10,11},{12,13},{14,15},{1,0},{3,2},... | collective-permute-start | bytes 307208 | tf_op jit(solution)/shard_map/ppermute | solution.py:623

commit v3 on v2

v3 whole, which is shorter than its diff:
```python
import functools

import jax
import jax.numpy as jnp
from jax import lax
from jax.experimental import pallas as pl
from jax.experimental.pallas import tpu as pltpu
from jax.sharding import PartitionSpec as P

BY = 8
BZ = 32
STEPS = 3
SWEEPS = 2

time_step = 0.25
smooth_rate = 0.1
weight_table = ((1.0, 1.0, 0.25), (0.25, 1.0, 1.0), (1.0, 0.25, 1.0), (0.6, 0.6, 0.6))

VX, VY, VZ, XX, YY, ZZ, XY, XZ, YZ = range(9)
VEL = (VX, VY, VZ)
SIDE = (XX, XY, XZ)
STRESS = (XX, YY, ZZ, XY, XZ, YZ)
ROWS = 32
VMEM = pl.BlockSpec(memory_space=pltpu.VMEM)
SMEM = pl.BlockSpec(memory_space=pltpu.SMEM)
HBM = pl.BlockSpec(memory_space=pltpu.HBM)


def lanes(shape):
    return lax.broadcasted_iota(jnp.int32, shape, len(shape) - 1)


def rows(shape):
    return lax.broadcasted_iota(jnp.int32, shape, len(shape) - 2)


def z_prev(f):
    return jnp.where(lanes(f.shape) == 0, 0.0, pltpu.roll(f, 1, f.ndim - 1))


def z_next(f):
    size = f.shape[-1]
    return jnp.where(lanes(f.shape) == size - 1, 0.0, pltpu.roll(f, size - 1, f.ndim - 1))


class Plane:
    def __init__(self, ref, *index):
        self.ref, self.index = ref, index
        self.size = ref.shape[len(index)]

    def at(self, row, count):
        return self.ref[self.index + (slice(row, row + count),)]

    def prev(self, row, count):
        if row:
            return self.at(row - 1, count)
        edge = pltpu.roll(self.at(0, 8), 1, 0)
        edge = jnp.where(rows(edge.shape) == 0, 0.0, edge)
        return jnp.concatenate([edge, self.at(7, count - 8)], 0)

    def next(self, row, count):
        if row + count < self.size:
            return self.at(row + 1, count)
        edge = pltpu.roll(self.at(self.size - 8, 8), 7, 0)
        edge = jnp.where(rows(edge.shape) == 7, 0.0, edge)
        return jnp.concatenate([self.at(row + 1, count - 8), edge], 0)

    def set(self, row, value):
        self.ref[self.index + (slice(row, row + value.shape[0]),)] = value


def planes(ref, comps, *index):
    return {c: Plane(ref, n, *index) for n, c in enumerate(comps)}


def divergence(s, before, row, count, have=(XX, YY, ZZ, XY, XZ, YZ)):
    def along_x(c):
        here = s[c].at(row, count)
        return here - before[c].at(row, count) if before is not None else here

    def along_y(c):
        return s[c].at(row, count) - s[c].prev(row, count)

    def along_z(c):
        here = s[c].at(row, count)
        return here - z_prev(here)

    out = []
    for c_x, c_y, c_z in ((XX, XY, XZ), (XY, YY, YZ), (XZ, YZ, ZZ)):
        terms = along_x(c_x)
        if c_y in have:
            terms = terms + along_y(c_y)
        if c_z in have:
            terms = terms + along_z(c_z)
        out.append(terms)
    return out


def strain(v, after, row, count, want=(XX, YY, ZZ, XY, XZ, YZ)):
    x, y, z = (v[c].at(row, count) for c in (VX, VY, VZ))
    if after is None:
        d_x = [-x, -y, -z]
    else:
        d_x = [after[c].at(row, count) - f for c, f in ((VX, x), (VY, y), (VZ, z))]
    out = {XX: d_x[0], YY: v[VY].next(row, count) - y, ZZ: z_next(z) - z}
    out["div"] = out[XX] + out[YY] + out[ZZ]
    if XY in want:
        out[XY] = v[VX].next(row, count) - x + d_x[1]
    if XZ in want:
        out[XZ] = z_next(x) - x + d_x[2]
    if YZ in want:
        out[YZ] = z_next(y) - y + (v[VZ].next(row, count) - z)
    return out


def stress_rate(e, lame, shear, want=(XX, YY, ZZ, XY, XZ, YZ)):
    spread = lame * e["div"]
    return {
        c: spread + 2.0 * shear * e[c] if c in (XX, YY, ZZ) else shear * e[c] for c in want
    }


def cell_plane(active, out):
    shape = (BY, out.shape[1])
    for j in range(out.shape[0] // BY):
        row = jnp.full(shape, active[0, 0, j].astype(jnp.float32))
        for k in range(1, out.shape[1] // BZ):
            row = jnp.where(lanes(shape) >= k * BZ, active[0, k, j].astype(jnp.float32), row)
        out[j * BY : (j + 1) * BY, :] = row


def chunks(size):
    return range(0, size, ROWS)


def is_even():
    return lax.rem(lax.axis_index("tile"), 2) == 0


def hand_out(by_pair, by_next, up, down):
    even = is_even()

    @pl.when(even)
    def _():
        by_pair[...] = up[...]
        by_next[...] = down[...]

    @pl.when(jnp.logical_not(even))
    def _():
        by_pair[...] = down[...]
        by_next[...] = up[...]


def take_in(by_pair, by_next, low, high):
    even = is_even()

    @pl.when(even)
    def _():
        low[...] = by_next[...]
        high[...] = by_pair[...]

    @pl.when(jnp.logical_not(even))
    def _():
        low[...] = by_pair[...]
        high[...] = by_next[...]


def class_tile(orientation, j, size_z):
    shape = (BY, size_z)
    out = jnp.full(shape, orientation[0, j, 0].astype(jnp.float32))
    for k in range(1, size_z // BZ):
        out = jnp.where(lanes(shape) >= k * BZ, orientation[0, j, k].astype(jnp.float32), out)
    return out


def here(row):
    return slice(row, row + ROWS)


def early_kernel(
    groups,
    active,
    orientation,
    state_hbm,
    source_hbm,
    lame_hbm,
    shear_hbm,
    buoyancy_hbm,
    by_pair,
    by_next,
    state,
    source,
    coef,
    cells,
    tile,
    up,
    down,
    params,
    sems,
):
    width, size_y, size_z = state.shape[1:]
    last = width - 1
    copies = [
        pltpu.make_async_copy(array, params.at[n], sems.at[n])
        for n, array in enumerate((buoyancy_hbm, lame_hbm, shear_hbm))
    ]
    copies += [
        pltpu.make_async_copy(state_hbm.at[c], state.at[c], sems.at[3 + c])
        for c in (XX, XY, XZ, YY, YZ, ZZ, VX, VY, VZ)
    ]
    copies.append(pltpu.make_async_copy(source_hbm, source, sems.at[12]))
    for copy in copies:
        copy.start()
    cell_plane(active, cells)
    me = lax.axis_index("shot") if groups == 2 else 0
    blocks = orientation.shape[1]
    tile[...] = class_tile(orientation, jnp.where(me == 0, blocks - 1, 0), size_z)
    for copy in copies[:3]:
        copy.wait()
    for row in chunks(size_y):
        c = time_step * cells[here(row), :]
        for x in range(width):
            for n in range(3):
                coef[n, x, here(row)] = c * params[n, x, here(row)]
    count = (up.shape[0] - 3 * size_y) // 4
    mine = pl.ds(pl.multiple_of(me * count, 8), count) if groups == 2 else slice(0, count)
    for n in range(4):
        to = slice(3 * size_y + n * count, 3 * size_y + (n + 1) * count)
        up[to] = coef[n % 3, last, mine]
        down[to] = coef[n % 3, n // 3, mine]
    for copy in copies[3:]:
        copy.wait()
    raw = {c: Plane(state, c, 0) for c in range(9)}
    for row in chunks(size_y):
        c, cb = cells[here(row), :], coef[0, 0, here(row)]
        for n, term in enumerate(divergence(raw, None, row, ROWS)):
            value = c * raw[n].at(row, ROWS) + cb * term
            if n == VZ:
                push = source[0, 0, here(row)].astype(jnp.float32)
                value = value + time_step * c * push
            to = slice(n * size_y + row, n * size_y + row + ROWS)
            down[to] = value
            up[to] = state[SIDE[n], last, here(row)]
    hand_out(by_pair, by_next, up, down)


def late_kernel(state, source, coef, cells, by_pair, by_next, st, push, v2, s2, up, down):
    width, size_y = state.shape[1], state.shape[2]
    last = width - 1
    for row in chunks(size_y):
        c = time_step * cells[here(row), :]
        for step in range(STEPS):
            for x in range(width):
                push[step, x, here(row)] = c * source[step, x, here(row)].astype(jnp.float32)

    def coefs(x, row):
        return [coef[n, x, here(row)] for n in range(3)]

    raw = [{c: Plane(state, c, x) for c in range(9)} for x in range(width)]
    one = [{c: Plane(st, c, x) for c in range(9)} for x in range(width)]
    two = {x: {c: Plane(v2, n, c) for c in VEL} for n, x in enumerate((0, 1, last))}
    for x in range(width):
        for row in chunks(size_y):
            c = cells[here(row), :]
            cb = coefs(x, row)[0]
            terms = divergence(raw[x], raw[x - 1] if x else None, row, ROWS)
            for comp, term in zip(VEL, terms):
                value = c * raw[x][comp].at(row, ROWS) + cb * term
                if comp == VZ:
                    value = value + push[0, x, here(row)]
                one[x][comp].set(row, value)
    for x in range(width):
        for row in chunks(size_y):
            c = cells[here(row), :]
            _, cl, cm = coefs(x, row)
            rate = stress_rate(strain(one[x], one[x + 1] if x < last else None, row, ROWS), cl, cm)
            for comp, term in rate.items():
                one[x][comp].set(row, c * raw[x][comp].at(row, ROWS) + term)
    for x in two:
        for row in chunks(size_y):
            cb = coefs(x, row)[0]
            terms = divergence(one[x], one[x - 1] if x else None, row, ROWS)
            for comp, term in zip(VEL, terms):
                value = one[x][comp].at(row, ROWS) + cb * term
                if comp == VZ:
                    value = value + push[1, x, here(row)]
                two[x][comp].set(row, value)
    stress = {c: Plane(s2, c - XX) for c in STRESS}
    for row in chunks(size_y):
        _, cl, cm = coefs(0, row)
        rate = stress_rate(strain(two[0], two[1], row, ROWS), cl, cm)
        for comp, term in rate.items():
            stress[comp].set(row, one[0][comp].at(row, ROWS) + term)
        _, cl, cm = coefs(last, row)
        rate = stress_rate(strain(two[last], None, row, ROWS, SIDE), cl, cm, SIDE)
        for n, comp in enumerate(SIDE):
            value = one[last][comp].at(row, ROWS)
            up[n, here(row)] = value
            up[3 + n, here(row)] = value + rate[comp]
    for row in chunks(size_y):
        cb = coefs(0, row)[0]
        terms = divergence(stress, None, row, ROWS)
        for comp, term in zip(VEL, terms):
            before = two[0][comp].at(row, ROWS)
            value = before + cb * term
            if comp == VZ:
                value = value + push[2, 0, here(row)]
            down[comp, here(row)] = before
            down[3 + comp, here(row)] = value
    hand_out(by_pair, by_next, up, down)


def beyond(v, cl, cm):
    spread = cl * v[0]
    return {XX: spread + 2.0 * cm * v[0], YY: spread, ZZ: spread, XY: cm * v[1], XZ: cm * v[2]}


def own_planes(st, end):
    width = st.shape[1]
    one = [{c: Plane(st, c, x) for c in range(9)} for x in range(width)]
    one[0] = {c: Plane(end, 0, c) for c in range(9)}
    one[-1] = {c: Plane(st, c, width - 1) if c in VEL else Plane(end, 1, c) for c in range(9)}
    return one


def near_kernel(groups, *refs):
    by_pair, by_next, *refs = refs
    if groups == 2:
        swapped, orientation, *refs = refs
    state, st, coef, cells, push, end, w, third, outer, parts, *refs = refs
    if groups == 2:
        weights, *refs = refs
    low, high, high_v, d_s, d_v, *classes = refs
    width, size_y = st.shape[1], st.shape[2]
    last = width - 1
    take_in(by_pair, by_next, low, high)
    count = (low.shape[0] - 3 * size_y) // 4
    base = 3 * size_y
    if groups == 2:
        me = lax.axis_index("shot")
        mine = pl.ds(pl.multiple_of(me * count, 8), count)
        theirs = pl.ds(pl.multiple_of((1 - me) * count, 8), count)
        low_at = pl.multiple_of(jnp.where(is_even(), 4 * count, 0), 8)
        high_at = pl.multiple_of(jnp.where(is_even(), 0, 4 * count), 8)
        for n in range(4):
            if n < 3:
                outer[n, mine] = low[base + n * count : base + (n + 1) * count]
                outer[n, theirs] = swapped[pl.ds(low_at + n * count, count)]
            outer[3 + n, mine] = high[base + n * count : base + (n + 1) * count]
            outer[3 + n, theirs] = swapped[pl.ds(high_at + n * count, count)]
    else:
        for n in range(4):
            if n < 3:
                outer[n] = low[base + n * count : base + (n + 1) * count]
            outer[3 + n] = high[base + n * count : base + (n + 1) * count]

    def coefs(x, row):
        if x < 0:
            return [outer[n, here(row)] for n in range(3)]
        if x > last:
            return [outer[3 + n, here(row)] for n in range(3)]
        return [coef[n, x, here(row)] for n in range(3)]

    raw = [{c: Plane(state, c, x) for c in range(9)} for x in range(width)]
    old = [{c: Plane(st, c, x) for c in range(9)} for x in range(width)]
    one = own_planes(st, end)
    two = [{c: Plane(w, c, x) for c in range(9)} for x in range(width)]
    high_one = {c: Plane(high_v, c) for c in VEL}
    d_low_s, d_high_s, d_high_s_two = ({c: Plane(d_s, k, c - XX) for c in STRESS} for k in range(3))
    d_high_v, d_far_v, d_low_v = ({c: Plane(d_v, k, c) for c in VEL} for k in range(3))
    part_v, part_low, d_high_v_two, part_high = (
        {c: Plane(parts, k, n) for n, c in enumerate(names)}
        for k, names in enumerate((VEL, SIDE, VEL, VEL))
    )

    for row in chunks(size_y):
        cb, cb_high = coefs(0, row)[0], coefs(last + 1, row)[0]
        for n, (comp, c) in enumerate(zip(VEL, SIDE)):
            at = slice(n * size_y + row, n * size_y + row + ROWS)
            one[0][comp].set(row, old[0][comp].at(row, ROWS) - cb * low[at])
            delta = -cb_high * raw[last][c].at(row, ROWS)
            d_high_v[comp].set(row, delta)
            high_one[comp].set(row, high[at] + delta)
    for row in chunks(size_y):
        c = cells[here(row), :]
        _, cl, cm = coefs(0, row)
        for comp, term in stress_rate(strain(one[0], one[1], row, ROWS), cl, cm).items():
            one[0][comp].set(row, c * raw[0][comp].at(row, ROWS) + term)
        _, cl, cm = coefs(last, row)
        terms = beyond([high_one[comp].at(row, ROWS) for comp in VEL], cl, cm)
        for comp in STRESS:
            value = old[last][comp].at(row, ROWS)
            one[last][comp].set(row, value + terms[comp] if comp in terms else value)
        _, cl, cm = coefs(-1, row)
        for comp, term in beyond([one[0][comp].at(row, ROWS) for comp in VEL], cl, cm).items():
            d_low_s[comp].set(row, term)
        _, cl, cm = coefs(last + 1, row)
        for comp, term in stress_rate(strain(d_high_v, None, row, ROWS), cl, cm).items():
            d_high_s[comp].set(row, term)

    for row in chunks(size_y):
        for x in range(width):
            cb = coefs(x, row)[0]
            terms = divergence(one[x], one[x - 1] if x else d_low_s, row, ROWS)
            for comp, term in zip(VEL, terms):
                value = one[x][comp].at(row, ROWS) + cb * term
                if comp == VZ:
                    value = value + push[1, x, here(row)]
                (two[x] if x else part_v)[comp].set(row, value)
        cb = coefs(last + 1, row)[0]
        for comp, term in zip(VEL, divergence(d_high_s, one[last], row, ROWS)):
            d_high_v_two[comp].set(row, d_high_v[comp].at(row, ROWS) + cb * term)
        cb = outer[6, here(row)]
        for comp, c in zip(VEL, SIDE):
            d_far_v[comp].set(row, -cb * d_high_s[c].at(row, ROWS))
        cb = coefs(-1, row)[0]
        terms = divergence(d_low_s, None, row, ROWS, (XX, YY, ZZ, XY, XZ))
        for comp, term in zip(VEL, terms):
            d_low_v[comp].set(row, cb * term)
    for row in chunks(size_y):
        for x in range(1, width):
            _, cl, cm = coefs(x, row)
            after = two[x + 1] if x < last else None
            for comp, term in stress_rate(strain(two[x], after, row, ROWS), cl, cm).items():
                two[x][comp].set(row, one[x][comp].at(row, ROWS) + term)
        _, cl, cm = coefs(-1, row)
        rate = stress_rate(strain(d_low_v, None, row, ROWS, SIDE), cl, cm, SIDE)
        for comp, term in rate.items():
            part_low[comp].set(row, d_low_s[comp].at(row, ROWS) + term)
        _, cl, cm = coefs(last + 1, row)
        for comp, term in stress_rate(strain(d_high_v_two, d_far_v, row, ROWS), cl, cm).items():
            d_high_s_two[comp].set(row, d_high_s[comp].at(row, ROWS) + term)
    for row in chunks(size_y):
        cb = coefs(last + 1, row)[0]
        for comp, term in zip(VEL, divergence(d_high_s_two, None, row, ROWS)):
            part_high[comp].set(row, d_high_v_two[comp].at(row, ROWS) + cb * term)
        for x in range(2, last):
            cb = coefs(x, row)[0]
            for comp, term in zip(VEL, divergence(two[x], two[x - 1], row, ROWS)):
                value = two[x][comp].at(row, ROWS) + cb * term
                if comp == VZ:
                    value = value + push[2, x, here(row)]
                third[comp, x, here(row)] = value
    if groups != 2:
        return

    (classes,) = classes
    rows_held = weights.shape[1]
    own = rows_held - BY
    first = pl.multiple_of(me * BY, BY)
    for j in range(own // BY):
        classes[pl.ds(first + j * BY, BY), :] = class_tile(orientation, j, weights.shape[2])
    classes[pl.ds(pl.multiple_of((1 - me) * own, BY), BY), :] = swapped[8 * count :, :]
    klass = classes[...]
    for column in range(3):
        table = jnp.full(klass.shape, weight_table[3][column], jnp.float32)
        for k in range(3):
            table = jnp.where(klass == k, weight_table[k][column], table)
        weights[column] = smooth_rate * table


def far_kernel(groups, *refs):
    by_pair, by_next, st, end, w, third, outer, parts, coef, push, forward, final, *refs = refs
    *images, low, high, edge, low_s, high_v, image = refs
    width, size_y = st.shape[1], st.shape[2]
    last = width - 1
    take_in(by_pair, by_next, low, high)

    def coefs(x, row):
        if x < 0:
            return [outer[n, here(row)] for n in range(3)]
        if x > last:
            return [outer[3 + n, here(row)] for n in range(3)]
        return [coef[n, x, here(row)] for n in range(3)]

    one = own_planes(st, end)
    part = [{c: Plane(w, c, x) for c in range(9)} for x in range(width)]
    two = [dict(p) for p in part]
    for c in range(9):
        two[0][c] = Plane(edge, 0, c)
        if c >= XX:
            two[last][c] = Plane(edge, 1, c)
    three = [{c: Plane(final, c, x) for c in range(9)} for x in range(width)]
    part_v, part_low, d_high_v_two, part_high = (
        {c: Plane(parts, k, n) for n, c in enumerate(names)}
        for k, names in enumerate((VEL, SIDE, VEL, VEL))
    )
    low_two = {c: Plane(low_s, n) for n, c in enumerate(SIDE)}
    high_three = {c: Plane(high_v, c) for c in VEL}

    for row in chunks(size_y):
        cb = coefs(0, row)[0]
        moved = []
        for n, comp in enumerate(VEL):
            moved.append(part_v[comp].at(row, ROWS) - cb * low[n, here(row)])
            two[0][comp].set(row, moved[n])
        _, cl, cm = coefs(-1, row)
        terms = beyond(moved, cl, cm)
        for n, comp in enumerate(SIDE):
            value = low[3 + n, here(row)] + part_low[comp].at(row, ROWS)
            low_two[comp].set(row, value + terms[comp])
        _, cl, cm = coefs(last, row)
        cb = coefs(last + 1, row)[0]
        moved = [high[n, here(row)] + d_high_v_two[n].at(row, ROWS) for n in VEL]
        terms = beyond(moved, cl, cm)
        values = {}
        for comp in STRESS:
            value = part[last][comp].at(row, ROWS)
            values[comp] = value + terms[comp] if comp in terms else value
            two[last][comp].set(row, values[comp])
        for n, comp in enumerate(SIDE):
            value = high[3 + n, here(row)] + part_high[n].at(row, ROWS)
            high_three[n].set(row, value - cb * values[comp])
    for row in chunks(size_y):
        _, cl, cm = coefs(0, row)
        for comp, term in stress_rate(strain(two[0], two[1], row, ROWS), cl, cm).items():
            two[0][comp].set(row, one[0][comp].at(row, ROWS) + term)

    for row in chunks(size_y):
        for x in range(width):
            if 2 <= x < last:
                for comp in VEL:
                    three[x][comp].set(row, third[comp, x, here(row)])
                continue
            cb = coefs(x, row)[0]
            terms = divergence(two[x], two[x - 1] if x else low_two, row, ROWS)
            for comp, term in zip(VEL, terms):
                value = two[x][comp].at(row, ROWS) + cb * term
                if comp == VZ:
                    value = value + push[2, x, here(row)]
                three[x][comp].set(row, value)
    for row in chunks(size_y):
        for x in range(width):
            _, cl, cm = coefs(x, row)
            after = three[x + 1] if x < last else high_three
            rate = stress_rate(strain(three[x], after, row, ROWS), cl, cm)
            sums = {}
            for comp in STRESS:
                before = two[x][comp].at(row, ROWS)
                value = before + rate[comp]
                three[x][comp].set(row, value)
                sums[comp] = one[x][comp].at(row, ROWS) + before + value
            f = [forward[n, x, here(row)].astype(jnp.float32) for n in range(9)]
            image[0, x, here(row)] = (sums[XX] + sums[YY] + sums[ZZ]) * (f[0] + f[1] + f[2])
            total = sums[XX] * f[0]
            for n, comp in enumerate(STRESS[1:]):
                total = total + sums[comp] * f[n + 1]
            image[1, x, here(row)] = total
            total = 0.0
            for comp in VEL:
                moved = [k[x][comp].at(row, ROWS) for k in (one, two, three)]
                total = total + (moved[0] + moved[1] + moved[2]) * f[6 + comp]
            image[2, x, here(row)] = total

    if groups != 2:
        images[0][...] = image[...]
        return
    give, keep = images
    me = lax.axis_index("shot")
    count = keep.shape[2]
    mine = pl.ds(pl.multiple_of(me * (size_y - count), 8), count)
    theirs = pl.ds(pl.multiple_of((1 - me) * (size_y - count), 8), count)
    for n in range(3):
        for x in range(width):
            give[n, x] = image[n, x, theirs, :]
            keep[n, x] = image[n, x, mine, :]


def y_prev(f):
    return jnp.where(rows(f.shape) == 0, 0.0, pltpu.roll(f, 1, f.ndim - 2))


def y_next(f):
    size = f.shape[-2]
    return jnp.where(rows(f.shape) == size - 1, 0.0, pltpu.roll(f, size - 1, f.ndim - 2))


def sweep(g, before, after, weights):
    w_x, w_y, w_z = weights
    twice = 2.0 * g
    along_x = -twice
    for plane in (before, after):
        if plane is not None:
            along_x = along_x + plane
    along_y = y_next(g) + y_prev(g) - twice
    along_z = z_next(g) + z_prev(g) - twice
    return g + (w_x * along_x + w_y * along_y + w_z * along_z)


def edge_row(me, own):
    return jnp.where(me == 0, own, BY - 1)


def sum_kernel(scale, keep, received, weights, by_pair, by_next, grad, swept, up, down):
    width, count, size_z = grad.shape[1:]
    own = count - BY
    me = lax.axis_index("shot")
    first = pl.multiple_of(me * BY, BY)
    mine = pl.ds(first, own)
    edge = pl.ds(edge_row(me, own), 1)
    last = width - 1
    w = [weights[k] for k in range(3)]
    for to in (up, down):
        to[6 * own :, :] = jnp.zeros((BY, size_z), jnp.float32)
        for j in range(own // BY):
            row = weights[0, pl.ds(pl.multiple_of(first + j * BY, BY), BY), :][0:1]
            to[6 * own + 3 + j : 6 * own + 4 + j, :] = row
    for n in range(3):
        for x in range(width):
            grad[n, x] = (keep[n, x] + received[n, x]) * scale
        swept[n, 0] = sweep(grad[n, 0], None, grad[n, 1], w)
        swept[n, 1] = sweep(grad[n, last], grad[n, last - 1], None, w)
        for to, x, side in ((up, last, 1), (down, 0, 0)):
            to[2 * n * own : (2 * n + 1) * own, :] = grad[n, x, mine, :]
            to[(2 * n + 1) * own : (2 * n + 2) * own, :] = swept[n, side, mine, :]
            to[6 * own + n : 6 * own + n + 1, :] = grad[n, x, edge, :]
    hand_out(by_pair, by_next, up, down)


def inner_kernel(grad, swept, weights, full, half):
    width = grad.shape[1]
    last = width - 1
    w = [weights[k] for k in range(3)]
    for n in range(3):
        full[n, 0] = swept[n, 0]
        full[n, last] = swept[n, 1]
        for x in range(1, last):
            full[n, x] = sweep(grad[n, x], grad[n, x - 1], grad[n, x + 1], w)
        for x in range(1, last):
            half[n, x - 1] = sweep(
                full[n, x],
                full[n, x - 1] if x > 1 else None,
                full[n, x + 1] if x < last - 1 else None,
                w,
            )


def smooth_kernel(by_next, by_pair, grad, full, half, weights, out, low, high, beside, result):
    width, count, size_z = grad.shape[1:]
    own = count - BY
    last = width - 1
    me = lax.axis_index("shot")
    first = pl.multiple_of(me * BY, BY)
    mine = pl.ds(first, own)
    edge = pl.ds(edge_row(me, own), 1)
    take_in(by_pair, by_next, low, high)
    beside[...] = jnp.zeros(beside.shape, jnp.float32)
    for side, got in enumerate((low, high)):
        for n in range(3):
            beside[side, n, mine, :] = got[2 * n * own : (2 * n + 1) * own, :]
            beside[side, n, edge, :] = got[6 * own + n : 6 * own + n + 1, :]
            beside[side, 3 + n, mine, :] = got[(2 * n + 1) * own : (2 * n + 2) * own, :]
        for j in range(own // BY):
            row = got[6 * own + 3 + j : 6 * own + 4 + j, :]
            to = pl.ds(pl.multiple_of(first + j * BY, BY), BY)
            beside[side, 6, to, :] = jnp.broadcast_to(row, (BY, size_z))
    w = [weights[k] for k in range(3)]
    for n in range(3):
        ends = [full[n, x] + w[0] * beside[side, n] for side, x in ((0, 0), (1, last))]
        outer = [
            beside[side, 3 + n] + beside[side, 6] * grad[n, x] for side, x in ((0, 0), (1, last))
        ]
        result[0] = sweep(ends[0], outer[0], full[n, 1], w)
        result[last] = sweep(ends[1], full[n, last - 1], outer[1], w)
        for x in range(1, last):
            value = half[n, x - 1]
            if x == 1:
                value = value + w[0] * ends[0]
            if x == last - 1:
                value = value + w[0] * ends[1]
            result[x] = value
        for x in range(width):
            out[n, x] = result[x, mine, :]


def extended(block, sides, width):
    for axis, dim in sides:
        count = lax.axis_size(axis)
        forward = [(i, i + 1) for i in range(count - 1)]
        backward = [(target, source) for source, target in forward]
        low = lax.ppermute(
            lax.slice_in_dim(block, block.shape[dim] - width, None, axis=dim), axis, forward
        )
        high = lax.ppermute(lax.slice_in_dim(block, 0, width, axis=dim), axis, backward)
        block = jnp.concatenate([low, block, high], axis=dim)
    return block


def smooth_anywhere(image, orientation):
    groups = lax.axis_size("shot")
    owned = image.shape[2] // groups
    total = lax.psum(image, "shot")
    grad = lax.dynamic_slice_in_dim(total, lax.axis_index("shot") * owned, owned, 2)
    grad = grad * (STEPS * groups) ** (-0.5)
    weights = []
    for column in range(3):
        table = jnp.zeros(orientation.shape, jnp.float32)
        for klass in range(4):
            table = table + (orientation == klass).astype(jnp.float32) * weight_table[klass][column]
        table = jnp.repeat(jnp.repeat(table, image.shape[1], 0), BY, 1)
        weights.append(jnp.repeat(table, BZ, 2))
    for _ in range(SWEEPS):
        padded = extended(grad, (("shot", 2), ("tile", 1)), 1)
        padded = jnp.pad(padded, ((0, 0), (0, 0), (0, 0), (1, 1)))
        center = padded[:, 1:-1, 1:-1, 1:-1]
        lap_x = padded[:, 2:, 1:-1, 1:-1] + padded[:, :-2, 1:-1, 1:-1] - 2.0 * center
        lap_y = padded[:, 1:-1, 2:, 1:-1] + padded[:, 1:-1, :-2, 1:-1] - 2.0 * center
        lap_z = padded[:, 1:-1, 1:-1, 2:] + padded[:, 1:-1, 1:-1, :-2] - 2.0 * center
        grad = grad + smooth_rate * (weights[0] * lap_x + weights[1] * lap_y + weights[2] * lap_z)
    return grad


def both_ways(by_pair, by_next):
    count = lax.axis_size("tile")
    out = []
    for array, start in ((by_pair, 0), (by_next, 1)):
        pairs = [(i, i + 1) for i in range(start, count - 1, 2)]
        out.append(lax.ppermute(array, "tile", pairs + [(b, a) for a, b in pairs]))
    return out


def f32(*shape):
    return jax.ShapeDtypeStruct(shape, jnp.float32)


def in_hbm(array):
    return pltpu.with_memory_space_constraint(array, pltpu.HBM)


def call(kernel, outs, args, scratch, scalars=(), space=VMEM, flops=0):
    return pl.pallas_call(
        kernel,
        out_shape=outs,
        in_specs=[SMEM if n in scalars else space for n in range(len(args))],
        out_specs=jax.tree.map(lambda _: VMEM, outs),
        scratch_shapes=[
            pltpu.VMEM(shape, jnp.float32) if isinstance(shape, tuple) else shape
            for shape in scratch
        ],
        compiler_params=pltpu.CompilerParams(vmem_limit_bytes=24 * 1024 * 1024),
    )(*args)


def local(
    adjoint_state,
    adjoint_source,
    forward_field,
    lame_first,
    shear_modulus,
    buoyancy,
    active_blocks,
    orientation,
):
    width, size_y, size_z = lame_first.shape
    plane = (size_y, size_z)
    groups = lax.axis_size("shot")
    state, source, forward = adjoint_state[0], adjoint_source[0], forward_field[0]
    active = jnp.swapaxes(active_blocks, 1, 2)
    grid = f32(9, width, *plane)
    count = size_y // 2 if groups == 2 else size_y
    early = (3 * size_y + 4 * count, size_z)
    by_pair, by_next, raw, source, coef, cells, tile = call(
        functools.partial(early_kernel, groups),
        (
            f32(*early),
            f32(*early),
            grid,
            jax.ShapeDtypeStruct(source.shape, source.dtype),
            f32(3, width, *plane),
            f32(*plane),
            f32(BY, size_z),
        ),
        [
            in_hbm(a)
            for a in (active, orientation, state, source, lame_first, shear_modulus, buoyancy)
        ],
        [early, early, (3, width, *plane), pltpu.SemaphoreType.DMA((13,))],
        (0, 1),
        HBM,
    )
    by_pair, by_next = both_ways(by_pair, by_next)
    late_pair, late_next, st, push = call(
        late_kernel,
        (f32(6, *plane), f32(6, *plane), grid, f32(STEPS, width, *plane)),
        (raw, source, coef, cells),
        [(3, 3, *plane), (6, *plane), (6, *plane), (6, *plane)],
    )
    late_pair, late_next = both_ways(late_pair, late_next)
    args, outs, scalars = [by_pair, by_next], [], ()
    scratch = [early, early, (3, *plane), (3, 6, *plane), (3, 3, *plane)]
    owned = size_y // groups
    held = owned + BY
    if groups == 2:
        swapped = jnp.concatenate([by_pair[3 * size_y :], by_next[3 * size_y :], tile])
        swapped = lax.ppermute(swapped, "shot", [(0, 1), (1, 0)])
        args += [swapped, orientation]
        outs = [f32(3, held, size_z)]
        scratch += [(held, size_z)]
        scalars = (3,)
    end, w, third, outer, parts, *weights = call(
        functools.partial(near_kernel, groups),
        [f32(2, 9, *plane), grid, f32(3, width, *plane), f32(7, *plane), f32(4, 3, *plane), *outs],
        [*args, raw, st, coef, cells, push],
        scratch,
        scalars,
    )
    block = (3, width, held, size_z)
    images = [f32(*block), f32(*block)] if groups == 2 else [f32(3, width, *plane)]
    final, *images = call(
        functools.partial(far_kernel, groups),
        [grid, *images],
        [late_pair, late_next, st, end, w, third, outer, parts, coef, push, forward],
        [(6, *plane), (6, *plane), (2, 9, *plane), (3, *plane), (3, *plane), (3, width, *plane)],
    )
    if groups != 2:
        return final[None], smooth_anywhere(images[0], orientation)
    give, keep = images
    (weights,) = weights
    received = lax.ppermute(give, "shot", [(0, 1), (1, 0)])
    message = (6 * owned + BY, size_z)
    by_pair, by_next, grad, swept = call(
        functools.partial(sum_kernel, (STEPS * groups) ** (-0.5)),
        [f32(*message), f32(*message), f32(*block), f32(3, 2, held, size_z)],
        (keep, received, weights),
        [message, message],
    )
    by_pair, by_next = both_ways(by_pair, by_next)
    full, half = call(
        inner_kernel,
        [f32(*block), f32(3, width - 2, held, size_z)],
        (grad, swept, weights),
        [],
    )
    gradient = call(
        smooth_kernel,
        f32(3, width, owned, size_z),
        (by_next, by_pair, grad, full, half, weights),
        [message, message, (2, 7, held, size_z), (width, held, size_z)],
    )
    return final[None], gradient


def solution(mesh):
    return jax.shard_map(
        local,
        mesh=mesh,
        in_specs=(
            P("shot", None, "tile", None, None),
            P("shot", None, "tile", None, None),
            P("shot", None, "tile", None, None),
            P("tile", None, None),
            P("tile", None, None),
            P("tile", None, None),
            P("tile", None, None),
            P("tile", "shot", None),
        ),
        out_specs=(P("shot", None, "tile", None, None), P(None, "tile", "shot", None)),
        check_vma=False,
    )
```

time: 44.6 us -> 37.6 us (0.84)
  waiting for transfers between devices: 25.4 us -> 14.2 us
  starting transfers between devices: 10.2 us -> 14.6 us
    ppermute x4 -> x6, waiting for transfers between devices: 23.9 us -> 11.3 us  [both_ways(): out.append(lax.ppermute(array, 'tile', pairs + [(b, a) for a, b in pairs]))]
    ppermute x4 -> x6, starting transfers between devices: 10.2 us -> 14.6 us  [both_ways(): out.append(lax.ppermute(array, 'tile', pairs + [(b, a) for a, b in pairs]))]
    ppermute x0 -> x1, waiting for transfers between devices: none -> 1.34 us  [local(): swapped = lax.ppermute(swapped, 'shot', [(0, 1), (1, 0)])]
    pallas_call x4 -> x7, Pallas kernels: 8.08 us -> 7.76 us  [call(): pl.pallas_call(kernel, out_shape=outs, in_specs=[SMEM if n in scalars els...]
  transfers between devices with their start and end apart: 5 -> 8, of which waited for: 3 -> 4; matrix products, arithmetic and copies ran while one was open for 0% -> 0% of each run, Pallas kernels for 0% -> 6%
where the time goes in v3:
time: 37.6 us; the launch traced here: 37.4 us
  starting transfers between devices  14.6 us (39%)
  waiting for transfers between devices  14.2 us (38%)
  Pallas kernels  7.76 us (21%)
  between operations  0.76 us (2%)
    ppermute x6, starting transfers between devices, both_ways(): out.append(lax.ppermute(array, 'tile', pairs + [(b, a) for a, b in pairs]))  14.6 us
    ppermute x6, waiting for transfers between devices, both_ways(): out.append(lax.ppermute(array, 'tile', pairs + [(b, a) for a, b in pairs]))  11.3 us
    pallas_call x7, Pallas kernels, call(): pl.pallas_call(kernel, out_shape=outs, in_specs=[SMEM if n in scalars els...  7.76 us
    ppermute x1, waiting for transfers between devices, local(): received = lax.ppermute(give, 'shot', [(0, 1), (1, 0)])  1.5 us
    ppermute x1, waiting for transfers between devices, local(): swapped = lax.ppermute(swapped, 'shot', [(0, 1), (1, 0)])  1.34 us
  transfers between devices with their start and end apart: 8, of which 4 were waited for; matrix products, arithmetic and copies ran while one was open for 0% of the time, Pallas kernels for 6%

profile of v3, /device:TPU:0, one launch (start us, length us, event | category | flops | bytes accessed | tf_op | source)
XLA Modules:
  0.0 37.4 jit_solution(17448678365817598397)
XLA Ops:
  0.6 2.5 %shard_map.95 = (f32[320,128]{1,0:T(8,128)S(1)}, f32[320,128]{1,0:T(8,128)S(1)}, f32[9,4,64,128]{3,2,1,0:T(8,128)S(1)}, bf16[3,4,64,128]{3,2,1,0:T(8,128)(2,1)S(...) custom-call(s32[1,4,8]{2,1,0:T(4,128)} %bitcast.8, s32[1,4,4]{2,1,0:T(4,128)} %refs_3_.1, ...), custom_call_target="tpu_custom_call" | custom-call | tf_op jit(solution)/shard_map/pallas_call | solution.py:731
  3.1 0.0 copy-start.1
  3.1 3.0 %collective-permute-start.2 = (f32[320,128]{1,0:T(8,128)S(1)}, f32[320,128]{1,0:T(8,128)S(1)}, u32[]{:S(2)}, u32[]{:S(2)}) collective-permute-start(f32[320,128]{1,0:T(8,128)S(1)} %get-tuple-element.35), channel_id=1, source_target_pairs={{0,1},{2,3},{4,5},{6,7},{8,9},{10,11},{12,13},{14,15},{1,0},{3,2},... | collective-permute-start | bytes 491528 | tf_op jit(solution)/shard_map/ppermute | solution.py:718
  6.1 0.7 %collective-permute-start.3 = (f32[320,128]{1,0:T(8,128)S(1)}, f32[320,128]{1,0:T(8,128)S(1)}, u32[]{:S(2)}, u32[]{:S(2)}) collective-permute-start(f32[320,128]{1,0:T(8,128)S(1)} %get-tuple-element.36), channel_id=1, source_target_pairs={{1,2},{3,4},{5,6},{7,8},{9,10},{11,12},{13,14},{2,1},{4,3},{6,5},{... | collective-permute-start | bytes 491528 | tf_op jit(solution)/shard_map/ppermute | solution.py:718
  6.8 0.8 %shard_map.96 = (f32[6,64,128]{2,1,0:T(8,128)S(1)}, f32[6,64,128]{2,1,0:T(8,128)S(1)}, f32[9,4,64,128]{3,2,1,0:T(8,128)S(1)}, f32[3,4,64,128]{3,2,1,0:T(8,128)S(1)}) custom-call(f32[9,4,64,128]{3,2,1,0:T(8,128)S(1)} %get-tuple-element.28.state.refs_4_, bf16[3,4,64,128]{3,2,1,0:T(8,128)(2,1)S(1)} %get-tuple-element.29.source, ...), custom_call_target="tpu_custom_call" | custom-call | tf_op jit(solution)/shard_map/pallas_call | solution.py:731
  7.6 4.3 %collective-permute-start = (f32[6,64,128]{2,1,0:T(8,128)S(1)}, f32[6,64,128]{2,1,0:T(8,128)S(1)}, u32[]{:S(2)}, u32[]{:S(2)}) collective-permute-start(f32[6,64,128]{2,1,0:T(8,128)S(1)} %get-tuple-element.32), channel_id=1, source_target_pairs={{0,1},{2,3},{4,5},{6,7},{8,9},{10,11},{12,13},{14,15},{1,0},{3,2},... | collective-permute-start | bytes 589832 | tf_op jit(solution)/shard_map/ppermute | solution.py:718
  11.9 0.7 %collective-permute-start.1 = (f32[6,64,128]{2,1,0:T(8,128)S(1)}, f32[6,64,128]{2,1,0:T(8,128)S(1)}, u32[]{:S(2)}, u32[]{:S(2)}) collective-permute-start(f32[6,64,128]{2,1,0:T(8,128)S(1)} %get-tuple-element.33), channel_id=1, source_target_pairs={{1,2},{3,4},{5,6},{7,8},{9,10},{11,12},{13,14},{2,1},{4,3},{6,5},{... | collective-permute-start | bytes 589832 | tf_op jit(solution)/shard_map/ppermute | solution.py:718
  12.5 0.0 collective-permute-done.2.refs_0_
  12.5 0.0 collective-permute-done.3.refs_1_
  12.6 0.1 collective-permute-start.4
  12.7 1.3 %collective-permute-done.4.refs_2_ = f32[264,128]{1,0:T(8,128)S(1)} collective-permute-done((f32[264,128]{1,0:T(8,128)S(1)}, f32[264,128]{1,0:T(8,128)S(1)}, u32[]{:S(2)}, u32[]{:S(2)}) %collective-permute-start.4) | collective-permute-done | bytes 135200 | tf_op jit(solution)/shard_map/ppermute | solution.py:795
  14.0 0.0 copy-done.1
  14.0 0.0 copy-start
  14.0 1.4 %shard_map.97 = (f32[2,9,64,128]{3,2,1,0:T(8,128)S(1)}, f32[9,4,64,128]{3,2,1,0:T(8,128)S(1)}, f32[3,4,64,128]{3,2,1,0:T(8,128)S(1)}, f32[7,64,128]{2,1,0:T(8,12...) custom-call(f32[320,128]{1,0:T(8,128)S(1)} %collective-permute-done.2.refs_0_, ...), custom_call_target="tpu_custom_call" | custom-call | tf_op jit(solution)/shard_map/pallas_call | solution.py:731
  15.4 6.6 %collective-permute-done.refs_0_ = f32[6,64,128]{2,1,0:T(8,128)S(1)} collective-permute-done((f32[6,64,128]{2,1,0:T(8,128)S(1)}, f32[6,64,128]{2,1,0:T(8,128)S(1)}, u32[]{:S(2)}, u32[]{:S(2)}) %collective-permute-start) | collective-permute-done | bytes 196640 | tf_op jit(solution)/shard_map/ppermute | solution.py:718
  22.0 0.0 collective-permute-done.1.refs_1_
  22.0 0.0 copy-done
  22.0 1.8 %shard_map.98 = (f32[9,4,64,128]{3,2,1,0:T(8,128)}, f32[3,4,40,128]{3,2,1,0:T(8,128)S(1)}, f32[3,4,40,128]{3,2,1,0:T(8,128)S(1)}) custom-call(f32[6,64,128]{2,1,0:T(8,128)S(1)} %collective-permute-done.refs_0_, f32[6,64,128]{2,1,0:T(8,128)S(1)} %collective-permute-done.1.refs_1_, f32[9,4,64,128]{3,2,1,0:T(8,128)S(1)} %get-tuple-element.34.refs_5_.refs_2_, ...), custom_call_target="tpu_custom_call" | custom-call | tf_op jit(solution)/shard_map/pallas_call | solution.py:731
  23.8 0.0 collective-permute-start.5
  23.8 1.5 %collective-permute-done.5.received = f32[3,4,40,128]{3,2,1,0:T(8,128)S(1)} collective-permute-done((f32[3,4,40,128]{3,2,1,0:T(8,128)S(1)}, f32[3,4,40,128]{3,2,1,0:T(8,128)S(1)}, u32[]{:S(2)}, u32[]{:S(2)}) %collective-permute-start.5) | collective-permute-done | bytes 245792 | tf_op jit(solution)/shard_map/ppermute | solution.py:819
  25.3 0.2 shard_map.99
  25.5 0.7 %collective-permute-start.6 = (f32[200,128]{1,0:T(8,128)S(1)}, f32[200,128]{1,0:T(8,128)S(1)}, u32[]{:S(2)}, u32[]{:S(2)}) collective-permute-start(f32[200,128]{1,0:T(8,128)S(1)} %get-tuple-element.48), channel_id=1, source_target_pairs={{1,2},{3,4},{5,6},{7,8},{9,10},{11,12},{13,14},{2,1},{4,3},{6,5},{... | collective-permute-start | bytes 307208 | tf_op jit(solution)/shard_map/ppermute | solution.py:718
  26.2 5.3 %collective-permute-start.7 = (f32[200,128]{1,0:T(8,128)S(1)}, f32[200,128]{1,0:T(8,128)S(1)}, u32[]{:S(2)}, u32[]{:S(2)}) collective-permute-start(f32[200,128]{1,0:T(8,128)S(1)} %get-tuple-element.49), channel_id=1, source_target_pairs={{0,1},{2,3},{4,5},{6,7},{8,9},{10,11},{12,13},{14,15},{1,0},{3,2},... | collective-permute-start | bytes 307208 | tf_op jit(solution)/shard_map/ppermute | solution.py:718
  31.5 0.3 shard_map.100
  31.7 0.0 collective-permute-done.6.by_next
  31.7 4.7 %collective-permute-done.7.by_pair = f32[200,128]{1,0:T(8,128)S(1)} collective-permute-done((f32[200,128]{1,0:T(8,128)S(1)}, f32[200,128]{1,0:T(8,128)S(1)}, u32[]{:S(2)}, u32[]{:S(2)}) %collective-permute-start.7) | collective-permute-done | bytes 102432 | tf_op jit(solution)/shard_map/ppermute | solution.py:718
  36.5 0.9 %shard_map.101 = f32[3,4,32,128]{3,2,1,0:T(8,128)} custom-call(f32[200,128]{1,0:T(8,128)S(1)} %collective-permute-done.6.by_next, f32[200,128]{1,0:T(8,128)S(1)} %collective-permute-done.7.by_pair, f32[3,4,40,128]{3,2,1,0:T(8,128)S(1)} %get-tuple-element.50.grad, f32[3,4,40,128]{3,2,1,0:T(8,128)S(1)} %get-tuple-element.52.full, ...), custom_call_target="tpu_custom_call" | custom-call | tf_op jit(solution)/shard_map/pallas_call | solution.py:731
  (3 shorter events, 0.0 us)
Async XLA Ops:
  3.1 10.9 %copy-start.1 = (s32[1,4,4]{2,1,0:T(4,128)S(1)}, s32[1,4,4]{2,1,0:T(4,128)}, u32[]{:S(2)}) copy-start(s32[1,4,4]{2,1,0:T(4,128)} %refs_3_.1) | copy-start | bytes 196
  3.1 9.4 %collective-permute-start.2 = (f32[320,128]{1,0:T(8,128)S(1)}, f32[320,128]{1,0:T(8,128)S(1)}, u32[]{:S(2)}, u32[]{:S(2)}) collective-permute-start(f32[320,128]{1,0:T(8,128)S(1)} %get-tuple-element.35), channel_id=1, source_target_pairs={{0,1},{2,3},{4,5},{6,7},{8,9},{10,11},{12,13},{14,15},{1,0},{3,2},... | collective-permute-start | bytes 491528 | tf_op jit(solution)/shard_map/ppermute | solution.py:718
  6.1 6.4 %collective-permute-start.3 = (f32[320,128]{1,0:T(8,128)S(1)}, f32[320,128]{1,0:T(8,128)S(1)}, u32[]{:S(2)}, u32[]{:S(2)}) collective-permute-start(f32[320,128]{1,0:T(8,128)S(1)} %get-tuple-element.36), channel_id=1, source_target_pairs={{1,2},{3,4},{5,6},{7,8},{9,10},{11,12},{13,14},{2,1},{4,3},{6,5},{... | collective-permute-start | bytes 491528 | tf_op jit(solution)/shard_map/ppermute | solution.py:718
  7.6 14.4 %collective-permute-start = (f32[6,64,128]{2,1,0:T(8,128)S(1)}, f32[6,64,128]{2,1,0:T(8,128)S(1)}, u32[]{:S(2)}, u32[]{:S(2)}) collective-permute-start(f32[6,64,128]{2,1,0:T(8,128)S(1)} %get-tuple-element.32), channel_id=1, source_target_pairs={{0,1},{2,3},{4,5},{6,7},{8,9},{10,11},{12,13},{14,15},{1,0},{3,2},... | collective-permute-start | bytes 589832 | tf_op jit(solution)/shard_map/ppermute | solution.py:718
  11.9 10.1 %collective-permute-start.1 = (f32[6,64,128]{2,1,0:T(8,128)S(1)}, f32[6,64,128]{2,1,0:T(8,128)S(1)}, u32[]{:S(2)}, u32[]{:S(2)}) collective-permute-start(f32[6,64,128]{2,1,0:T(8,128)S(1)} %get-tuple-element.33), channel_id=1, source_target_pairs={{1,2},{3,4},{5,6},{7,8},{9,10},{11,12},{13,14},{2,1},{4,3},{6,5},{... | collective-permute-start | bytes 589832 | tf_op jit(solution)/shard_map/ppermute | solution.py:718
  12.6 1.4 %collective-permute-start.4 = (f32[264,128]{1,0:T(8,128)S(1)}, f32[264,128]{1,0:T(8,128)S(1)}, u32[]{:S(2)}, u32[]{:S(2)}) collective-permute-start(f32[264,128]{1,0:T(8,128)S(1)} %pad_maximum_fusion), channel_id=1, source_target_pairs={{0,16},{16,0},{1,17},{17,1},{2,18},{18,2},{3,19},{19,3},{4,20},{20... | collective-permute-start | bytes 405512 | tf_op jit(solution)/shard_map/ppermute | solution.py:795
  14.0 8.0 %copy-start = (bf16[1,9,4,64,128]{4,3,2,1,0:T(8,128)(2,1)S(1)}, bf16[1,9,4,64,128]{4,3,2,1,0:T(8,128)(2,1)}, u32[]{:S(2)}) copy-start(bf16[1,9,4,64,128]{4,3,2,1,0:T(8,128)(2,1)} %param.10) | copy-start | bytes 1769476
  23.8 1.5 %collective-permute-start.5 = (f32[3,4,40,128]{3,2,1,0:T(8,128)S(1)}, f32[3,4,40,128]{3,2,1,0:T(8,128)S(1)}, u32[]{:S(2)}, u32[]{:S(2)}) collective-permute-start(f32[3,4,40,128]{3,2,1,0:T(8,128)S(1)} %get-tuple-element.46), channel_id=1, source_target_pairs={{0,16},{16,0},{1,17},{17,1},{2,18},{18,2},{3,19},{19,3},{4,20},{20... | collective-permute-start | bytes 737288 | tf_op jit(solution)/shard_map/ppermute | solution.py:819
  25.5 6.2 %collective-permute-start.6 = (f32[200,128]{1,0:T(8,128)S(1)}, f32[200,128]{1,0:T(8,128)S(1)}, u32[]{:S(2)}, u32[]{:S(2)}) collective-permute-start(f32[200,128]{1,0:T(8,128)S(1)} %get-tuple-element.48), channel_id=1, source_target_pairs={{1,2},{3,4},{5,6},{7,8},{9,10},{11,12},{13,14},{2,1},{4,3},{6,5},{... | collective-permute-start | bytes 307208 | tf_op jit(solution)/shard_map/ppermute | solution.py:718
  26.2 10.3 %collective-permute-start.7 = (f32[200,128]{1,0:T(8,128)S(1)}, f32[200,128]{1,0:T(8,128)S(1)}, u32[]{:S(2)}, u32[]{:S(2)}) collective-permute-start(f32[200,128]{1,0:T(8,128)S(1)} %get-tuple-element.49), channel_id=1, source_target_pairs={{0,1},{2,3},{4,5},{6,7},{8,9},{10,11},{12,13},{14,15},{1,0},{3,2},... | collective-permute-start | bytes 307208 | tf_op jit(solution)/shard_map/ppermute | solution.py:718

commit v4 on v3

--- a/solution.py
+++ b/solution.py
@@ -179,8 +179,8 @@
 
 def early_kernel(
     groups,
-    active,
-    orientation,
+    active_hbm,
+    orientation_hbm,
     state_hbm,
     source_hbm,
     lame_hbm,
@@ -188,63 +188,64 @@
     buoyancy_hbm,
     by_pair,
     by_next,
-    state,
-    source,
-    coef,
     cells,
     tile,
     up,
     down,
+    first,
+    push,
     params,
+    active,
+    orientation,
     sems,
 ):
-    width, size_y, size_z = state.shape[1:]
-    last = width - 1
-    copies = [
-        pltpu.make_async_copy(array, params.at[n], sems.at[n])
-        for n, array in enumerate((buoyancy_hbm, lame_hbm, shear_hbm))
+    size_y, size_z = cells.shape
+    last = state_hbm.shape[1] - 1
+    planes_at = (0, 0, 0, 1, last, last, last)
+    arrays = (buoyancy_hbm, lame_hbm, shear_hbm)
+    ends = [(active_hbm, active), (orientation_hbm, orientation)]
+    ends += [(arrays[n % 3].at[x], params.at[n]) for n, x in enumerate(planes_at)]
+    ends += [(state_hbm.at[:, 0], first), (source_hbm.at[0, 0], push)]
+    ends += [
+        (state_hbm.at[c, last], up.at[n * size_y : (n + 1) * size_y]) for n, c in enumerate(SIDE)
     ]
-    copies += [
-        pltpu.make_async_copy(state_hbm.at[c], state.at[c], sems.at[3 + c])
-        for c in (XX, XY, XZ, YY, YZ, ZZ, VX, VY, VZ)
-    ]
-    copies.append(pltpu.make_async_copy(source_hbm, source, sems.at[12]))
+    copies = [pltpu.make_async_copy(*pair, sems.at[n]) for n, pair in enumerate(ends)]
     for copy in copies:
         copy.start()
+    for copy in copies[:2]:
+        copy.wait()
     cell_plane(active, cells)
     me = lax.axis_index("shot") if groups == 2 else 0
-    blocks = orientation.shape[1]
-    tile[...] = class_tile(orientation, jnp.where(me == 0, blocks - 1, 0), size_z)
-    for copy in copies[:3]:
+    last_block = orientation.shape[1] - 1
+    tile[...] = class_tile(orientation, jnp.where(me == 0, last_block, 0), size_z)
+    for copy in copies[2:9]:
         copy.wait()
     for row in chunks(size_y):
         c = time_step * cells[here(row), :]
-        for x in range(width):
-            for n in range(3):
-                coef[n, x, here(row)] = c * params[n, x, here(row)]
+        for n in range(7):
+            params[n, here(row)] = c * params[n, here(row)]
     count = (up.shape[0] - 3 * size_y) // 4
     mine = pl.ds(pl.multiple_of(me * count, 8), count) if groups == 2 else slice(0, count)
     for n in range(4):
         to = slice(3 * size_y + n * count, 3 * size_y + (n + 1) * count)
-        up[to] = coef[n % 3, last, mine]
-        down[to] = coef[n % 3, n // 3, mine]
-    for copy in copies[3:]:
+        down[to] = params[n, mine]
+        up[to] = params[(6, 4, 5, 6)[n], mine]
+    for copy in copies[9:]:
         copy.wait()
-    raw = {c: Plane(state, c, 0) for c in range(9)}
-    for row in chunks(size_y):
-        c, cb = cells[here(row), :], coef[0, 0, here(row)]
+    raw = {c: Plane(first, c) for c in range(9)}
+    for row in chunks(size_y):
+        c, cb = cells[here(row), :], params[0, here(row)]
         for n, term in enumerate(divergence(raw, None, row, ROWS)):
             value = c * raw[n].at(row, ROWS) + cb * term
             if n == VZ:
-                push = source[0, 0, here(row)].astype(jnp.float32)
-                value = value + time_step * c * push
-            to = slice(n * size_y + row, n * size_y + row + ROWS)
-            down[to] = value
-            up[to] = state[SIDE[n], last, here(row)]
+                value = value + time_step * c * push[here(row)].astype(jnp.float32)
+            down[n * size_y + row : n * size_y + row + ROWS] = value
     hand_out(by_pair, by_next, up, down)
 
 
-def late_kernel(state, source, coef, cells, by_pair, by_next, st, push, v2, s2, up, down):
+def late_kernel(
+    state, source, buoyancy, lame, shear, cells, by_pair, by_next, st, push, coef, v2, s2, up, down
+):
     width, size_y = state.shape[1], state.shape[2]
     last = width - 1
     for row in chunks(size_y):
@@ -252,6 +253,9 @@
         for step in range(STEPS):
             for x in range(width):
                 push[step, x, here(row)] = c * source[step, x, here(row)].astype(jnp.float32)
+        for n, param in enumerate((buoyancy, lame, shear)):
+            for x in range(width):
+                coef[n, x, here(row)] = c * param[x, here(row)]
 
     def coefs(x, row):
         return [coef[n, x, here(row)] for n in range(3)]
@@ -635,7 +639,7 @@
             )
 
 
-def smooth_kernel(by_next, by_pair, grad, full, half, weights, out, low, high, beside, result):
+def smooth_kernel(by_pair, by_next, grad, full, half, weights, out, low, high, beside, result):
     width, count, size_z = grad.shape[1:]
     own = count - BY
     last = width - 1
@@ -727,7 +731,7 @@
     return pltpu.with_memory_space_constraint(array, pltpu.HBM)
 
 
-def call(kernel, outs, args, scratch, scalars=(), space=VMEM, flops=0):
+def call(kernel, outs, args, scratch, scalars=(), space=VMEM):
     return pl.pallas_call(
         kernel,
         out_shape=outs,
@@ -759,30 +763,30 @@
     grid = f32(9, width, *plane)
     count = size_y // 2 if groups == 2 else size_y
     early = (3 * size_y + 4 * count, size_z)
-    by_pair, by_next, raw, source, coef, cells, tile = call(
+    by_pair, by_next, cells, tile = call(
         functools.partial(early_kernel, groups),
-        (
-            f32(*early),
-            f32(*early),
-            grid,
-            jax.ShapeDtypeStruct(source.shape, source.dtype),
-            f32(3, width, *plane),
-            f32(*plane),
-            f32(BY, size_z),
-        ),
+        [f32(*early), f32(*early), f32(*plane), f32(BY, size_z)],
         [
             in_hbm(a)
             for a in (active, orientation, state, source, lame_first, shear_modulus, buoyancy)
         ],
-        [early, early, (3, width, *plane), pltpu.SemaphoreType.DMA((13,))],
-        (0, 1),
-        HBM,
+        [
+            early,
+            early,
+            (9, *plane),
+            pltpu.VMEM(plane, source.dtype),
+            (7, *plane),
+            pltpu.SMEM(active.shape, jnp.int32),
+            pltpu.SMEM(orientation.shape, jnp.int32),
+            pltpu.SemaphoreType.DMA((14,)),
+        ],
+        space=HBM,
     )
     by_pair, by_next = both_ways(by_pair, by_next)
-    late_pair, late_next, st, push = call(
+    late_pair, late_next, st, push, coef = call(
         late_kernel,
-        (f32(6, *plane), f32(6, *plane), grid, f32(STEPS, width, *plane)),
-        (raw, source, coef, cells),
+        [f32(6, *plane), f32(6, *plane), grid, f32(STEPS, width, *plane), f32(3, width, *plane)],
+        (state, source, buoyancy, lame_first, shear_modulus, cells),
         [(3, 3, *plane), (6, *plane), (6, *plane), (6, *plane)],
     )
     late_pair, late_next = both_ways(late_pair, late_next)
@@ -800,7 +804,7 @@
     end, w, third, outer, parts, *weights = call(
         functools.partial(near_kernel, groups),
         [f32(2, 9, *plane), grid, f32(3, width, *plane), f32(7, *plane), f32(4, 3, *plane), *outs],
-        [*args, raw, st, coef, cells, push],
+        [*args, state, st, coef, cells, push],
         scratch,
         scalars,
     )
@@ -808,7 +812,7 @@
     images = [f32(*block), f32(*block)] if groups == 2 else [f32(3, width, *plane)]
     final, *images = call(
         functools.partial(far_kernel, groups),
-        [grid, *images],
+        [pltpu.VMEM(grid.shape, grid.dtype), *images],
         [late_pair, late_next, st, end, w, third, outer, parts, coef, push, forward],
         [(6, *plane), (6, *plane), (2, 9, *plane), (3, *plane), (3, *plane), (3, width, *plane)],
     )
@@ -834,7 +838,7 @@
     gradient = call(
         smooth_kernel,
         f32(3, width, owned, size_z),
-        (by_next, by_pair, grad, full, half, weights),
+        (by_pair, by_next, grad, full, half, weights),
         [message, message, (2, 7, held, size_z), (width, held, size_z)],
     )
     return final[None], gradient

time: 37.6 us -> 34.7 us (0.923)
  the two profiles are of different devices: /device:TPU:0 before, /device:TPU:8 now
where the time goes in v4:
time: 34.7 us; the launch traced here: 34.5 us
  starting transfers between devices  15.2 us (44%)
  waiting for transfers between devices  11.6 us (33%)
  Pallas kernels  5.77 us (17%)
  local copies, waits for them, and re-layouts  1.06 us (3%)
  between operations  0.82 us (2%)
    ppermute x6, starting transfers between devices, both_ways(): out.append(lax.ppermute(array, 'tile', pairs + [(b, a) for a, b in pairs]))  15.1 us
    ppermute x6, waiting for transfers between devices, both_ways(): out.append(lax.ppermute(array, 'tile', pairs + [(b, a) for a, b in pairs]))  8.72 us
    pallas_call x7, Pallas kernels, call(): pl.pallas_call(kernel, out_shape=outs, in_specs=[SMEM if n in scalars els...  5.77 us
    ppermute x1, waiting for transfers between devices, local(): received = lax.ppermute(give, 'shot', [(0, 1), (1, 0)])  1.5 us
    ppermute x1, waiting for transfers between devices, local(): swapped = lax.ppermute(swapped, 'shot', [(0, 1), (1, 0)])  1.34 us
    unnamed x15, local copies, waits for them, and re-layouts  1.05 us
  transfers between devices with their start and end apart: 8, of which 5 were waited for; matrix products, arithmetic and copies ran while one was open for 3% of the time, Pallas kernels for 7%

profile of v4, /device:TPU:8, one launch (start us, length us, event | category | flops | bytes accessed | tf_op | source)
XLA Modules:
  0.0 34.5 jit_solution(7847915518023917409)
XLA Ops:
  0.6 0.0 copy-start.3
  0.6 0.0 copy-start.5
  0.7 1.4 %shard_map.95 = (f32[320,128]{1,0:T(8,128)S(1)}, f32[320,128]{1,0:T(8,128)S(1)}, f32[64,128]{1,0:T(8,128)S(1)}, f32[8,128]{1,0:T(8,128)S(1)}) custom-call(s32[1,4,8]{2,1,0:T(4,128)} %bitcast.12, s32[1,4,4]{2,1,0:T(4,128)} %refs_3_.1, f32[9,4,64,128]{3,2,1,0:T(8,128)} %bitcast.6, bf16[3,4,64,128]{3,2,1,0:T(8,128)(2,1)} %bitcast.9, f32[4,64,128]{2,1,0:T(8,128)} %lame.1, ...), custom_call_target="tpu_custom_call" | custom-call | tf_op jit(solution)/shard_map/pallas_call | solution.py:735
  2.1 0.0 copy-start.6
  2.1 1.6 %collective-permute-start.2 = (f32[320,128]{1,0:T(8,128)S(1)}, f32[320,128]{1,0:T(8,128)S(1)}, u32[]{:S(2)}, u32[]{:S(2)}) collective-permute-start(f32[320,128]{1,0:T(8,128)S(1)} %get-tuple-element.30), channel_id=1, source_target_pairs={{0,1},{2,3},{4,5},{6,7},{8,9},{10,11},{12,13},{14,15},{1,0},{3,2},... | collective-permute-start | bytes 491528 | tf_op jit(solution)/shard_map/ppermute | solution.py:722
  3.7 3.3 %collective-permute-start.3 = (f32[320,128]{1,0:T(8,128)S(1)}, f32[320,128]{1,0:T(8,128)S(1)}, u32[]{:S(2)}, u32[]{:S(2)}) collective-permute-start(f32[320,128]{1,0:T(8,128)S(1)} %get-tuple-element.31), channel_id=1, source_target_pairs={{1,2},{3,4},{5,6},{7,8},{9,10},{11,12},{13,14},{2,1},{4,3},{6,5},{... | collective-permute-start | bytes 491528 | tf_op jit(solution)/shard_map/ppermute | solution.py:722
  7.0 0.0 copy-done.3
  7.0 0.0 copy-done.5
  7.0 0.0 copy-done.4
  7.0 0.0 copy-done.1
  7.0 0.0 copy-done
  7.0 0.8 %shard_map.96 = (f32[6,64,128]{2,1,0:T(8,128)S(1)}, f32[6,64,128]{2,1,0:T(8,128)S(1)}, f32[9,4,64,128]{3,2,1,0:T(8,128)S(1)}, f32[3,4,64,128]{3,2,1,0:T(8,128)S(1)}, f32[3,4,64,128]{3,2,1,0:T(8,128)S(1)}) custom-call(f32[9,4,64,128]{3,2,1,0:T(8,128)S(1)} %bitcast.7, bf16[3,4,64,128]{3,2,1,0:T(8,128)(2,1)S(1)} %bitcast.10, f32[4,64,128]{2,1,0:T(8,128)S(1)} %copy-done.3, ...), custom_call_target="tpu_custom_call" | custom-call | tf_op jit(solution)/shard_map/pallas_call | solution.py:735
  7.8 1.7 %collective-permute-start = (f32[6,64,128]{2,1,0:T(8,128)S(1)}, f32[6,64,128]{2,1,0:T(8,128)S(1)}, u32[]{:S(2)}, u32[]{:S(2)}) collective-permute-start(f32[6,64,128]{2,1,0:T(8,128)S(1)} %get-tuple-element.27), channel_id=1, source_target_pairs={{0,1},{2,3},{4,5},{6,7},{8,9},{10,11},{12,13},{14,15},{1,0},{3,2},... | collective-permute-start | bytes 589832 | tf_op jit(solution)/shard_map/ppermute | solution.py:722
  9.5 2.8 %collective-permute-start.1 = (f32[6,64,128]{2,1,0:T(8,128)S(1)}, f32[6,64,128]{2,1,0:T(8,128)S(1)}, u32[]{:S(2)}, u32[]{:S(2)}) collective-permute-start(f32[6,64,128]{2,1,0:T(8,128)S(1)} %get-tuple-element.28), channel_id=1, source_target_pairs={{1,2},{3,4},{5,6},{7,8},{9,10},{11,12},{13,14},{2,1},{4,3},{6,5},{... | collective-permute-start | bytes 589832 | tf_op jit(solution)/shard_map/ppermute | solution.py:722
  12.3 0.0 collective-permute-done.2.refs_0_
  12.3 0.9 %collective-permute-done.3.refs_1_ = f32[320,128]{1,0:T(8,128)S(1)} collective-permute-done((f32[320,128]{1,0:T(8,128)S(1)}, f32[320,128]{1,0:T(8,128)S(1)}, u32[]{:S(2)}, u32[]{:S(2)}) %collective-permute-start.3) | collective-permute-done | bytes 163872 | tf_op jit(solution)/shard_map/ppermute | solution.py:722
  13.2 0.1 collective-permute-start.4
  13.3 1.3 %collective-permute-done.4.refs_2_ = f32[264,128]{1,0:T(8,128)S(1)} collective-permute-done((f32[264,128]{1,0:T(8,128)S(1)}, f32[264,128]{1,0:T(8,128)S(1)}, u32[]{:S(2)}, u32[]{:S(2)}) %collective-permute-start.4) | collective-permute-done | bytes 135200 | tf_op jit(solution)/shard_map/ppermute | solution.py:799
  14.6 1.4 %shard_map.97 = (f32[2,9,64,128]{3,2,1,0:T(8,128)S(1)}, f32[9,4,64,128]{3,2,1,0:T(8,128)S(1)}, f32[3,4,64,128]{3,2,1,0:T(8,128)S(1)}, f32[7,64,128]{2,1,0:T(8,12...) custom-call(f32[320,128]{1,0:T(8,128)S(1)} %collective-permute-done.2.refs_0_, ...), custom_call_target="tpu_custom_call" | custom-call | tf_op jit(solution)/shard_map/pallas_call | solution.py:735
  16.0 3.6 %collective-permute-done.refs_0_ = f32[6,64,128]{2,1,0:T(8,128)S(1)} collective-permute-done((f32[6,64,128]{2,1,0:T(8,128)S(1)}, f32[6,64,128]{2,1,0:T(8,128)S(1)}, u32[]{:S(2)}, u32[]{:S(2)}) %collective-permute-start) | collective-permute-done | bytes 196640 | tf_op jit(solution)/shard_map/ppermute | solution.py:722
  19.6 0.0 collective-permute-done.1.refs_1_
  19.6 0.8 %shard_map.98 = (f32[9,4,64,128]{3,2,1,0:T(8,128)S(1)}, f32[3,4,40,128]{3,2,1,0:T(8,128)S(1)}, f32[3,4,40,128]{3,2,1,0:T(8,128)S(1)}) custom-call(f32[6,64,128]{2,1,0:T(8,128)S(1)} %collective-permute-done.refs_0_, f32[6,64,128]{2,1,0:T(8,128)S(1)} %collective-permute-done.1.refs_1_, f32[9,4,64,128]{3,2,1,0:T(8,128)S(1)} %get-tuple-element.29.refs_5_.refs_2_, ...), custom_call_target="tpu_custom_call" | custom-call | tf_op jit(solution)/shard_map/pallas_call | solution.py:735
  20.4 0.1 collective-permute-start.5
  20.5 1.5 %collective-permute-done.5.received = f32[3,4,40,128]{3,2,1,0:T(8,128)S(1)} collective-permute-done((f32[3,4,40,128]{3,2,1,0:T(8,128)S(1)}, f32[3,4,40,128]{3,2,1,0:T(8,128)S(1)}, u32[]{:S(2)}, u32[]{:S(2)}) %collective-permute-start.5) | collective-permute-done | bytes 245792 | tf_op jit(solution)/shard_map/ppermute | solution.py:823
  22.0 0.2 shard_map.99
  22.2 3.0 %collective-permute-start.6 = (f32[200,128]{1,0:T(8,128)S(1)}, f32[200,128]{1,0:T(8,128)S(1)}, u32[]{:S(2)}, u32[]{:S(2)}) collective-permute-start(f32[200,128]{1,0:T(8,128)S(1)} %get-tuple-element.44), channel_id=1, source_target_pairs={{0,1},{2,3},{4,5},{6,7},{8,9},{10,11},{12,13},{14,15},{1,0},{3,2},... | collective-permute-start | bytes 307208 | tf_op jit(solution)/shard_map/ppermute | solution.py:722
  25.2 2.8 %collective-permute-start.7 = (f32[200,128]{1,0:T(8,128)S(1)}, f32[200,128]{1,0:T(8,128)S(1)}, u32[]{:S(2)}, u32[]{:S(2)}) collective-permute-start(f32[200,128]{1,0:T(8,128)S(1)} %get-tuple-element.45), channel_id=1, source_target_pairs={{1,2},{3,4},{5,6},{7,8},{9,10},{11,12},{13,14},{2,1},{4,3},{6,5},{... | collective-permute-start | bytes 307208 | tf_op jit(solution)/shard_map/ppermute | solution.py:722
  28.0 1.0 %copy.10 = f32[1,9,4,64,128]{4,3,2,1,0:T(8,128)} copy(f32[1,9,4,64,128]{4,3,2,1,0:T(8,128)S(1)} %bitcast.5) | data formatting | bytes 2359296
  29.0 0.3 shard_map.100
  29.3 0.0 collective-permute-done.6.by_pair
  29.3 4.2 %collective-permute-done.7.by_next = f32[200,128]{1,0:T(8,128)S(1)} collective-permute-done((f32[200,128]{1,0:T(8,128)S(1)}, f32[200,128]{1,0:T(8,128)S(1)}, u32[]{:S(2)}, u32[]{:S(2)}) %collective-permute-start.7) | collective-permute-done | bytes 102432 | tf_op jit(solution)/shard_map/ppermute | solution.py:722
  33.5 0.9 %shard_map.101 = f32[3,4,32,128]{3,2,1,0:T(8,128)} custom-call(f32[200,128]{1,0:T(8,128)S(1)} %collective-permute-done.6.by_pair, f32[200,128]{1,0:T(8,128)S(1)} %collective-permute-done.7.by_next, f32[3,4,40,128]{3,2,1,0:T(8,128)S(1)} %get-tuple-element.46.grad, f32[3,4,40,128]{3,2,1,0:T(8,128)S(1)} %get-tuple-element.48.full, ...), custom_call_target="tpu_custom_call" | custom-call | tf_op jit(solution)/shard_map/pallas_call | solution.py:735
  (9 shorter events, 0.0 us)
Async XLA Ops:
  0.6 6.4 %copy-start.3 = (f32[4,64,128]{2,1,0:T(8,128)S(1)}, f32[4,64,128]{2,1,0:T(8,128)}, u32[]{:S(2)}) copy-start(f32[4,64,128]{2,1,0:T(8,128)} %buoyancy.1) | copy-start | bytes 393220
  0.6 6.4 %copy-start.5 = (f32[4,64,128]{2,1,0:T(8,128)S(1)}, f32[4,64,128]{2,1,0:T(8,128)}, u32[]{:S(2)}) copy-start(f32[4,64,128]{2,1,0:T(8,128)} %shear.1) | copy-start | bytes 393220
  0.7 6.4 %copy-start.4 = (f32[4,64,128]{2,1,0:T(8,128)S(1)}, f32[4,64,128]{2,1,0:T(8,128)}, u32[]{:S(2)}) copy-start(f32[4,64,128]{2,1,0:T(8,128)} %lame.1) | copy-start | bytes 393220
  0.7 6.4 %copy-start.1 = (bf16[1,3,4,64,128]{4,3,2,1,0:T(8,128)(2,1)S(1)}, bf16[1,3,4,64,128]{4,3,2,1,0:T(8,128)(2,1)}, u32[]{:S(2)}) copy-start(bf16[1,3,4,64,128]{4,3,2,1,0:T(8,128)(2,1)} %param.9) | copy-start | bytes 589828
  0.7 6.4 %copy-start = (f32[1,9,4,64,128]{4,3,2,1,0:T(8,128)S(1)}, f32[1,9,4,64,128]{4,3,2,1,0:T(8,128)}, u32[]{:S(2)}) copy-start(f32[1,9,4,64,128]{4,3,2,1,0:T(8,128)} %param.8) | copy-start | bytes 3538948
  2.1 12.5 %copy-start.6 = (s32[1,4,4]{2,1,0:T(4,128)S(1)}, s32[1,4,4]{2,1,0:T(4,128)}, u32[]{:S(2)}) copy-start(s32[1,4,4]{2,1,0:T(4,128)} %refs_3_.1) | copy-start | bytes 196
  2.1 10.1 %collective-permute-start.2 = (f32[320,128]{1,0:T(8,128)S(1)}, f32[320,128]{1,0:T(8,128)S(1)}, u32[]{:S(2)}, u32[]{:S(2)}) collective-permute-start(f32[320,128]{1,0:T(8,128)S(1)} %get-tuple-element.30), channel_id=1, source_target_pairs={{0,1},{2,3},{4,5},{6,7},{8,9},{10,11},{12,13},{14,15},{1,0},{3,2},... | collective-permute-start | bytes 491528 | tf_op jit(solution)/shard_map/ppermute | solution.py:722
  3.7 9.4 %collective-permute-start.3 = (f32[320,128]{1,0:T(8,128)S(1)}, f32[320,128]{1,0:T(8,128)S(1)}, u32[]{:S(2)}, u32[]{:S(2)}) collective-permute-start(f32[320,128]{1,0:T(8,128)S(1)} %get-tuple-element.31), channel_id=1, source_target_pairs={{1,2},{3,4},{5,6},{7,8},{9,10},{11,12},{13,14},{2,1},{4,3},{6,5},{... | collective-permute-start | bytes 491528 | tf_op jit(solution)/shard_map/ppermute | solution.py:722
  7.8 11.8 %collective-permute-start = (f32[6,64,128]{2,1,0:T(8,128)S(1)}, f32[6,64,128]{2,1,0:T(8,128)S(1)}, u32[]{:S(2)}, u32[]{:S(2)}) collective-permute-start(f32[6,64,128]{2,1,0:T(8,128)S(1)} %get-tuple-element.27), channel_id=1, source_target_pairs={{0,1},{2,3},{4,5},{6,7},{8,9},{10,11},{12,13},{14,15},{1,0},{3,2},... | collective-permute-start | bytes 589832 | tf_op jit(solution)/shard_map/ppermute | solution.py:722
  9.5 10.1 %collective-permute-start.1 = (f32[6,64,128]{2,1,0:T(8,128)S(1)}, f32[6,64,128]{2,1,0:T(8,128)S(1)}, u32[]{:S(2)}, u32[]{:S(2)}) collective-permute-start(f32[6,64,128]{2,1,0:T(8,128)S(1)} %get-tuple-element.28), channel_id=1, source_target_pairs={{1,2},{3,4},{5,6},{7,8},{9,10},{11,12},{13,14},{2,1},{4,3},{6,5},{... | collective-permute-start | bytes 589832 | tf_op jit(solution)/shard_map/ppermute | solution.py:722
  13.2 1.4 %collective-permute-start.4 = (f32[264,128]{1,0:T(8,128)S(1)}, f32[264,128]{1,0:T(8,128)S(1)}, u32[]{:S(2)}, u32[]{:S(2)}) collective-permute-start(f32[264,128]{1,0:T(8,128)S(1)} %pad_maximum_fusion), channel_id=1, source_target_pairs={{0,16},{16,0},{1,17},{17,1},{2,18},{18,2},{3,19},{19,3},{4,20},{20... | collective-permute-start | bytes 405512 | tf_op jit(solution)/shard_map/ppermute | solution.py:799
  14.6 5.0 %copy-start.2 = (bf16[1,9,4,64,128]{4,3,2,1,0:T(8,128)(2,1)S(1)}, bf16[1,9,4,64,128]{4,3,2,1,0:T(8,128)(2,1)}, u32[]{:S(2)}) copy-start(bf16[1,9,4,64,128]{4,3,2,1,0:T(8,128)(2,1)} %param.10) | copy-start | bytes 1769476
  20.4 1.6 %collective-permute-start.5 = (f32[3,4,40,128]{3,2,1,0:T(8,128)S(1)}, f32[3,4,40,128]{3,2,1,0:T(8,128)S(1)}, u32[]{:S(2)}, u32[]{:S(2)}) collective-permute-start(f32[3,4,40,128]{3,2,1,0:T(8,128)S(1)} %get-tuple-element.42), channel_id=1, source_target_pairs={{0,16},{16,0},{1,17},{17,1},{2,18},{18,2},{3,19},{19,3},{4,20},{20... | collective-permute-start | bytes 737288 | tf_op jit(solution)/shard_map/ppermute | solution.py:823
  22.2 7.1 %collective-permute-start.6 = (f32[200,128]{1,0:T(8,128)S(1)}, f32[200,128]{1,0:T(8,128)S(1)}, u32[]{:S(2)}, u32[]{:S(2)}) collective-permute-start(f32[200,128]{1,0:T(8,128)S(1)} %get-tuple-element.44), channel_id=1, source_target_pairs={{0,1},{2,3},{4,5},{6,7},{8,9},{10,11},{12,13},{14,15},{1,0},{3,2},... | collective-permute-start | bytes 307208 | tf_op jit(solution)/shard_map/ppermute | solution.py:722
  25.2 8.3 %collective-permute-start.7 = (f32[200,128]{1,0:T(8,128)S(1)}, f32[200,128]{1,0:T(8,128)S(1)}, u32[]{:S(2)}, u32[]{:S(2)}) collective-permute-start(f32[200,128]{1,0:T(8,128)S(1)} %get-tuple-element.45), channel_id=1, source_target_pairs={{1,2},{3,4},{5,6},{7,8},{9,10},{11,12},{13,14},{2,1},{4,3},{6,5},{... | collective-permute-start | bytes 307208 | tf_op jit(solution)/shard_map/ppermute | solution.py:722

commit v5 on v4

--- a/solution.py
+++ b/solution.py
@@ -319,6 +319,18 @@
     return {XX: spread + 2.0 * cm * v[0], YY: spread, ZZ: spread, XY: cm * v[1], XZ: cm * v[2]}
 
 
+def add(terms):
+    return functools.reduce(jnp.add, terms)
+
+
+def imaged(moved, forward, x, row):
+    f = [forward[n, x, here(row)].astype(jnp.float32) for n in range(9)]
+    trace = (moved[XX] + moved[YY] + moved[ZZ]) * (f[0] + f[1] + f[2])
+    shear = add([moved[comp] * f[n] for n, comp in enumerate(STRESS)])
+    density = add([moved[c] * f[6 + c] for c in VEL]) if VX in moved else None
+    return trace, shear, density
+
+
 def own_planes(st, end):
     width = st.shape[1]
     one = [{c: Plane(st, c, x) for c in range(9)} for x in range(width)]
@@ -331,7 +343,7 @@
     by_pair, by_next, *refs = refs
     if groups == 2:
         swapped, orientation, *refs = refs
-    state, st, coef, cells, push, end, w, third, outer, parts, *refs = refs
+    state, st, coef, cells, push, forward, end, w, third, outer, parts, known, *refs = refs
     if groups == 2:
         weights, *refs = refs
     low, high, high_v, d_s, d_v, *classes = refs
@@ -445,6 +457,18 @@
                 if comp == VZ:
                     value = value + push[2, x, here(row)]
                 third[comp, x, here(row)] = value
+    for row in chunks(size_y):
+        for x in range(width):
+            inner = 1 <= x < last
+            v, t = [one[x]], [one[x]] + [two[x]] * inner
+            if x:
+                v.append(two[x])
+            if 2 <= x < last:
+                v.append({c: Plane(third, c, x) for c in VEL})
+            moved = {c: add([k[c].at(row, ROWS) for k in v]) for c in VEL}
+            moved |= {c: add([k[c].at(row, ROWS) for k in t]) for c in STRESS}
+            for n, value in enumerate(imaged(moved, forward, x, row)):
+                known[n, x, here(row)] = value
     if groups != 2:
         return
 
@@ -464,7 +488,7 @@
 
 
 def far_kernel(groups, *refs):
-    by_pair, by_next, st, end, w, third, outer, parts, coef, push, forward, final, *refs = refs
+    by_pair, by_next, st, end, w, third, outer, parts, known, coef, push, forward, final, *refs = refs
     *images, low, high, edge, low_s, high_v, image = refs
     width, size_y = st.shape[1], st.shape[2]
     last = width - 1
@@ -538,23 +562,20 @@
             _, cl, cm = coefs(x, row)
             after = three[x + 1] if x < last else high_three
             rate = stress_rate(strain(three[x], after, row, ROWS), cl, cm)
-            sums = {}
+            moved = {}
             for comp in STRESS:
                 before = two[x][comp].at(row, ROWS)
                 value = before + rate[comp]
                 three[x][comp].set(row, value)
-                sums[comp] = one[x][comp].at(row, ROWS) + before + value
-            f = [forward[n, x, here(row)].astype(jnp.float32) for n in range(9)]
-            image[0, x, here(row)] = (sums[XX] + sums[YY] + sums[ZZ]) * (f[0] + f[1] + f[2])
-            total = sums[XX] * f[0]
-            for n, comp in enumerate(STRESS[1:]):
-                total = total + sums[comp] * f[n + 1]
-            image[1, x, here(row)] = total
-            total = 0.0
-            for comp in VEL:
-                moved = [k[x][comp].at(row, ROWS) for k in (one, two, three)]
-                total = total + (moved[0] + moved[1] + moved[2]) * f[6 + comp]
-            image[2, x, here(row)] = total
+                moved[comp] = value if 1 <= x < last else before + value
+            if not 2 <= x < last:
+                for comp in VEL:
+                    moved[comp] = three[x][comp].at(row, ROWS)
+                    if not x:
+                        moved[comp] = two[x][comp].at(row, ROWS) + moved[comp]
+            for n, value in enumerate(imaged(moved, forward, x, row)):
+                before = known[n, x, here(row)]
+                image[n, x, here(row)] = before if value is None else before + value
 
     if groups != 2:
         images[0][...] = image[...]
@@ -639,42 +660,43 @@
             )
 
 
-def smooth_kernel(by_pair, by_next, grad, full, half, weights, out, low, high, beside, result):
+def side_kernel(near, *refs):
+    got, *refs = refs
+    if not near:
+        _, *refs = refs
+    grad, full, half, weights, out, beside, result, sems = refs
     width, count, size_z = grad.shape[1:]
     own = count - BY
-    last = width - 1
     me = lax.axis_index("shot")
     first = pl.multiple_of(me * BY, BY)
     mine = pl.ds(first, own)
     edge = pl.ds(edge_row(me, own), 1)
-    take_in(by_pair, by_next, low, high)
+    upper = is_even() if near else jnp.logical_not(is_even())
+    end = jnp.where(upper, width - 1, 0)
+    inner = jnp.where(upper, width - 2, 1)
     beside[...] = jnp.zeros(beside.shape, jnp.float32)
-    for side, got in enumerate((low, high)):
-        for n in range(3):
-            beside[side, n, mine, :] = got[2 * n * own : (2 * n + 1) * own, :]
-            beside[side, n, edge, :] = got[6 * own + n : 6 * own + n + 1, :]
-            beside[side, 3 + n, mine, :] = got[(2 * n + 1) * own : (2 * n + 2) * own, :]
-        for j in range(own // BY):
-            row = got[6 * own + 3 + j : 6 * own + 4 + j, :]
-            to = pl.ds(pl.multiple_of(first + j * BY, BY), BY)
-            beside[side, 6, to, :] = jnp.broadcast_to(row, (BY, size_z))
+    for n in range(3):
+        beside[n, mine, :] = got[2 * n * own : (2 * n + 1) * own, :]
+        beside[n, edge, :] = got[6 * own + n : 6 * own + n + 1, :]
+        beside[3 + n, mine, :] = got[(2 * n + 1) * own : (2 * n + 2) * own, :]
+    for j in range(own // BY):
+        row = got[6 * own + 3 + j : 6 * own + 4 + j, :]
+        to = pl.ds(pl.multiple_of(first + j * BY, BY), BY)
+        beside[6, to, :] = jnp.broadcast_to(row, (BY, size_z))
     w = [weights[k] for k in range(3)]
     for n in range(3):
-        ends = [full[n, x] + w[0] * beside[side, n] for side, x in ((0, 0), (1, last))]
-        outer = [
-            beside[side, 3 + n] + beside[side, 6] * grad[n, x] for side, x in ((0, 0), (1, last))
-        ]
-        result[0] = sweep(ends[0], outer[0], full[n, 1], w)
-        result[last] = sweep(ends[1], full[n, last - 1], outer[1], w)
-        for x in range(1, last):
-            value = half[n, x - 1]
-            if x == 1:
-                value = value + w[0] * ends[0]
-            if x == last - 1:
-                value = value + w[0] * ends[1]
-            result[x] = value
-        for x in range(width):
-            out[n, x] = result[x, mine, :]
+        value = full[n, end] + w[0] * beside[n]
+        outer = beside[3 + n] + beside[6] * grad[n, end]
+        result[n, 0] = sweep(value, outer, full[n, inner], w)
+        result[n, 1] = half[n, inner - 1] + w[0] * value
+    copies = [
+        pltpu.make_async_copy(result.at[:, k, mine, :], out.at[:, x], sems.at[k])
+        for k, x in enumerate((end, inner))
+    ]
+    for copy in copies:
+        copy.start()
+    for copy in copies:
+        copy.wait()
 
 
 def extended(block, sides, width):
@@ -731,16 +753,18 @@
     return pltpu.with_memory_space_constraint(array, pltpu.HBM)
 
 
-def call(kernel, outs, args, scratch, scalars=(), space=VMEM):
+def call(kernel, outs, args, scratch, scalars=(), space=VMEM, out_space=VMEM, held=None):
+    specs = [SMEM if n in scalars else HBM if n == held else space for n in range(len(args))]
     return pl.pallas_call(
         kernel,
         out_shape=outs,
-        in_specs=[SMEM if n in scalars else space for n in range(len(args))],
-        out_specs=jax.tree.map(lambda _: VMEM, outs),
+        in_specs=specs,
+        out_specs=jax.tree.map(lambda _: out_space, outs),
         scratch_shapes=[
             pltpu.VMEM(shape, jnp.float32) if isinstance(shape, tuple) else shape
             for shape in scratch
         ],
+        input_output_aliases={} if held is None else {held: 0},
         compiler_params=pltpu.CompilerParams(vmem_limit_bytes=24 * 1024 * 1024),
     )(*args)
 
@@ -801,10 +825,11 @@
         outs = [f32(3, held, size_z)]
         scratch += [(held, size_z)]
         scalars = (3,)
-    end, w, third, outer, parts, *weights = call(
+    three = f32(3, width, *plane)
+    end, w, third, outer, parts, known, *weights = call(
         functools.partial(near_kernel, groups),
-        [f32(2, 9, *plane), grid, f32(3, width, *plane), f32(7, *plane), f32(4, 3, *plane), *outs],
-        [*args, state, st, coef, cells, push],
+        [f32(2, 9, *plane), grid, three, f32(7, *plane), f32(4, 3, *plane), three, *outs],
+        [*args, state, st, coef, cells, push, forward],
         scratch,
         scalars,
     )
@@ -813,7 +838,7 @@
     final, *images = call(
         functools.partial(far_kernel, groups),
         [pltpu.VMEM(grid.shape, grid.dtype), *images],
-        [late_pair, late_next, st, end, w, third, outer, parts, coef, push, forward],
+        [late_pair, late_next, st, end, w, third, outer, parts, known, coef, push, forward],
         [(6, *plane), (6, *plane), (2, 9, *plane), (3, *plane), (3, *plane), (3, width, *plane)],
     )
     if groups != 2:
@@ -835,11 +860,19 @@
         (grad, swept, weights),
         [],
     )
+    gradient = f32(3, width, owned, size_z)
+    scratch = [(7, held, size_z), (3, 2, held, size_z), pltpu.SemaphoreType.DMA((2,))]
+    rest = (grad, full, half, weights)
     gradient = call(
-        smooth_kernel,
-        f32(3, width, owned, size_z),
-        (by_pair, by_next, grad, full, half, weights),
-        [message, message, (2, 7, held, size_z), (width, held, size_z)],
+        functools.partial(side_kernel, True), gradient, (by_pair, *rest), scratch, out_space=HBM
+    )
+    gradient = call(
+        functools.partial(side_kernel, False),
+        f32(*gradient.shape),
+        (by_next, gradient, *rest),
+        scratch,
+        out_space=HBM,
+        held=1,
     )
     return final[None], gradient
 

time: 34.7 us -> 34.4 us (level)
  waiting for transfers between devices: 11.6 us -> 10.6 us
  Pallas kernels: 5.77 us -> 6.48 us
    ppermute x6, waiting for transfers between devices: 8.72 us -> 7.78 us  [both_ways(): out.append(lax.ppermute(array, 'tile', pairs + [(b, a) for a, b in pairs]))]
    pallas_call x7 -> x8, Pallas kernels: 5.77 us -> 6.48 us  [call(): pl.pallas_call(kernel, out_shape=outs, in_specs=specs, out_specs=jax.tree...]
  transfers between devices with their start and end apart: 8 -> 8, of which waited for: 5 -> 5; matrix products, arithmetic and copies ran while one was open for 3% -> 3% of each run, Pallas kernels for 7% -> 10%
where the time goes in v5:
time: 34.4 us; the launch traced here: 34.3 us
  starting transfers between devices  15.2 us (44%)
  waiting for transfers between devices  10.6 us (31%)
  Pallas kernels  6.48 us (19%)
  local copies, waits for them, and re-layouts  1.06 us (3%)
  between operations  0.84 us (2%)
    ppermute x6, starting transfers between devices, both_ways(): out.append(lax.ppermute(array, 'tile', pairs + [(b, a) for a, b in pairs]))  15.1 us
    ppermute x6, waiting for transfers between devices, both_ways(): out.append(lax.ppermute(array, 'tile', pairs + [(b, a) for a, b in pairs]))  7.78 us
    pallas_call x8, Pallas kernels, call(): pl.pallas_call(kernel, out_shape=outs, in_specs=specs, out_specs=jax.tree...  6.48 us
    ppermute x1, waiting for transfers between devices, local(): received = lax.ppermute(give, 'shot', [(0, 1), (1, 0)])  1.5 us
    ppermute x1, waiting for transfers between devices, local(): swapped = lax.ppermute(swapped, 'shot', [(0, 1), (1, 0)])  1.34 us
    unnamed x15, local copies, waits for them, and re-layouts  1.05 us
  transfers between devices with their start and end apart: 8, of which 5 were waited for; matrix products, arithmetic and copies ran while one was open for 3% of the time, Pallas kernels for 10%

profile of v5, /device:TPU:8, one launch (start us, length us, event | category | flops | bytes accessed | tf_op | source)
XLA Modules:
  0.0 34.3 jit_solution(10860979801933245714)
XLA Ops:
  0.7 1.4 %shard_map.95 = (f32[320,128]{1,0:T(8,128)S(1)}, f32[320,128]{1,0:T(8,128)S(1)}, f32[64,128]{1,0:T(8,128)S(1)}, f32[8,128]{1,0:T(8,128)S(1)}) custom-call(s32[1,4,8]{2,1,0:T(4,128)} %bitcast.13, s32[1,4,4]{2,1,0:T(4,128)} %refs_3_.1, f32[9,4,64,128]{3,2,1,0:T(8,128)} %bitcast.6, bf16[3,4,64,128]{3,2,1,0:T(8,128)(2,1)} %bitcast.11, f32[4,64,128]{2,1,0:T(8,128)} %lame.1, ...), custom_call_target="tpu_custom_call" | custom-call | tf_op jit(solution)/shard_map/pallas_call | solution.py:758
  2.1 0.0 copy-start.1
  2.1 0.0 copy-start.6
  2.2 1.6 %collective-permute-start.2 = (f32[320,128]{1,0:T(8,128)S(1)}, f32[320,128]{1,0:T(8,128)S(1)}, u32[]{:S(2)}, u32[]{:S(2)}) collective-permute-start(f32[320,128]{1,0:T(8,128)S(1)} %get-tuple-element.31), channel_id=1, source_target_pairs={{0,1},{2,3},{4,5},{6,7},{8,9},{10,11},{12,13},{14,15},{1,0},{3,2},... | collective-permute-start | bytes 491528 | tf_op jit(solution)/shard_map/ppermute | solution.py:744
  3.7 3.3 %collective-permute-start.3 = (f32[320,128]{1,0:T(8,128)S(1)}, f32[320,128]{1,0:T(8,128)S(1)}, u32[]{:S(2)}, u32[]{:S(2)}) collective-permute-start(f32[320,128]{1,0:T(8,128)S(1)} %get-tuple-element.32), channel_id=1, source_target_pairs={{1,2},{3,4},{5,6},{7,8},{9,10},{11,12},{13,14},{2,1},{4,3},{6,5},{... | collective-permute-start | bytes 491528 | tf_op jit(solution)/shard_map/ppermute | solution.py:744
  7.0 0.0 copy-done.3
  7.0 0.0 copy-done.5
  7.0 0.0 copy-done.4
  7.0 0.0 copy-done.2
  7.0 0.0 copy-done
  7.0 0.8 %shard_map.96 = (f32[6,64,128]{2,1,0:T(8,128)S(1)}, f32[6,64,128]{2,1,0:T(8,128)S(1)}, f32[9,4,64,128]{3,2,1,0:T(8,128)S(1)}, f32[3,4,64,128]{3,2,1,0:T(8,128)S(1)}, f32[3,4,64,128]{3,2,1,0:T(8,128)S(1)}) custom-call(f32[9,4,64,128]{3,2,1,0:T(8,128)S(1)} %bitcast.7, bf16[3,4,64,128]{3,2,1,0:T(8,128)(2,1)S(1)} %bitcast.12, f32[4,64,128]{2,1,0:T(8,128)S(1)} %copy-done.3, ...), custom_call_target="tpu_custom_call" | custom-call | tf_op jit(solution)/shard_map/pallas_call | solution.py:758
  7.8 1.7 %collective-permute-start = (f32[6,64,128]{2,1,0:T(8,128)S(1)}, f32[6,64,128]{2,1,0:T(8,128)S(1)}, u32[]{:S(2)}, u32[]{:S(2)}) collective-permute-start(f32[6,64,128]{2,1,0:T(8,128)S(1)} %get-tuple-element.28), channel_id=1, source_target_pairs={{0,1},{2,3},{4,5},{6,7},{8,9},{10,11},{12,13},{14,15},{1,0},{3,2},... | collective-permute-start | bytes 589832 | tf_op jit(solution)/shard_map/ppermute | solution.py:744
  9.5 2.8 %collective-permute-start.1 = (f32[6,64,128]{2,1,0:T(8,128)S(1)}, f32[6,64,128]{2,1,0:T(8,128)S(1)}, u32[]{:S(2)}, u32[]{:S(2)}) collective-permute-start(f32[6,64,128]{2,1,0:T(8,128)S(1)} %get-tuple-element.29), channel_id=1, source_target_pairs={{1,2},{3,4},{5,6},{7,8},{9,10},{11,12},{13,14},{2,1},{4,3},{6,5},{... | collective-permute-start | bytes 589832 | tf_op jit(solution)/shard_map/ppermute | solution.py:744
  12.3 0.0 collective-permute-done.2.refs_0_
  12.3 0.9 %collective-permute-done.3.refs_1_ = f32[320,128]{1,0:T(8,128)S(1)} collective-permute-done((f32[320,128]{1,0:T(8,128)S(1)}, f32[320,128]{1,0:T(8,128)S(1)}, u32[]{:S(2)}, u32[]{:S(2)}) %collective-permute-start.3) | collective-permute-done | bytes 163872 | tf_op jit(solution)/shard_map/ppermute | solution.py:744
  13.2 0.1 collective-permute-start.4
  13.3 1.3 %collective-permute-done.4.refs_2_ = f32[264,128]{1,0:T(8,128)S(1)} collective-permute-done((f32[264,128]{1,0:T(8,128)S(1)}, f32[264,128]{1,0:T(8,128)S(1)}, u32[]{:S(2)}, u32[]{:S(2)}) %collective-permute-start.4) | collective-permute-done | bytes 135200 | tf_op jit(solution)/shard_map/ppermute | solution.py:823
  14.6 1.5 %shard_map.97 = (f32[2,9,64,128]{3,2,1,0:T(8,128)S(1)}, f32[9,4,64,128]{3,2,1,0:T(8,128)S(1)}, f32[3,4,64,128]{3,2,1,0:T(8,128)S(1)}, f32[7,64,128]{2,1,0:T(8,12...) custom-call(f32[320,128]{1,0:T(8,128)S(1)} %collective-permute-done.2.refs_0_, ...), custom_call_target="tpu_custom_call" | custom-call | tf_op jit(solution)/shard_map/pallas_call | solution.py:758
  16.1 3.5 %collective-permute-done.refs_0_ = f32[6,64,128]{2,1,0:T(8,128)S(1)} collective-permute-done((f32[6,64,128]{2,1,0:T(8,128)S(1)}, f32[6,64,128]{2,1,0:T(8,128)S(1)}, u32[]{:S(2)}, u32[]{:S(2)}) %collective-permute-start) | collective-permute-done | bytes 196640 | tf_op jit(solution)/shard_map/ppermute | solution.py:744
  19.6 0.0 collective-permute-done.1.refs_1_
  19.6 0.7 %shard_map.98 = (f32[9,4,64,128]{3,2,1,0:T(8,128)S(1)}, f32[3,4,40,128]{3,2,1,0:T(8,128)S(1)}, f32[3,4,40,128]{3,2,1,0:T(8,128)S(1)}) custom-call(f32[6,64,128]{2,1,0:T(8,128)S(1)} %collective-permute-done.refs_0_, f32[6,64,128]{2,1,0:T(8,128)S(1)} %collective-permute-done.1.refs_1_, f32[9,4,64,128]{3,2,1,0:T(8,128)S(1)} %get-tuple-element.30.refs_5_.refs_2_, ...), custom_call_target="tpu_custom_call" | custom-call | tf_op jit(solution)/shard_map/pallas_call | solution.py:758
  20.3 0.1 collective-permute-start.5
  20.4 1.5 %collective-permute-done.5.received = f32[3,4,40,128]{3,2,1,0:T(8,128)S(1)} collective-permute-done((f32[3,4,40,128]{3,2,1,0:T(8,128)S(1)}, f32[3,4,40,128]{3,2,1,0:T(8,128)S(1)}, u32[]{:S(2)}, u32[]{:S(2)}) %collective-permute-start.5) | collective-permute-done | bytes 245792 | tf_op jit(solution)/shard_map/ppermute | solution.py:848
  21.9 0.2 shard_map.99
  22.1 3.0 %collective-permute-start.7 = (f32[200,128]{1,0:T(8,128)S(1)}, f32[200,128]{1,0:T(8,128)S(1)}, u32[]{:S(2)}, u32[]{:S(2)}) collective-permute-start(f32[200,128]{1,0:T(8,128)S(1)} %get-tuple-element.47), channel_id=1, source_target_pairs={{0,1},{2,3},{4,5},{6,7},{8,9},{10,11},{12,13},{14,15},{1,0},{3,2},... | collective-permute-start | bytes 307208 | tf_op jit(solution)/shard_map/ppermute | solution.py:744
  25.1 2.8 %collective-permute-start.6 = (f32[200,128]{1,0:T(8,128)S(1)}, f32[200,128]{1,0:T(8,128)S(1)}, u32[]{:S(2)}, u32[]{:S(2)}) collective-permute-start(f32[200,128]{1,0:T(8,128)S(1)} %get-tuple-element.46), channel_id=1, source_target_pairs={{1,2},{3,4},{5,6},{7,8},{9,10},{11,12},{13,14},{2,1},{4,3},{6,5},{... | collective-permute-start | bytes 307208 | tf_op jit(solution)/shard_map/ppermute | solution.py:744
  27.9 1.0 %copy.12 = f32[1,9,4,64,128]{4,3,2,1,0:T(8,128)} copy(f32[1,9,4,64,128]{4,3,2,1,0:T(8,128)S(1)} %bitcast.5) | data formatting | bytes 2359296
  28.9 0.3 shard_map.100
  29.2 0.0 collective-permute-done.7.refs_0_
  29.2 0.8 %shard_map.101.refs_1_ = f32[3,4,32,128]{3,2,1,0:T(8,128)} custom-call(f32[200,128]{1,0:T(8,128)S(1)} %collective-permute-done.7.refs_0_, f32[3,4,40,128]{3,2,1,0:T(8,128)S(1)} %get-tuple-element.48.grad.refs_1_.refs_2_, f32[3,4,40,128]{3,2,1,0:T(8,128)S(1)} %get-tuple-element.50.refs_2_.refs_3_, f32[3,2,40,128]{3,2,1,0:T(8,128)S(1)} %get-tuple-element.51.refs_3_.refs_4_, ...), custom_call_target="tpu_custom_call" | custom-call | tf_op jit(solution)/shard_map/pallas_call | solution.py:758
  30.0 3.4 %collective-permute-done.6.refs_0_ = f32[200,128]{1,0:T(8,128)S(1)} collective-permute-done((f32[200,128]{1,0:T(8,128)S(1)}, f32[200,128]{1,0:T(8,128)S(1)}, u32[]{:S(2)}, u32[]{:S(2)}) %collective-permute-start.6) | collective-permute-done | bytes 102432 | tf_op jit(solution)/shard_map/ppermute | solution.py:744
  33.5 0.8 %shard_map.102 = f32[3,4,32,128]{3,2,1,0:T(8,128)} custom-call(f32[200,128]{1,0:T(8,128)S(1)} %collective-permute-done.6.refs_0_, f32[3,4,32,128]{3,2,1,0:T(8,128)} %shard_map.101.refs_1_, f32[3,4,40,128]{3,2,1,0:T(8,128)S(1)} %get-tuple-element.48.grad.refs_1_.refs_2_, ...), custom_call_target="tpu_custom_call", output_to_operand_aliasing={{}: (1, {})} | custom-call | tf_op jit(solution)/shard_map/pallas_call | solution.py:758
  (10 shorter events, 0.0 us)
Async XLA Ops:
  0.6 6.4 %copy-start.3 = (f32[4,64,128]{2,1,0:T(8,128)S(1)}, f32[4,64,128]{2,1,0:T(8,128)}, u32[]{:S(2)}) copy-start(f32[4,64,128]{2,1,0:T(8,128)} %buoyancy.1) | copy-start | bytes 393220
  0.6 6.4 %copy-start.5 = (f32[4,64,128]{2,1,0:T(8,128)S(1)}, f32[4,64,128]{2,1,0:T(8,128)}, u32[]{:S(2)}) copy-start(f32[4,64,128]{2,1,0:T(8,128)} %shear.1) | copy-start | bytes 393220
  0.7 6.4 %copy-start.4 = (f32[4,64,128]{2,1,0:T(8,128)S(1)}, f32[4,64,128]{2,1,0:T(8,128)}, u32[]{:S(2)}) copy-start(f32[4,64,128]{2,1,0:T(8,128)} %lame.1) | copy-start | bytes 393220
  0.7 6.4 %copy-start.2 = (bf16[1,3,4,64,128]{4,3,2,1,0:T(8,128)(2,1)S(1)}, bf16[1,3,4,64,128]{4,3,2,1,0:T(8,128)(2,1)}, u32[]{:S(2)}) copy-start(bf16[1,3,4,64,128]{4,3,2,1,0:T(8,128)(2,1)} %param.9) | copy-start | bytes 589828
  0.7 6.4 %copy-start = (f32[1,9,4,64,128]{4,3,2,1,0:T(8,128)S(1)}, f32[1,9,4,64,128]{4,3,2,1,0:T(8,128)}, u32[]{:S(2)}) copy-start(f32[1,9,4,64,128]{4,3,2,1,0:T(8,128)} %param.8) | copy-start | bytes 3538948
  2.1 12.5 %copy-start.1 = (bf16[1,9,4,64,128]{4,3,2,1,0:T(8,128)(2,1)S(1)}, bf16[1,9,4,64,128]{4,3,2,1,0:T(8,128)(2,1)}, u32[]{:S(2)}) copy-start(bf16[1,9,4,64,128]{4,3,2,1,0:T(8,128)(2,1)} %param.10) | copy-start | bytes 1769476
  2.1 12.5 %copy-start.6 = (s32[1,4,4]{2,1,0:T(4,128)S(1)}, s32[1,4,4]{2,1,0:T(4,128)}, u32[]{:S(2)}) copy-start(s32[1,4,4]{2,1,0:T(4,128)} %refs_3_.1) | copy-start | bytes 196
  2.2 10.1 %collective-permute-start.2 = (f32[320,128]{1,0:T(8,128)S(1)}, f32[320,128]{1,0:T(8,128)S(1)}, u32[]{:S(2)}, u32[]{:S(2)}) collective-permute-start(f32[320,128]{1,0:T(8,128)S(1)} %get-tuple-element.31), channel_id=1, source_target_pairs={{0,1},{2,3},{4,5},{6,7},{8,9},{10,11},{12,13},{14,15},{1,0},{3,2},... | collective-permute-start | bytes 491528 | tf_op jit(solution)/shard_map/ppermute | solution.py:744
  3.7 9.4 %collective-permute-start.3 = (f32[320,128]{1,0:T(8,128)S(1)}, f32[320,128]{1,0:T(8,128)S(1)}, u32[]{:S(2)}, u32[]{:S(2)}) collective-permute-start(f32[320,128]{1,0:T(8,128)S(1)} %get-tuple-element.32), channel_id=1, source_target_pairs={{1,2},{3,4},{5,6},{7,8},{9,10},{11,12},{13,14},{2,1},{4,3},{6,5},{... | collective-permute-start | bytes 491528 | tf_op jit(solution)/shard_map/ppermute | solution.py:744
  7.8 11.8 %collective-permute-start = (f32[6,64,128]{2,1,0:T(8,128)S(1)}, f32[6,64,128]{2,1,0:T(8,128)S(1)}, u32[]{:S(2)}, u32[]{:S(2)}) collective-permute-start(f32[6,64,128]{2,1,0:T(8,128)S(1)} %get-tuple-element.28), channel_id=1, source_target_pairs={{0,1},{2,3},{4,5},{6,7},{8,9},{10,11},{12,13},{14,15},{1,0},{3,2},... | collective-permute-start | bytes 589832 | tf_op jit(solution)/shard_map/ppermute | solution.py:744
  9.5 10.1 %collective-permute-start.1 = (f32[6,64,128]{2,1,0:T(8,128)S(1)}, f32[6,64,128]{2,1,0:T(8,128)S(1)}, u32[]{:S(2)}, u32[]{:S(2)}) collective-permute-start(f32[6,64,128]{2,1,0:T(8,128)S(1)} %get-tuple-element.29), channel_id=1, source_target_pairs={{1,2},{3,4},{5,6},{7,8},{9,10},{11,12},{13,14},{2,1},{4,3},{6,5},{... | collective-permute-start | bytes 589832 | tf_op jit(solution)/shard_map/ppermute | solution.py:744
  13.2 1.4 %collective-permute-start.4 = (f32[264,128]{1,0:T(8,128)S(1)}, f32[264,128]{1,0:T(8,128)S(1)}, u32[]{:S(2)}, u32[]{:S(2)}) collective-permute-start(f32[264,128]{1,0:T(8,128)S(1)} %pad_maximum_fusion), channel_id=1, source_target_pairs={{0,16},{16,0},{1,17},{17,1},{2,18},{18,2},{3,19},{19,3},{4,20},{20... | collective-permute-start | bytes 405512 | tf_op jit(solution)/shard_map/ppermute | solution.py:823
  20.3 1.6 %collective-permute-start.5 = (f32[3,4,40,128]{3,2,1,0:T(8,128)S(1)}, f32[3,4,40,128]{3,2,1,0:T(8,128)S(1)}, u32[]{:S(2)}, u32[]{:S(2)}) collective-permute-start(f32[3,4,40,128]{3,2,1,0:T(8,128)S(1)} %get-tuple-element.44), channel_id=1, source_target_pairs={{0,16},{16,0},{1,17},{17,1},{2,18},{18,2},{3,19},{19,3},{4,20},{20... | collective-permute-start | bytes 737288 | tf_op jit(solution)/shard_map/ppermute | solution.py:848
  22.1 7.1 %collective-permute-start.7 = (f32[200,128]{1,0:T(8,128)S(1)}, f32[200,128]{1,0:T(8,128)S(1)}, u32[]{:S(2)}, u32[]{:S(2)}) collective-permute-start(f32[200,128]{1,0:T(8,128)S(1)} %get-tuple-element.47), channel_id=1, source_target_pairs={{0,1},{2,3},{4,5},{6,7},{8,9},{10,11},{12,13},{14,15},{1,0},{3,2},... | collective-permute-start | bytes 307208 | tf_op jit(solution)/shard_map/ppermute | solution.py:744
  25.1 8.3 %collective-permute-start.6 = (f32[200,128]{1,0:T(8,128)S(1)}, f32[200,128]{1,0:T(8,128)S(1)}, u32[]{:S(2)}, u32[]{:S(2)}) collective-permute-start(f32[200,128]{1,0:T(8,128)S(1)} %get-tuple-element.46), channel_id=1, source_target_pairs={{1,2},{3,4},{5,6},{7,8},{9,10},{11,12},{13,14},{2,1},{4,3},{6,5},{... | collective-permute-start | bytes 307208 | tf_op jit(solution)/shard_map/ppermute | solution.py:744

commit v6 on v5

--- a/solution.py
+++ b/solution.py
@@ -810,7 +810,7 @@
     late_pair, late_next, st, push, coef = call(
         late_kernel,
         [f32(6, *plane), f32(6, *plane), grid, f32(STEPS, width, *plane), f32(3, width, *plane)],
-        (state, source, buoyancy, lame_first, shear_modulus, cells),
+        [*(in_hbm(a) for a in (state, source, buoyancy, lame_first, shear_modulus)), cells],
         [(3, 3, *plane), (6, *plane), (6, *plane), (6, *plane)],
     )
     late_pair, late_next = both_ways(late_pair, late_next)

time: 34.4 us -> 34.3 us (level)
  Pallas kernels: 6.48 us -> 7.85 us
  starting transfers between devices: 15.2 us -> 14.3 us
  waiting for transfers between devices: 10.6 us -> 10.1 us
    pallas_call x8, Pallas kernels: 6.48 us -> 7.85 us  [call(): pl.pallas_call(kernel, out_shape=outs, in_specs=specs, out_specs=jax.tree...]
    ppermute x6, starting transfers between devices: 15.1 us -> 14.2 us  [both_ways(): out.append(lax.ppermute(array, 'tile', pairs + [(b, a) for a, b in pairs]))]
    ppermute x6, waiting for transfers between devices: 7.78 us -> 7.23 us  [both_ways(): out.append(lax.ppermute(array, 'tile', pairs + [(b, a) for a, b in pairs]))]
    unnamed x15 -> x7, local copies, waits for them, and re-layouts: 1.05 us -> 1.03 us
  transfers between devices with their start and end apart: 8 -> 8, of which waited for: 5 -> 5; matrix products, arithmetic and copies ran while one was open for 3% -> 3% of each run, Pallas kernels for 10% -> 14%
where the time goes in v6:
time: 34.3 us; the launch traced here: 34.1 us
  starting transfers between devices  14.3 us (42%)
  waiting for transfers between devices  10.1 us (29%)
  Pallas kernels  7.85 us (23%)
  local copies, waits for them, and re-layouts  1.05 us (3%)
  between operations  0.8 us (2%)
    ppermute x6, starting transfers between devices, both_ways(): out.append(lax.ppermute(array, 'tile', pairs + [(b, a) for a, b in pairs]))  14.2 us
    pallas_call x8, Pallas kernels, call(): pl.pallas_call(kernel, out_shape=outs, in_specs=specs, out_specs=jax.tree...  7.85 us
    ppermute x6, waiting for transfers between devices, both_ways(): out.append(lax.ppermute(array, 'tile', pairs + [(b, a) for a, b in pairs]))  7.23 us
    ppermute x1, waiting for transfers between devices, local(): received = lax.ppermute(give, 'shot', [(0, 1), (1, 0)])  1.5 us
    ppermute x1, waiting for transfers between devices, local(): swapped = lax.ppermute(swapped, 'shot', [(0, 1), (1, 0)])  1.34 us
    unnamed x7, local copies, waits for them, and re-layouts  1.03 us
  transfers between devices with their start and end apart: 8, of which 5 were waited for; matrix products, arithmetic and copies ran while one was open for 3% of the time, Pallas kernels for 14%

profile of v6, /device:TPU:8, one launch (start us, length us, event | category | flops | bytes accessed | tf_op | source)
XLA Modules:
  0.0 34.1 jit_solution(9171000108370372638)
XLA Ops:
  0.6 1.4 %shard_map.95 = (f32[320,128]{1,0:T(8,128)S(1)}, f32[320,128]{1,0:T(8,128)S(1)}, f32[64,128]{1,0:T(8,128)S(1)}, f32[8,128]{1,0:T(8,128)S(1)}) custom-call(s32[1,4,8]{2,1,0:T(4,128)} %bitcast.13, s32[1,4,4]{2,1,0:T(4,128)} %refs_3_.1, f32[9,4,64,128]{3,2,1,0:T(8,128)} %bitcast.6, bf16[3,4,64,128]{3,2,1,0:T(8,128)(2,1)} %bitcast.11, f32[4,64,128]{2,1,0:T(8,128)} %lame.1, ...), custom_call_target="tpu_custom_call" | custom-call | tf_op jit(solution)/shard_map/pallas_call | solution.py:758
  2.0 0.0 copy-start
  2.0 0.0 copy-start.1
  2.0 0.0 copy-start.2
  2.0 1.6 %collective-permute-start.2 = (f32[320,128]{1,0:T(8,128)S(1)}, f32[320,128]{1,0:T(8,128)S(1)}, u32[]{:S(2)}, u32[]{:S(2)}) collective-permute-start(f32[320,128]{1,0:T(8,128)S(1)} %get-tuple-element.31), channel_id=1, source_target_pairs={{0,1},{2,3},{4,5},{6,7},{8,9},{10,11},{12,13},{14,15},{1,0},{3,2},... | collective-permute-start | bytes 491528 | tf_op jit(solution)/shard_map/ppermute | solution.py:744
  3.6 3.3 %collective-permute-start.3 = (f32[320,128]{1,0:T(8,128)S(1)}, f32[320,128]{1,0:T(8,128)S(1)}, u32[]{:S(2)}, u32[]{:S(2)}) collective-permute-start(f32[320,128]{1,0:T(8,128)S(1)} %get-tuple-element.32), channel_id=1, source_target_pairs={{1,2},{3,4},{5,6},{7,8},{9,10},{11,12},{13,14},{2,1},{4,3},{6,5},{... | collective-permute-start | bytes 491528 | tf_op jit(solution)/shard_map/ppermute | solution.py:744
  6.9 2.2 %shard_map.96 = (f32[6,64,128]{2,1,0:T(8,128)S(1)}, f32[6,64,128]{2,1,0:T(8,128)S(1)}, f32[9,4,64,128]{3,2,1,0:T(8,128)S(1)}, f32[3,4,64,128]{3,2,1,0:T(8,128)S(1)}, f32[3,4,64,128]{3,2,1,0:T(8,128)S(1)}) custom-call(f32[9,4,64,128]{3,2,1,0:T(8,128)} %bitcast.7, bf16[3,4,64,128]{3,2,1,0:T(8,128)(2,1)} %bitcast.12, f32[4,64,128]{2,1,0:T(8,128)} %buoyancy.1, ...), custom_call_target="tpu_custom_call" | custom-call | tf_op jit(solution)/shard_map/pallas_call | solution.py:758
  9.1 1.7 %collective-permute-start = (f32[6,64,128]{2,1,0:T(8,128)S(1)}, f32[6,64,128]{2,1,0:T(8,128)S(1)}, u32[]{:S(2)}, u32[]{:S(2)}) collective-permute-start(f32[6,64,128]{2,1,0:T(8,128)S(1)} %get-tuple-element.28), channel_id=1, source_target_pairs={{0,1},{2,3},{4,5},{6,7},{8,9},{10,11},{12,13},{14,15},{1,0},{3,2},... | collective-permute-start | bytes 589832 | tf_op jit(solution)/shard_map/ppermute | solution.py:744
  10.8 2.8 %collective-permute-start.1 = (f32[6,64,128]{2,1,0:T(8,128)S(1)}, f32[6,64,128]{2,1,0:T(8,128)S(1)}, u32[]{:S(2)}, u32[]{:S(2)}) collective-permute-start(f32[6,64,128]{2,1,0:T(8,128)S(1)} %get-tuple-element.29), channel_id=1, source_target_pairs={{1,2},{3,4},{5,6},{7,8},{9,10},{11,12},{13,14},{2,1},{4,3},{6,5},{... | collective-permute-start | bytes 589832 | tf_op jit(solution)/shard_map/ppermute | solution.py:744
  13.6 0.0 collective-permute-done.2.refs_0_
  13.6 0.0 collective-permute-done.3.refs_1_
  13.6 0.1 collective-permute-start.4
  13.7 1.3 %collective-permute-done.4.refs_2_ = f32[264,128]{1,0:T(8,128)S(1)} collective-permute-done((f32[264,128]{1,0:T(8,128)S(1)}, f32[264,128]{1,0:T(8,128)S(1)}, u32[]{:S(2)}, u32[]{:S(2)}) %collective-permute-start.4) | collective-permute-done | bytes 135200 | tf_op jit(solution)/shard_map/ppermute | solution.py:823
  15.1 0.0 copy-done
  15.1 0.0 copy-done.1
  15.1 0.0 copy-done.2
  15.1 1.5 %shard_map.97 = (f32[2,9,64,128]{3,2,1,0:T(8,128)S(1)}, f32[9,4,64,128]{3,2,1,0:T(8,128)S(1)}, f32[3,4,64,128]{3,2,1,0:T(8,128)S(1)}, f32[7,64,128]{2,1,0:T(8,12...) custom-call(f32[320,128]{1,0:T(8,128)S(1)} %collective-permute-done.2.refs_0_, ...), custom_call_target="tpu_custom_call" | custom-call | tf_op jit(solution)/shard_map/pallas_call | solution.py:758
  16.6 3.0 %collective-permute-done.refs_0_ = f32[6,64,128]{2,1,0:T(8,128)S(1)} collective-permute-done((f32[6,64,128]{2,1,0:T(8,128)S(1)}, f32[6,64,128]{2,1,0:T(8,128)S(1)}, u32[]{:S(2)}, u32[]{:S(2)}) %collective-permute-start) | collective-permute-done | bytes 196640 | tf_op jit(solution)/shard_map/ppermute | solution.py:744
  19.6 0.8 %collective-permute-done.1.refs_1_ = f32[6,64,128]{2,1,0:T(8,128)S(1)} collective-permute-done((f32[6,64,128]{2,1,0:T(8,128)S(1)}, f32[6,64,128]{2,1,0:T(8,128)S(1)}, u32[]{:S(2)}, u32[]{:S(2)}) %collective-permute-start.1) | collective-permute-done | bytes 196640 | tf_op jit(solution)/shard_map/ppermute | solution.py:744
  20.4 0.7 %shard_map.98 = (f32[9,4,64,128]{3,2,1,0:T(8,128)S(1)}, f32[3,4,40,128]{3,2,1,0:T(8,128)S(1)}, f32[3,4,40,128]{3,2,1,0:T(8,128)S(1)}) custom-call(f32[6,64,128]{2,1,0:T(8,128)S(1)} %collective-permute-done.refs_0_, f32[6,64,128]{2,1,0:T(8,128)S(1)} %collective-permute-done.1.refs_1_, f32[9,4,64,128]{3,2,1,0:T(8,128)S(1)} %get-tuple-element.30.refs_5_.refs_2_, ...), custom_call_target="tpu_custom_call" | custom-call | tf_op jit(solution)/shard_map/pallas_call | solution.py:758
  21.1 0.1 collective-permute-start.5
  21.2 1.5 %collective-permute-done.5.received = f32[3,4,40,128]{3,2,1,0:T(8,128)S(1)} collective-permute-done((f32[3,4,40,128]{3,2,1,0:T(8,128)S(1)}, f32[3,4,40,128]{3,2,1,0:T(8,128)S(1)}, u32[]{:S(2)}, u32[]{:S(2)}) %collective-permute-start.5) | collective-permute-done | bytes 245792 | tf_op jit(solution)/shard_map/ppermute | solution.py:848
  22.7 0.2 shard_map.99
  22.8 2.1 %collective-permute-start.7 = (f32[200,128]{1,0:T(8,128)S(1)}, f32[200,128]{1,0:T(8,128)S(1)}, u32[]{:S(2)}, u32[]{:S(2)}) collective-permute-start(f32[200,128]{1,0:T(8,128)S(1)} %get-tuple-element.47), channel_id=1, source_target_pairs={{0,1},{2,3},{4,5},{6,7},{8,9},{10,11},{12,13},{14,15},{1,0},{3,2},... | collective-permute-start | bytes 307208 | tf_op jit(solution)/shard_map/ppermute | solution.py:744
  25.0 2.8 %collective-permute-start.6 = (f32[200,128]{1,0:T(8,128)S(1)}, f32[200,128]{1,0:T(8,128)S(1)}, u32[]{:S(2)}, u32[]{:S(2)}) collective-permute-start(f32[200,128]{1,0:T(8,128)S(1)} %get-tuple-element.46), channel_id=1, source_target_pairs={{1,2},{3,4},{5,6},{7,8},{9,10},{11,12},{13,14},{2,1},{4,3},{6,5},{... | collective-permute-start | bytes 307208 | tf_op jit(solution)/shard_map/ppermute | solution.py:744
  27.8 1.0 %copy.12 = f32[1,9,4,64,128]{4,3,2,1,0:T(8,128)} copy(f32[1,9,4,64,128]{4,3,2,1,0:T(8,128)S(1)} %bitcast.5) | data formatting | bytes 2359296
  28.8 0.3 shard_map.100
  29.0 0.0 collective-permute-done.7.refs_0_
  29.1 0.8 %shard_map.101.refs_1_ = f32[3,4,32,128]{3,2,1,0:T(8,128)} custom-call(f32[200,128]{1,0:T(8,128)S(1)} %collective-permute-done.7.refs_0_, f32[3,4,40,128]{3,2,1,0:T(8,128)S(1)} %get-tuple-element.48.grad.refs_1_.refs_2_, f32[3,4,40,128]{3,2,1,0:T(8,128)S(1)} %get-tuple-element.50.refs_2_.refs_3_, f32[3,2,40,128]{3,2,1,0:T(8,128)S(1)} %get-tuple-element.51.refs_3_.refs_4_, ...), custom_call_target="tpu_custom_call" | custom-call | tf_op jit(solution)/shard_map/pallas_call | solution.py:758
  29.9 3.4 %collective-permute-done.6.refs_0_ = f32[200,128]{1,0:T(8,128)S(1)} collective-permute-done((f32[200,128]{1,0:T(8,128)S(1)}, f32[200,128]{1,0:T(8,128)S(1)}, u32[]{:S(2)}, u32[]{:S(2)}) %collective-permute-start.6) | collective-permute-done | bytes 102432 | tf_op jit(solution)/shard_map/ppermute | solution.py:744
  33.3 0.8 %shard_map.102 = f32[3,4,32,128]{3,2,1,0:T(8,128)} custom-call(f32[200,128]{1,0:T(8,128)S(1)} %collective-permute-done.6.refs_0_, f32[3,4,32,128]{3,2,1,0:T(8,128)} %shard_map.101.refs_1_, f32[3,4,40,128]{3,2,1,0:T(8,128)S(1)} %get-tuple-element.48.grad.refs_1_.refs_2_, ...), custom_call_target="tpu_custom_call", output_to_operand_aliasing={{}: (1, {})} | custom-call | tf_op jit(solution)/shard_map/pallas_call | solution.py:758
  (3 shorter events, 0.0 us)
Async XLA Ops:
  2.0 13.1 %copy-start = (f32[1,9,4,64,128]{4,3,2,1,0:T(8,128)S(1)}, f32[1,9,4,64,128]{4,3,2,1,0:T(8,128)}, u32[]{:S(2)}) copy-start(f32[1,9,4,64,128]{4,3,2,1,0:T(8,128)} %param.8) | copy-start | bytes 3538948
  2.0 13.1 %copy-start.1 = (bf16[1,9,4,64,128]{4,3,2,1,0:T(8,128)(2,1)S(1)}, bf16[1,9,4,64,128]{4,3,2,1,0:T(8,128)(2,1)}, u32[]{:S(2)}) copy-start(bf16[1,9,4,64,128]{4,3,2,1,0:T(8,128)(2,1)} %param.10) | copy-start | bytes 1769476
  2.0 13.0 %copy-start.2 = (s32[1,4,4]{2,1,0:T(4,128)S(1)}, s32[1,4,4]{2,1,0:T(4,128)}, u32[]{:S(2)}) copy-start(s32[1,4,4]{2,1,0:T(4,128)} %refs_3_.1) | copy-start | bytes 196
  2.0 11.5 %collective-permute-start.2 = (f32[320,128]{1,0:T(8,128)S(1)}, f32[320,128]{1,0:T(8,128)S(1)}, u32[]{:S(2)}, u32[]{:S(2)}) collective-permute-start(f32[320,128]{1,0:T(8,128)S(1)} %get-tuple-element.31), channel_id=1, source_target_pairs={{0,1},{2,3},{4,5},{6,7},{8,9},{10,11},{12,13},{14,15},{1,0},{3,2},... | collective-permute-start | bytes 491528 | tf_op jit(solution)/shard_map/ppermute | solution.py:744
  3.6 10.0 %collective-permute-start.3 = (f32[320,128]{1,0:T(8,128)S(1)}, f32[320,128]{1,0:T(8,128)S(1)}, u32[]{:S(2)}, u32[]{:S(2)}) collective-permute-start(f32[320,128]{1,0:T(8,128)S(1)} %get-tuple-element.32), channel_id=1, source_target_pairs={{1,2},{3,4},{5,6},{7,8},{9,10},{11,12},{13,14},{2,1},{4,3},{6,5},{... | collective-permute-start | bytes 491528 | tf_op jit(solution)/shard_map/ppermute | solution.py:744
  9.1 10.5 %collective-permute-start = (f32[6,64,128]{2,1,0:T(8,128)S(1)}, f32[6,64,128]{2,1,0:T(8,128)S(1)}, u32[]{:S(2)}, u32[]{:S(2)}) collective-permute-start(f32[6,64,128]{2,1,0:T(8,128)S(1)} %get-tuple-element.28), channel_id=1, source_target_pairs={{0,1},{2,3},{4,5},{6,7},{8,9},{10,11},{12,13},{14,15},{1,0},{3,2},... | collective-permute-start | bytes 589832 | tf_op jit(solution)/shard_map/ppermute | solution.py:744
  10.8 9.6 %collective-permute-start.1 = (f32[6,64,128]{2,1,0:T(8,128)S(1)}, f32[6,64,128]{2,1,0:T(8,128)S(1)}, u32[]{:S(2)}, u32[]{:S(2)}) collective-permute-start(f32[6,64,128]{2,1,0:T(8,128)S(1)} %get-tuple-element.29), channel_id=1, source_target_pairs={{1,2},{3,4},{5,6},{7,8},{9,10},{11,12},{13,14},{2,1},{4,3},{6,5},{... | collective-permute-start | bytes 589832 | tf_op jit(solution)/shard_map/ppermute | solution.py:744
  13.6 1.4 %collective-permute-start.4 = (f32[264,128]{1,0:T(8,128)S(1)}, f32[264,128]{1,0:T(8,128)S(1)}, u32[]{:S(2)}, u32[]{:S(2)}) collective-permute-start(f32[264,128]{1,0:T(8,128)S(1)} %pad_maximum_fusion), channel_id=1, source_target_pairs={{0,16},{16,0},{1,17},{17,1},{2,18},{18,2},{3,19},{19,3},{4,20},{20... | collective-permute-start | bytes 405512 | tf_op jit(solution)/shard_map/ppermute | solution.py:823
  21.1 1.6 %collective-permute-start.5 = (f32[3,4,40,128]{3,2,1,0:T(8,128)S(1)}, f32[3,4,40,128]{3,2,1,0:T(8,128)S(1)}, u32[]{:S(2)}, u32[]{:S(2)}) collective-permute-start(f32[3,4,40,128]{3,2,1,0:T(8,128)S(1)} %get-tuple-element.44), channel_id=1, source_target_pairs={{0,16},{16,0},{1,17},{17,1},{2,18},{18,2},{3,19},{19,3},{4,20},{20... | collective-permute-start | bytes 737288 | tf_op jit(solution)/shard_map/ppermute | solution.py:848
  22.8 6.2 %collective-permute-start.7 = (f32[200,128]{1,0:T(8,128)S(1)}, f32[200,128]{1,0:T(8,128)S(1)}, u32[]{:S(2)}, u32[]{:S(2)}) collective-permute-start(f32[200,128]{1,0:T(8,128)S(1)} %get-tuple-element.47), channel_id=1, source_target_pairs={{0,1},{2,3},{4,5},{6,7},{8,9},{10,11},{12,13},{14,15},{1,0},{3,2},... | collective-permute-start | bytes 307208 | tf_op jit(solution)/shard_map/ppermute | solution.py:744
  25.0 8.3 %collective-permute-start.6 = (f32[200,128]{1,0:T(8,128)S(1)}, f32[200,128]{1,0:T(8,128)S(1)}, u32[]{:S(2)}, u32[]{:S(2)}) collective-permute-start(f32[200,128]{1,0:T(8,128)S(1)} %get-tuple-element.46), channel_id=1, source_target_pairs={{1,2},{3,4},{5,6},{7,8},{9,10},{11,12},{13,14},{2,1},{4,3},{6,5},{... | collective-permute-start | bytes 307208 | tf_op jit(solution)/shard_map/ppermute | solution.py:744

commit v7 on v6

--- a/solution.py
+++ b/solution.py
@@ -163,6 +163,20 @@
     def _():
         low[...] = by_pair[...]
         high[...] = by_next[...]
+
+    clear_ends(low, high)
+
+
+def no_neighbour(upper):
+    return lax.axis_index("tile") == (lax.axis_size("tile") - 1 if upper else 0)
+
+
+def clear_ends(low, high):
+    for upper, ref in ((False, low), (True, high)):
+
+        @pl.when(no_neighbour(upper))
+        def _(ref=ref):
+            ref[...] = jnp.zeros(ref.shape, jnp.float32)
 
 
 def class_tile(orientation, j, size_z):
@@ -369,6 +383,7 @@
             if n < 3:
                 outer[n] = low[base + n * count : base + (n + 1) * count]
             outer[3 + n] = high[base + n * count : base + (n + 1) * count]
+    clear_ends(outer.at[0:3], outer.at[3:7])
 
     def coefs(x, row):
         if x < 0:
@@ -683,6 +698,10 @@
         row = got[6 * own + 3 + j : 6 * own + 4 + j, :]
         to = pl.ds(pl.multiple_of(first + j * BY, BY), BY)
         beside[6, to, :] = jnp.broadcast_to(row, (BY, size_z))
+    @pl.when(jnp.where(upper, no_neighbour(True), no_neighbour(False)))
+    def _():
+        beside[...] = jnp.zeros(beside.shape, jnp.float32)
+
     w = [weights[k] for k in range(3)]
     for n in range(3):
         value = full[n, end] + w[0] * beside[n]
@@ -737,11 +756,18 @@
 
 
 def both_ways(by_pair, by_next):
-    count = lax.axis_size("tile")
+    count, groups = lax.axis_size("tile"), lax.axis_size("shot")
     out = []
     for array, start in ((by_pair, 0), (by_next, 1)):
-        pairs = [(i, i + 1) for i in range(start, count - 1, 2)]
-        out.append(lax.ppermute(array, "tile", pairs + [(b, a) for a, b in pairs]))
+        to = {}
+        for i in range(start, count - 1, 2):
+            to[i], to[i + 1] = i + 1, i
+        pairs = [
+            (shot * count + i, shot * count + to[i] if i in to else (shot + 1) % groups * count + i)
+            for shot in range(groups)
+            for i in range(count)
+        ]
+        out.append(lax.ppermute(array, ("shot", "tile"), pairs))
     return out
 
 

time: 34.3 us -> 32.8 us (0.956); the launches traced: 34.1 us -> 32.2 us
  starting transfers between devices: 14.3 us -> 9.41 us
  waiting for transfers between devices: 10.1 us -> 13.1 us
    ppermute x6, starting transfers between devices: 14.2 us -> 9.15 us  [both_ways(): out.append(lax.ppermute(array, ('shot', 'tile'), pairs))]
    ppermute x6, waiting for transfers between devices: 7.23 us -> 10.4 us  [both_ways(): out.append(lax.ppermute(array, ('shot', 'tile'), pairs))]
  transfers between devices with their start and end apart: 8 -> 8, of which waited for: 5 -> 5; matrix products, arithmetic and copies ran while one was open for 3% -> 3% of each run, Pallas kernels for 14% -> 15%
where the time goes in v7:
time: 32.8 us; the launch traced here: 32.2 us
  waiting for transfers between devices  13.1 us (40%)
  starting transfers between devices  9.41 us (29%)
  Pallas kernels  7.86 us (24%)
  local copies, waits for them, and re-layouts  1.04 us (3%)
  between operations  0.74 us (2%)
    ppermute x6, waiting for transfers between devices, both_ways(): out.append(lax.ppermute(array, ('shot', 'tile'), pairs))  10.4 us
    ppermute x6, starting transfers between devices, both_ways(): out.append(lax.ppermute(array, ('shot', 'tile'), pairs))  9.15 us
    pallas_call x8, Pallas kernels, call(): pl.pallas_call(kernel, out_shape=outs, in_specs=specs, out_specs=jax.tree...  7.86 us
    ppermute x1, waiting for transfers between devices, local(): received = lax.ppermute(give, 'shot', [(0, 1), (1, 0)])  1.38 us
    ppermute x1, waiting for transfers between devices, local(): swapped = lax.ppermute(swapped, 'shot', [(0, 1), (1, 0)])  1.34 us
    unnamed x7, local copies, waits for them, and re-layouts  1.03 us
  transfers between devices with their start and end apart: 8, of which 5 were waited for; matrix products, arithmetic and copies ran while one was open for 3% of the time, Pallas kernels for 15%

profile of v7, /device:TPU:8, one launch (start us, length us, event | category | flops | bytes accessed | tf_op | source)
XLA Modules:
  0.0 32.2 jit_solution(6938140155325871330)
XLA Ops:
  0.6 1.4 %shard_map.95 = (f32[320,128]{1,0:T(8,128)S(1)}, f32[320,128]{1,0:T(8,128)S(1)}, f32[64,128]{1,0:T(8,128)S(1)}, f32[8,128]{1,0:T(8,128)S(1)}) custom-call(s32[1,4,8]{2,1,0:T(4,128)} %bitcast.13, s32[1,4,4]{2,1,0:T(4,128)} %refs_3_.1, f32[9,4,64,128]{3,2,1,0:T(8,128)} %bitcast.6, bf16[3,4,64,128]{3,2,1,0:T(8,128)(2,1)} %bitcast.11, f32[4,64,128]{2,1,0:T(8,128)} %lame.1, ...), custom_call_target="tpu_custom_call" | custom-call | tf_op jit(solution)/shard_map/pallas_call | solution.py:784
  2.0 0.0 copy-start
  2.0 0.0 copy-start.1
  2.0 0.0 copy-start.2
  2.0 1.6 %collective-permute-start.2 = (f32[320,128]{1,0:T(8,128)S(1)}, f32[320,128]{1,0:T(8,128)S(1)}, u32[]{:S(2)}, u32[]{:S(2)}) collective-permute-start(f32[320,128]{1,0:T(8,128)S(1)} %get-tuple-element.31), channel_id=1, source_target_pairs={{0,1},{1,0},{2,3},{3,2},{4,5},{5,4},{6,7},{7,6},{8,9},{9,8},{10,11... | collective-permute-start | bytes 491528 | tf_op jit(solution)/shard_map/ppermute | solution.py:770
  3.6 1.4 %collective-permute-start.3 = (f32[320,128]{1,0:T(8,128)S(1)}, f32[320,128]{1,0:T(8,128)S(1)}, u32[]{:S(2)}, u32[]{:S(2)}) collective-permute-start(f32[320,128]{1,0:T(8,128)S(1)} %get-tuple-element.32), channel_id=1, source_target_pairs={{0,16},{1,2},{2,1},{3,4},{4,3},{5,6},{6,5},{7,8},{8,7},{9,10},{10,... | collective-permute-start | bytes 491528 | tf_op jit(solution)/shard_map/ppermute | solution.py:770
  5.0 2.2 %shard_map.96 = (f32[6,64,128]{2,1,0:T(8,128)S(1)}, f32[6,64,128]{2,1,0:T(8,128)S(1)}, f32[9,4,64,128]{3,2,1,0:T(8,128)S(1)}, f32[3,4,64,128]{3,2,1,0:T(8,128)S(1)}, f32[3,4,64,128]{3,2,1,0:T(8,128)S(1)}) custom-call(f32[9,4,64,128]{3,2,1,0:T(8,128)} %bitcast.7, bf16[3,4,64,128]{3,2,1,0:T(8,128)(2,1)} %bitcast.12, f32[4,64,128]{2,1,0:T(8,128)} %buoyancy.1, ...), custom_call_target="tpu_custom_call" | custom-call | tf_op jit(solution)/shard_map/pallas_call | solution.py:784
  7.2 1.7 %collective-permute-start = (f32[6,64,128]{2,1,0:T(8,128)S(1)}, f32[6,64,128]{2,1,0:T(8,128)S(1)}, u32[]{:S(2)}, u32[]{:S(2)}) collective-permute-start(f32[6,64,128]{2,1,0:T(8,128)S(1)} %get-tuple-element.28), channel_id=1, source_target_pairs={{0,1},{1,0},{2,3},{3,2},{4,5},{5,4},{6,7},{7,6},{8,9},{9,8},{10,11... | collective-permute-start | bytes 589832 | tf_op jit(solution)/shard_map/ppermute | solution.py:770
  8.9 0.9 %collective-permute-start.1 = (f32[6,64,128]{2,1,0:T(8,128)S(1)}, f32[6,64,128]{2,1,0:T(8,128)S(1)}, u32[]{:S(2)}, u32[]{:S(2)}) collective-permute-start(f32[6,64,128]{2,1,0:T(8,128)S(1)} %get-tuple-element.29), channel_id=1, source_target_pairs={{0,16},{1,2},{2,1},{3,4},{4,3},{5,6},{6,5},{7,8},{8,7},{9,10},{10,... | collective-permute-start | bytes 589832 | tf_op jit(solution)/shard_map/ppermute | solution.py:770
  9.8 6.1 %collective-permute-done.2.refs_0_ = f32[320,128]{1,0:T(8,128)S(1)} collective-permute-done((f32[320,128]{1,0:T(8,128)S(1)}, f32[320,128]{1,0:T(8,128)S(1)}, u32[]{:S(2)}, u32[]{:S(2)}) %collective-permute-start.2) | collective-permute-done | bytes 163872 | tf_op jit(solution)/shard_map/ppermute | solution.py:770
  15.9 0.0 collective-permute-done.3.refs_1_
  16.0 0.1 collective-permute-start.4
  16.0 1.3 %collective-permute-done.4.refs_2_ = f32[264,128]{1,0:T(8,128)S(1)} collective-permute-done((f32[264,128]{1,0:T(8,128)S(1)}, f32[264,128]{1,0:T(8,128)S(1)}, u32[]{:S(2)}, u32[]{:S(2)}) %collective-permute-start.4) | collective-permute-done | bytes 135200 | tf_op jit(solution)/shard_map/ppermute | solution.py:849
  17.4 0.0 copy-done
  17.4 0.0 copy-done.1
  17.4 0.0 copy-done.2
  17.4 1.5 %shard_map.97 = (f32[2,9,64,128]{3,2,1,0:T(8,128)S(1)}, f32[9,4,64,128]{3,2,1,0:T(8,128)S(1)}, f32[3,4,64,128]{3,2,1,0:T(8,128)S(1)}, f32[7,64,128]{2,1,0:T(8,12...) custom-call(f32[320,128]{1,0:T(8,128)S(1)} %collective-permute-done.2.refs_0_, ...), custom_call_target="tpu_custom_call" | custom-call | tf_op jit(solution)/shard_map/pallas_call | solution.py:784
  18.9 0.0 collective-permute-done.refs_0_
  19.0 0.0 collective-permute-done.1.refs_1_
  19.0 0.7 %shard_map.98 = (f32[9,4,64,128]{3,2,1,0:T(8,128)S(1)}, f32[3,4,40,128]{3,2,1,0:T(8,128)S(1)}, f32[3,4,40,128]{3,2,1,0:T(8,128)S(1)}) custom-call(f32[6,64,128]{2,1,0:T(8,128)S(1)} %collective-permute-done.refs_0_, f32[6,64,128]{2,1,0:T(8,128)S(1)} %collective-permute-done.1.refs_1_, f32[9,4,64,128]{3,2,1,0:T(8,128)S(1)} %get-tuple-element.30.refs_5_.refs_2_, ...), custom_call_target="tpu_custom_call" | custom-call | tf_op jit(solution)/shard_map/pallas_call | solution.py:784
  19.7 0.2 collective-permute-start.5
  19.9 1.4 %collective-permute-done.5.received = f32[3,4,40,128]{3,2,1,0:T(8,128)S(1)} collective-permute-done((f32[3,4,40,128]{3,2,1,0:T(8,128)S(1)}, f32[3,4,40,128]{3,2,1,0:T(8,128)S(1)}, u32[]{:S(2)}, u32[]{:S(2)}) %collective-permute-start.5) | collective-permute-done | bytes 245792 | tf_op jit(solution)/shard_map/ppermute | solution.py:874
  21.3 0.2 shard_map.99
  21.5 3.5 %collective-permute-start.7 = (f32[200,128]{1,0:T(8,128)S(1)}, f32[200,128]{1,0:T(8,128)S(1)}, u32[]{:S(2)}, u32[]{:S(2)}) collective-permute-start(f32[200,128]{1,0:T(8,128)S(1)} %get-tuple-element.47), channel_id=1, source_target_pairs={{0,1},{1,0},{2,3},{3,2},{4,5},{5,4},{6,7},{7,6},{8,9},{9,8},{10,11... | collective-permute-start | bytes 307208 | tf_op jit(solution)/shard_map/ppermute | solution.py:770
  25.0 0.1 collective-permute-start.6
  25.1 1.0 %copy.12 = f32[1,9,4,64,128]{4,3,2,1,0:T(8,128)} copy(f32[1,9,4,64,128]{4,3,2,1,0:T(8,128)S(1)} %bitcast.5) | data formatting | bytes 2359296
  26.1 0.3 shard_map.100
  26.4 3.2 %collective-permute-done.7.refs_0_ = f32[200,128]{1,0:T(8,128)S(1)} collective-permute-done((f32[200,128]{1,0:T(8,128)S(1)}, f32[200,128]{1,0:T(8,128)S(1)}, u32[]{:S(2)}, u32[]{:S(2)}) %collective-permute-start.7) | collective-permute-done | bytes 102432 | tf_op jit(solution)/shard_map/ppermute | solution.py:770
  29.6 0.8 %shard_map.101.refs_1_ = f32[3,4,32,128]{3,2,1,0:T(8,128)} custom-call(f32[200,128]{1,0:T(8,128)S(1)} %collective-permute-done.7.refs_0_, f32[3,4,40,128]{3,2,1,0:T(8,128)S(1)} %get-tuple-element.48.grad.refs_1_.refs_2_, f32[3,4,40,128]{3,2,1,0:T(8,128)S(1)} %get-tuple-element.50.refs_2_.refs_3_, f32[3,2,40,128]{3,2,1,0:T(8,128)S(1)} %get-tuple-element.51.refs_3_.refs_4_, ...), custom_call_target="tpu_custom_call" | custom-call | tf_op jit(solution)/shard_map/pallas_call | solution.py:784
  30.4 1.0 %collective-permute-done.6.refs_0_ = f32[200,128]{1,0:T(8,128)S(1)} collective-permute-done((f32[200,128]{1,0:T(8,128)S(1)}, f32[200,128]{1,0:T(8,128)S(1)}, u32[]{:S(2)}, u32[]{:S(2)}) %collective-permute-start.6) | collective-permute-done | bytes 102432 | tf_op jit(solution)/shard_map/ppermute | solution.py:770
  31.4 0.8 %shard_map.102 = f32[3,4,32,128]{3,2,1,0:T(8,128)} custom-call(f32[200,128]{1,0:T(8,128)S(1)} %collective-permute-done.6.refs_0_, f32[3,4,32,128]{3,2,1,0:T(8,128)} %shard_map.101.refs_1_, f32[3,4,40,128]{3,2,1,0:T(8,128)S(1)} %get-tuple-element.48.grad.refs_1_.refs_2_, ...), custom_call_target="tpu_custom_call", output_to_operand_aliasing={{}: (1, {})} | custom-call | tf_op jit(solution)/shard_map/pallas_call | solution.py:784
  (3 shorter events, 0.0 us)
Async XLA Ops:
  2.0 15.4 %copy-start = (f32[1,9,4,64,128]{4,3,2,1,0:T(8,128)S(1)}, f32[1,9,4,64,128]{4,3,2,1,0:T(8,128)}, u32[]{:S(2)}) copy-start(f32[1,9,4,64,128]{4,3,2,1,0:T(8,128)} %param.8) | copy-start | bytes 3538948
  2.0 15.4 %copy-start.1 = (bf16[1,9,4,64,128]{4,3,2,1,0:T(8,128)(2,1)S(1)}, bf16[1,9,4,64,128]{4,3,2,1,0:T(8,128)(2,1)}, u32[]{:S(2)}) copy-start(bf16[1,9,4,64,128]{4,3,2,1,0:T(8,128)(2,1)} %param.10) | copy-start | bytes 1769476
  2.0 15.4 %copy-start.2 = (s32[1,4,4]{2,1,0:T(4,128)S(1)}, s32[1,4,4]{2,1,0:T(4,128)}, u32[]{:S(2)}) copy-start(s32[1,4,4]{2,1,0:T(4,128)} %refs_3_.1) | copy-start | bytes 196
  2.0 13.9 %collective-permute-start.2 = (f32[320,128]{1,0:T(8,128)S(1)}, f32[320,128]{1,0:T(8,128)S(1)}, u32[]{:S(2)}, u32[]{:S(2)}) collective-permute-start(f32[320,128]{1,0:T(8,128)S(1)} %get-tuple-element.31), channel_id=1, source_target_pairs={{0,1},{1,0},{2,3},{3,2},{4,5},{5,4},{6,7},{7,6},{8,9},{9,8},{10,11... | collective-permute-start | bytes 491528 | tf_op jit(solution)/shard_map/ppermute | solution.py:770
  3.6 12.3 %collective-permute-start.3 = (f32[320,128]{1,0:T(8,128)S(1)}, f32[320,128]{1,0:T(8,128)S(1)}, u32[]{:S(2)}, u32[]{:S(2)}) collective-permute-start(f32[320,128]{1,0:T(8,128)S(1)} %get-tuple-element.32), channel_id=1, source_target_pairs={{0,16},{1,2},{2,1},{3,4},{4,3},{5,6},{6,5},{7,8},{8,7},{9,10},{10,... | collective-permute-start | bytes 491528 | tf_op jit(solution)/shard_map/ppermute | solution.py:770
  7.2 11.8 %collective-permute-start = (f32[6,64,128]{2,1,0:T(8,128)S(1)}, f32[6,64,128]{2,1,0:T(8,128)S(1)}, u32[]{:S(2)}, u32[]{:S(2)}) collective-permute-start(f32[6,64,128]{2,1,0:T(8,128)S(1)} %get-tuple-element.28), channel_id=1, source_target_pairs={{0,1},{1,0},{2,3},{3,2},{4,5},{5,4},{6,7},{7,6},{8,9},{9,8},{10,11... | collective-permute-start | bytes 589832 | tf_op jit(solution)/shard_map/ppermute | solution.py:770
  8.9 10.1 %collective-permute-start.1 = (f32[6,64,128]{2,1,0:T(8,128)S(1)}, f32[6,64,128]{2,1,0:T(8,128)S(1)}, u32[]{:S(2)}, u32[]{:S(2)}) collective-permute-start(f32[6,64,128]{2,1,0:T(8,128)S(1)} %get-tuple-element.29), channel_id=1, source_target_pairs={{0,16},{1,2},{2,1},{3,4},{4,3},{5,6},{6,5},{7,8},{8,7},{9,10},{10,... | collective-permute-start | bytes 589832 | tf_op jit(solution)/shard_map/ppermute | solution.py:770
  16.0 1.4 %collective-permute-start.4 = (f32[264,128]{1,0:T(8,128)S(1)}, f32[264,128]{1,0:T(8,128)S(1)}, u32[]{:S(2)}, u32[]{:S(2)}) collective-permute-start(f32[264,128]{1,0:T(8,128)S(1)} %pad_maximum_fusion), channel_id=1, source_target_pairs={{0,16},{16,0},{1,17},{17,1},{2,18},{18,2},{3,19},{19,3},{4,20},{20... | collective-permute-start | bytes 405512 | tf_op jit(solution)/shard_map/ppermute | solution.py:849
  19.7 1.6 %collective-permute-start.5 = (f32[3,4,40,128]{3,2,1,0:T(8,128)S(1)}, f32[3,4,40,128]{3,2,1,0:T(8,128)S(1)}, u32[]{:S(2)}, u32[]{:S(2)}) collective-permute-start(f32[3,4,40,128]{3,2,1,0:T(8,128)S(1)} %get-tuple-element.44), channel_id=1, source_target_pairs={{0,16},{16,0},{1,17},{17,1},{2,18},{18,2},{3,19},{19,3},{4,20},{20... | collective-permute-start | bytes 737288 | tf_op jit(solution)/shard_map/ppermute | solution.py:874
  21.5 8.1 %collective-permute-start.7 = (f32[200,128]{1,0:T(8,128)S(1)}, f32[200,128]{1,0:T(8,128)S(1)}, u32[]{:S(2)}, u32[]{:S(2)}) collective-permute-start(f32[200,128]{1,0:T(8,128)S(1)} %get-tuple-element.47), channel_id=1, source_target_pairs={{0,1},{1,0},{2,3},{3,2},{4,5},{5,4},{6,7},{7,6},{8,9},{9,8},{10,11... | collective-permute-start | bytes 307208 | tf_op jit(solution)/shard_map/ppermute | solution.py:770
  25.0 6.5 %collective-permute-start.6 = (f32[200,128]{1,0:T(8,128)S(1)}, f32[200,128]{1,0:T(8,128)S(1)}, u32[]{:S(2)}, u32[]{:S(2)}) collective-permute-start(f32[200,128]{1,0:T(8,128)S(1)} %get-tuple-element.46), channel_id=1, source_target_pairs={{0,16},{1,2},{2,1},{3,4},{4,3},{5,6},{6,5},{7,8},{8,7},{9,10},{10,... | collective-permute-start | bytes 307208 | tf_op jit(solution)/shard_map/ppermute | solution.py:770

commit v8 on v7

--- a/solution.py
+++ b/solution.py
@@ -503,7 +503,7 @@
 
 
 def far_kernel(groups, *refs):
-    by_pair, by_next, st, end, w, third, outer, parts, known, coef, push, forward, final, *refs = refs
+    by_next, by_pair, st, end, w, third, outer, parts, known, coef, push, forward, final, *refs = refs
     *images, low, high, edge, low_s, high_v, image = refs
     width, size_y = st.shape[1], st.shape[2]
     last = width - 1
@@ -864,7 +864,7 @@
     final, *images = call(
         functools.partial(far_kernel, groups),
         [pltpu.VMEM(grid.shape, grid.dtype), *images],
-        [late_pair, late_next, st, end, w, third, outer, parts, known, coef, push, forward],
+        [late_next, late_pair, st, end, w, third, outer, parts, known, coef, push, forward],
         [(6, *plane), (6, *plane), (2, 9, *plane), (3, *plane), (3, *plane), (3, width, *plane)],
     )
     if groups != 2:

time: 32.8 us -> 31.6 us (0.963); the launches traced: 32.2 us -> 31.3 us
  starting transfers between devices: 9.41 us -> 8.08 us
  waiting for transfers between devices: 13.1 us -> 13.6 us
    ppermute x6, starting transfers between devices: 9.15 us -> 7.94 us  [both_ways(): out.append(lax.ppermute(array, ('shot', 'tile'), pairs))]
    ppermute x6, waiting for transfers between devices: 10.4 us -> 10.8 us  [both_ways(): out.append(lax.ppermute(array, ('shot', 'tile'), pairs))]
  transfers between devices with their start and end apart: 8 -> 8, of which waited for: 5 -> 6; matrix products, arithmetic and copies ran while one was open for 3% -> 3% of each run, Pallas kernels for 15% -> 15%
where the time goes in v8:
time: 31.6 us; the launch traced here: 31.3 us
  waiting for transfers between devices  13.6 us (43%)
  starting transfers between devices  8.08 us (26%)
  Pallas kernels  7.86 us (25%)
  local copies, waits for them, and re-layouts  1.04 us (3%)
  between operations  0.75 us (2%)
    ppermute x6, waiting for transfers between devices, both_ways(): out.append(lax.ppermute(array, ('shot', 'tile'), pairs))  10.8 us
    ppermute x6, starting transfers between devices, both_ways(): out.append(lax.ppermute(array, ('shot', 'tile'), pairs))  7.94 us
    pallas_call x8, Pallas kernels, call(): pl.pallas_call(kernel, out_shape=outs, in_specs=specs, out_specs=jax.tree...  7.86 us
    ppermute x1, waiting for transfers between devices, local(): received = lax.ppermute(give, 'shot', [(0, 1), (1, 0)])  1.5 us
    ppermute x1, waiting for transfers between devices, local(): swapped = lax.ppermute(swapped, 'shot', [(0, 1), (1, 0)])  1.34 us
    unnamed x7, local copies, waits for them, and re-layouts  1.03 us
  transfers between devices with their start and end apart: 8, of which 6 were waited for; matrix products, arithmetic and copies ran while one was open for 3% of the time, Pallas kernels for 15%

profile of v8, /device:TPU:8, one launch (start us, length us, event | category | flops | bytes accessed | tf_op | source)
XLA Modules:
  0.0 31.3 jit_solution(16076627702317655864)
XLA Ops:
  0.6 1.4 %shard_map.95 = (f32[320,128]{1,0:T(8,128)S(1)}, f32[320,128]{1,0:T(8,128)S(1)}, f32[64,128]{1,0:T(8,128)S(1)}, f32[8,128]{1,0:T(8,128)S(1)}) custom-call(s32[1,4,8]{2,1,0:T(4,128)} %bitcast.13, s32[1,4,4]{2,1,0:T(4,128)} %refs_3_.1, f32[9,4,64,128]{3,2,1,0:T(8,128)} %bitcast.6, bf16[3,4,64,128]{3,2,1,0:T(8,128)(2,1)} %bitcast.11, f32[4,64,128]{2,1,0:T(8,128)} %lame.1, ...), custom_call_target="tpu_custom_call" | custom-call | tf_op jit(solution)/shard_map/pallas_call | solution.py:784
  2.0 0.0 copy-start
  2.0 0.0 copy-start.1
  2.0 0.0 copy-start.2
  2.0 1.6 %collective-permute-start.2 = (f32[320,128]{1,0:T(8,128)S(1)}, f32[320,128]{1,0:T(8,128)S(1)}, u32[]{:S(2)}, u32[]{:S(2)}) collective-permute-start(f32[320,128]{1,0:T(8,128)S(1)} %get-tuple-element.31), channel_id=1, source_target_pairs={{0,1},{1,0},{2,3},{3,2},{4,5},{5,4},{6,7},{7,6},{8,9},{9,8},{10,11... | collective-permute-start | bytes 491528 | tf_op jit(solution)/shard_map/ppermute | solution.py:770
  3.6 1.4 %collective-permute-start.3 = (f32[320,128]{1,0:T(8,128)S(1)}, f32[320,128]{1,0:T(8,128)S(1)}, u32[]{:S(2)}, u32[]{:S(2)}) collective-permute-start(f32[320,128]{1,0:T(8,128)S(1)} %get-tuple-element.32), channel_id=1, source_target_pairs={{0,16},{1,2},{2,1},{3,4},{4,3},{5,6},{6,5},{7,8},{8,7},{9,10},{10,... | collective-permute-start | bytes 491528 | tf_op jit(solution)/shard_map/ppermute | solution.py:770
  5.0 2.2 %shard_map.96 = (f32[6,64,128]{2,1,0:T(8,128)S(1)}, f32[6,64,128]{2,1,0:T(8,128)S(1)}, f32[9,4,64,128]{3,2,1,0:T(8,128)S(1)}, f32[3,4,64,128]{3,2,1,0:T(8,128)S(1)}, f32[3,4,64,128]{3,2,1,0:T(8,128)S(1)}) custom-call(f32[9,4,64,128]{3,2,1,0:T(8,128)} %bitcast.7, bf16[3,4,64,128]{3,2,1,0:T(8,128)(2,1)} %bitcast.12, f32[4,64,128]{2,1,0:T(8,128)} %buoyancy.1, ...), custom_call_target="tpu_custom_call" | custom-call | tf_op jit(solution)/shard_map/pallas_call | solution.py:784
  7.2 2.5 %collective-permute-start = (f32[6,64,128]{2,1,0:T(8,128)S(1)}, f32[6,64,128]{2,1,0:T(8,128)S(1)}, u32[]{:S(2)}, u32[]{:S(2)}) collective-permute-start(f32[6,64,128]{2,1,0:T(8,128)S(1)} %get-tuple-element.28), channel_id=1, source_target_pairs={{0,16},{1,2},{2,1},{3,4},{4,3},{5,6},{6,5},{7,8},{8,7},{9,10},{10,... | collective-permute-start | bytes 589832 | tf_op jit(solution)/shard_map/ppermute | solution.py:770
  9.7 0.0 collective-permute-start.1
  9.7 6.2 %collective-permute-done.2.refs_0_ = f32[320,128]{1,0:T(8,128)S(1)} collective-permute-done((f32[320,128]{1,0:T(8,128)S(1)}, f32[320,128]{1,0:T(8,128)S(1)}, u32[]{:S(2)}, u32[]{:S(2)}) %collective-permute-start.2) | collective-permute-done | bytes 163872 | tf_op jit(solution)/shard_map/ppermute | solution.py:770
  15.9 0.0 collective-permute-done.3.refs_1_
  16.0 0.1 collective-permute-start.4
  16.0 1.3 %collective-permute-done.4.refs_2_ = f32[264,128]{1,0:T(8,128)S(1)} collective-permute-done((f32[264,128]{1,0:T(8,128)S(1)}, f32[264,128]{1,0:T(8,128)S(1)}, u32[]{:S(2)}, u32[]{:S(2)}) %collective-permute-start.4) | collective-permute-done | bytes 135200 | tf_op jit(solution)/shard_map/ppermute | solution.py:849
  17.4 0.0 copy-done
  17.4 0.0 copy-done.1
  17.4 0.0 copy-done.2
  17.4 1.5 %shard_map.97 = (f32[2,9,64,128]{3,2,1,0:T(8,128)S(1)}, f32[9,4,64,128]{3,2,1,0:T(8,128)S(1)}, f32[3,4,64,128]{3,2,1,0:T(8,128)S(1)}, f32[7,64,128]{2,1,0:T(8,12...) custom-call(f32[320,128]{1,0:T(8,128)S(1)} %collective-permute-done.2.refs_0_, ...), custom_call_target="tpu_custom_call" | custom-call | tf_op jit(solution)/shard_map/pallas_call | solution.py:784
  18.9 0.0 collective-permute-done.refs_0_
  19.0 1.0 %collective-permute-done.1.refs_1_ = f32[6,64,128]{2,1,0:T(8,128)S(1)} collective-permute-done((f32[6,64,128]{2,1,0:T(8,128)S(1)}, f32[6,64,128]{2,1,0:T(8,128)S(1)}, u32[]{:S(2)}, u32[]{:S(2)}) %collective-permute-start.1) | collective-permute-done | bytes 196640 | tf_op jit(solution)/shard_map/ppermute | solution.py:770
  20.0 0.7 %shard_map.98 = (f32[9,4,64,128]{3,2,1,0:T(8,128)S(1)}, f32[3,4,40,128]{3,2,1,0:T(8,128)S(1)}, f32[3,4,40,128]{3,2,1,0:T(8,128)S(1)}) custom-call(f32[6,64,128]{2,1,0:T(8,128)S(1)} %collective-permute-done.refs_0_, f32[6,64,128]{2,1,0:T(8,128)S(1)} %collective-permute-done.1.refs_1_, f32[9,4,64,128]{3,2,1,0:T(8,128)S(1)} %get-tuple-element.30.refs_5_.refs_2_, ...), custom_call_target="tpu_custom_call" | custom-call | tf_op jit(solution)/shard_map/pallas_call | solution.py:784
  20.7 0.1 collective-permute-start.5
  20.7 1.5 %collective-permute-done.5.received = f32[3,4,40,128]{3,2,1,0:T(8,128)S(1)} collective-permute-done((f32[3,4,40,128]{3,2,1,0:T(8,128)S(1)}, f32[3,4,40,128]{3,2,1,0:T(8,128)S(1)}, u32[]{:S(2)}, u32[]{:S(2)}) %collective-permute-start.5) | collective-permute-done | bytes 245792 | tf_op jit(solution)/shard_map/ppermute | solution.py:874
  22.2 0.2 shard_map.99
  22.4 1.6 %collective-permute-start.7 = (f32[200,128]{1,0:T(8,128)S(1)}, f32[200,128]{1,0:T(8,128)S(1)}, u32[]{:S(2)}, u32[]{:S(2)}) collective-permute-start(f32[200,128]{1,0:T(8,128)S(1)} %get-tuple-element.47), channel_id=1, source_target_pairs={{0,1},{1,0},{2,3},{3,2},{4,5},{5,4},{6,7},{7,6},{8,9},{9,8},{10,11... | collective-permute-start | bytes 307208 | tf_op jit(solution)/shard_map/ppermute | solution.py:770
  24.0 0.9 %collective-permute-start.6 = (f32[200,128]{1,0:T(8,128)S(1)}, f32[200,128]{1,0:T(8,128)S(1)}, u32[]{:S(2)}, u32[]{:S(2)}) collective-permute-start(f32[200,128]{1,0:T(8,128)S(1)} %get-tuple-element.46), channel_id=1, source_target_pairs={{0,16},{1,2},{2,1},{3,4},{4,3},{5,6},{6,5},{7,8},{8,7},{9,10},{10,... | collective-permute-start | bytes 307208 | tf_op jit(solution)/shard_map/ppermute | solution.py:770
  24.9 1.0 %copy.12 = f32[1,9,4,64,128]{4,3,2,1,0:T(8,128)} copy(f32[1,9,4,64,128]{4,3,2,1,0:T(8,128)S(1)} %bitcast.5) | data formatting | bytes 2359296
  25.9 0.3 shard_map.100
  26.2 1.2 %collective-permute-done.7.refs_0_ = f32[200,128]{1,0:T(8,128)S(1)} collective-permute-done((f32[200,128]{1,0:T(8,128)S(1)}, f32[200,128]{1,0:T(8,128)S(1)}, u32[]{:S(2)}, u32[]{:S(2)}) %collective-permute-start.7) | collective-permute-done | bytes 102432 | tf_op jit(solution)/shard_map/ppermute | solution.py:770
  27.4 0.8 %shard_map.101.refs_1_ = f32[3,4,32,128]{3,2,1,0:T(8,128)} custom-call(f32[200,128]{1,0:T(8,128)S(1)} %collective-permute-done.7.refs_0_, f32[3,4,40,128]{3,2,1,0:T(8,128)S(1)} %get-tuple-element.48.grad.refs_1_.refs_2_, f32[3,4,40,128]{3,2,1,0:T(8,128)S(1)} %get-tuple-element.50.refs_2_.refs_3_, f32[3,2,40,128]{3,2,1,0:T(8,128)S(1)} %get-tuple-element.51.refs_3_.refs_4_, ...), custom_call_target="tpu_custom_call" | custom-call | tf_op jit(solution)/shard_map/pallas_call | solution.py:784
  28.2 2.3 %collective-permute-done.6.refs_0_ = f32[200,128]{1,0:T(8,128)S(1)} collective-permute-done((f32[200,128]{1,0:T(8,128)S(1)}, f32[200,128]{1,0:T(8,128)S(1)}, u32[]{:S(2)}, u32[]{:S(2)}) %collective-permute-start.6) | collective-permute-done | bytes 102432 | tf_op jit(solution)/shard_map/ppermute | solution.py:770
  30.6 0.8 %shard_map.102 = f32[3,4,32,128]{3,2,1,0:T(8,128)} custom-call(f32[200,128]{1,0:T(8,128)S(1)} %collective-permute-done.6.refs_0_, f32[3,4,32,128]{3,2,1,0:T(8,128)} %shard_map.101.refs_1_, f32[3,4,40,128]{3,2,1,0:T(8,128)S(1)} %get-tuple-element.48.grad.refs_1_.refs_2_, ...), custom_call_target="tpu_custom_call", output_to_operand_aliasing={{}: (1, {})} | custom-call | tf_op jit(solution)/shard_map/pallas_call | solution.py:784
  (3 shorter events, 0.0 us)
Async XLA Ops:
  2.0 15.4 %copy-start = (f32[1,9,4,64,128]{4,3,2,1,0:T(8,128)S(1)}, f32[1,9,4,64,128]{4,3,2,1,0:T(8,128)}, u32[]{:S(2)}) copy-start(f32[1,9,4,64,128]{4,3,2,1,0:T(8,128)} %param.8) | copy-start | bytes 3538948
  2.0 15.4 %copy-start.1 = (bf16[1,9,4,64,128]{4,3,2,1,0:T(8,128)(2,1)S(1)}, bf16[1,9,4,64,128]{4,3,2,1,0:T(8,128)(2,1)}, u32[]{:S(2)}) copy-start(bf16[1,9,4,64,128]{4,3,2,1,0:T(8,128)(2,1)} %param.10) | copy-start | bytes 1769476
  2.0 15.4 %copy-start.2 = (s32[1,4,4]{2,1,0:T(4,128)S(1)}, s32[1,4,4]{2,1,0:T(4,128)}, u32[]{:S(2)}) copy-start(s32[1,4,4]{2,1,0:T(4,128)} %refs_3_.1) | copy-start | bytes 196
  2.0 13.9 %collective-permute-start.2 = (f32[320,128]{1,0:T(8,128)S(1)}, f32[320,128]{1,0:T(8,128)S(1)}, u32[]{:S(2)}, u32[]{:S(2)}) collective-permute-start(f32[320,128]{1,0:T(8,128)S(1)} %get-tuple-element.31), channel_id=1, source_target_pairs={{0,1},{1,0},{2,3},{3,2},{4,5},{5,4},{6,7},{7,6},{8,9},{9,8},{10,11... | collective-permute-start | bytes 491528 | tf_op jit(solution)/shard_map/ppermute | solution.py:770
  3.6 12.3 %collective-permute-start.3 = (f32[320,128]{1,0:T(8,128)S(1)}, f32[320,128]{1,0:T(8,128)S(1)}, u32[]{:S(2)}, u32[]{:S(2)}) collective-permute-start(f32[320,128]{1,0:T(8,128)S(1)} %get-tuple-element.32), channel_id=1, source_target_pairs={{0,16},{1,2},{2,1},{3,4},{4,3},{5,6},{6,5},{7,8},{8,7},{9,10},{10,... | collective-permute-start | bytes 491528 | tf_op jit(solution)/shard_map/ppermute | solution.py:770
  7.2 11.7 %collective-permute-start = (f32[6,64,128]{2,1,0:T(8,128)S(1)}, f32[6,64,128]{2,1,0:T(8,128)S(1)}, u32[]{:S(2)}, u32[]{:S(2)}) collective-permute-start(f32[6,64,128]{2,1,0:T(8,128)S(1)} %get-tuple-element.28), channel_id=1, source_target_pairs={{0,16},{1,2},{2,1},{3,4},{4,3},{5,6},{6,5},{7,8},{8,7},{9,10},{10,... | collective-permute-start | bytes 589832 | tf_op jit(solution)/shard_map/ppermute | solution.py:770
  9.7 10.2 %collective-permute-start.1 = (f32[6,64,128]{2,1,0:T(8,128)S(1)}, f32[6,64,128]{2,1,0:T(8,128)S(1)}, u32[]{:S(2)}, u32[]{:S(2)}) collective-permute-start(f32[6,64,128]{2,1,0:T(8,128)S(1)} %get-tuple-element.29), channel_id=1, source_target_pairs={{0,1},{1,0},{2,3},{3,2},{4,5},{5,4},{6,7},{7,6},{8,9},{9,8},{10,11... | collective-permute-start | bytes 589832 | tf_op jit(solution)/shard_map/ppermute | solution.py:770
  16.0 1.4 %collective-permute-start.4 = (f32[264,128]{1,0:T(8,128)S(1)}, f32[264,128]{1,0:T(8,128)S(1)}, u32[]{:S(2)}, u32[]{:S(2)}) collective-permute-start(f32[264,128]{1,0:T(8,128)S(1)} %pad_maximum_fusion), channel_id=1, source_target_pairs={{0,16},{16,0},{1,17},{17,1},{2,18},{18,2},{3,19},{19,3},{4,20},{20... | collective-permute-start | bytes 405512 | tf_op jit(solution)/shard_map/ppermute | solution.py:849
  20.7 1.6 %collective-permute-start.5 = (f32[3,4,40,128]{3,2,1,0:T(8,128)S(1)}, f32[3,4,40,128]{3,2,1,0:T(8,128)S(1)}, u32[]{:S(2)}, u32[]{:S(2)}) collective-permute-start(f32[3,4,40,128]{3,2,1,0:T(8,128)S(1)} %get-tuple-element.44), channel_id=1, source_target_pairs={{0,16},{16,0},{1,17},{17,1},{2,18},{18,2},{3,19},{19,3},{4,20},{20... | collective-permute-start | bytes 737288 | tf_op jit(solution)/shard_map/ppermute | solution.py:874
  22.4 5.0 %collective-permute-start.7 = (f32[200,128]{1,0:T(8,128)S(1)}, f32[200,128]{1,0:T(8,128)S(1)}, u32[]{:S(2)}, u32[]{:S(2)}) collective-permute-start(f32[200,128]{1,0:T(8,128)S(1)} %get-tuple-element.47), channel_id=1, source_target_pairs={{0,1},{1,0},{2,3},{3,2},{4,5},{5,4},{6,7},{7,6},{8,9},{9,8},{10,11... | collective-permute-start | bytes 307208 | tf_op jit(solution)/shard_map/ppermute | solution.py:770
  24.0 6.5 %collective-permute-start.6 = (f32[200,128]{1,0:T(8,128)S(1)}, f32[200,128]{1,0:T(8,128)S(1)}, u32[]{:S(2)}, u32[]{:S(2)}) collective-permute-start(f32[200,128]{1,0:T(8,128)S(1)} %get-tuple-element.46), channel_id=1, source_target_pairs={{0,16},{1,2},{2,1},{3,4},{4,3},{5,6},{6,5},{7,8},{8,7},{9,10},{10,... | collective-permute-start | bytes 307208 | tf_op jit(solution)/shard_map/ppermute | solution.py:770

commit v9 on v8

--- a/solution.py
+++ b/solution.py
@@ -224,7 +224,7 @@
         (state_hbm.at[c, last], up.at[n * size_y : (n + 1) * size_y]) for n, c in enumerate(SIDE)
     ]
     copies = [pltpu.make_async_copy(*pair, sems.at[n]) for n, pair in enumerate(ends)]
-    for copy in copies:
+    for copy in (copies[9], *copies[2:9], *copies[:2], *copies[10:]):
         copy.start()
     for copy in copies[:2]:
         copy.wait()

time: 31.6 us -> 31.4 us (level)
  no operation moved by 1% of the time
where the time goes in v9:
time: 31.4 us; the launch traced here: 31.2 us
  waiting for transfers between devices  13.6 us (43%)
  starting transfers between devices  8.08 us (26%)
  Pallas kernels  7.73 us (25%)
  local copies, waits for them, and re-layouts  1.04 us (3%)
  between operations  0.75 us (2%)
    ppermute x6, waiting for transfers between devices, both_ways(): out.append(lax.ppermute(array, ('shot', 'tile'), pairs))  10.8 us
    ppermute x6, starting transfers between devices, both_ways(): out.append(lax.ppermute(array, ('shot', 'tile'), pairs))  7.94 us
    pallas_call x8, Pallas kernels, call(): pl.pallas_call(kernel, out_shape=outs, in_specs=specs, out_specs=jax.tree...  7.73 us
    ppermute x1, waiting for transfers between devices, local(): received = lax.ppermute(give, 'shot', [(0, 1), (1, 0)])  1.5 us
    ppermute x1, waiting for transfers between devices, local(): swapped = lax.ppermute(swapped, 'shot', [(0, 1), (1, 0)])  1.34 us
    unnamed x7, local copies, waits for them, and re-layouts  1.03 us
  transfers between devices with their start and end apart: 8, of which 6 were waited for; matrix products, arithmetic and copies ran while one was open for 3% of the time, Pallas kernels for 15%

profile of v9, /device:TPU:8, one launch (start us, length us, event | category | flops | bytes accessed | tf_op | source)
XLA Modules:
  0.0 31.2 jit_solution(6260798548470663127)
XLA Ops:
  0.6 1.2 %shard_map.95 = (f32[320,128]{1,0:T(8,128)S(1)}, f32[320,128]{1,0:T(8,128)S(1)}, f32[64,128]{1,0:T(8,128)S(1)}, f32[8,128]{1,0:T(8,128)S(1)}) custom-call(s32[1,4,8]{2,1,0:T(4,128)} %bitcast.13, s32[1,4,4]{2,1,0:T(4,128)} %refs_3_.1, f32[9,4,64,128]{3,2,1,0:T(8,128)} %bitcast.6, bf16[3,4,64,128]{3,2,1,0:T(8,128)(2,1)} %bitcast.11, f32[4,64,128]{2,1,0:T(8,128)} %lame.1, ...), custom_call_target="tpu_custom_call" | custom-call | tf_op jit(solution)/shard_map/pallas_call | solution.py:784
  1.9 0.0 copy-start
  1.9 0.0 copy-start.1
  1.9 0.0 copy-start.2
  1.9 1.6 %collective-permute-start.2 = (f32[320,128]{1,0:T(8,128)S(1)}, f32[320,128]{1,0:T(8,128)S(1)}, u32[]{:S(2)}, u32[]{:S(2)}) collective-permute-start(f32[320,128]{1,0:T(8,128)S(1)} %get-tuple-element.31), channel_id=1, source_target_pairs={{0,1},{1,0},{2,3},{3,2},{4,5},{5,4},{6,7},{7,6},{8,9},{9,8},{10,11... | collective-permute-start | bytes 491528 | tf_op jit(solution)/shard_map/ppermute | solution.py:770
  3.5 1.4 %collective-permute-start.3 = (f32[320,128]{1,0:T(8,128)S(1)}, f32[320,128]{1,0:T(8,128)S(1)}, u32[]{:S(2)}, u32[]{:S(2)}) collective-permute-start(f32[320,128]{1,0:T(8,128)S(1)} %get-tuple-element.32), channel_id=1, source_target_pairs={{0,16},{1,2},{2,1},{3,4},{4,3},{5,6},{6,5},{7,8},{8,7},{9,10},{10,... | collective-permute-start | bytes 491528 | tf_op jit(solution)/shard_map/ppermute | solution.py:770
  4.8 2.2 %shard_map.96 = (f32[6,64,128]{2,1,0:T(8,128)S(1)}, f32[6,64,128]{2,1,0:T(8,128)S(1)}, f32[9,4,64,128]{3,2,1,0:T(8,128)S(1)}, f32[3,4,64,128]{3,2,1,0:T(8,128)S(1)}, f32[3,4,64,128]{3,2,1,0:T(8,128)S(1)}) custom-call(f32[9,4,64,128]{3,2,1,0:T(8,128)} %bitcast.7, bf16[3,4,64,128]{3,2,1,0:T(8,128)(2,1)} %bitcast.12, f32[4,64,128]{2,1,0:T(8,128)} %buoyancy.1, ...), custom_call_target="tpu_custom_call" | custom-call | tf_op jit(solution)/shard_map/pallas_call | solution.py:784
  7.1 2.5 %collective-permute-start = (f32[6,64,128]{2,1,0:T(8,128)S(1)}, f32[6,64,128]{2,1,0:T(8,128)S(1)}, u32[]{:S(2)}, u32[]{:S(2)}) collective-permute-start(f32[6,64,128]{2,1,0:T(8,128)S(1)} %get-tuple-element.28), channel_id=1, source_target_pairs={{0,16},{1,2},{2,1},{3,4},{4,3},{5,6},{6,5},{7,8},{8,7},{9,10},{10,... | collective-permute-start | bytes 589832 | tf_op jit(solution)/shard_map/ppermute | solution.py:770
  9.6 0.0 collective-permute-start.1
  9.6 6.2 %collective-permute-done.2.refs_0_ = f32[320,128]{1,0:T(8,128)S(1)} collective-permute-done((f32[320,128]{1,0:T(8,128)S(1)}, f32[320,128]{1,0:T(8,128)S(1)}, u32[]{:S(2)}, u32[]{:S(2)}) %collective-permute-start.2) | collective-permute-done | bytes 163872 | tf_op jit(solution)/shard_map/ppermute | solution.py:770
  15.8 0.0 collective-permute-done.3.refs_1_
  15.8 0.1 collective-permute-start.4
  15.9 1.3 %collective-permute-done.4.refs_2_ = f32[264,128]{1,0:T(8,128)S(1)} collective-permute-done((f32[264,128]{1,0:T(8,128)S(1)}, f32[264,128]{1,0:T(8,128)S(1)}, u32[]{:S(2)}, u32[]{:S(2)}) %collective-permute-start.4) | collective-permute-done | bytes 135200 | tf_op jit(solution)/shard_map/ppermute | solution.py:849
  17.3 0.0 copy-done
  17.3 0.0 copy-done.1
  17.3 0.0 copy-done.2
  17.3 1.5 %shard_map.97 = (f32[2,9,64,128]{3,2,1,0:T(8,128)S(1)}, f32[9,4,64,128]{3,2,1,0:T(8,128)S(1)}, f32[3,4,64,128]{3,2,1,0:T(8,128)S(1)}, f32[7,64,128]{2,1,0:T(8,12...) custom-call(f32[320,128]{1,0:T(8,128)S(1)} %collective-permute-done.2.refs_0_, ...), custom_call_target="tpu_custom_call" | custom-call | tf_op jit(solution)/shard_map/pallas_call | solution.py:784
  18.8 0.0 collective-permute-done.refs_0_
  18.8 1.0 %collective-permute-done.1.refs_1_ = f32[6,64,128]{2,1,0:T(8,128)S(1)} collective-permute-done((f32[6,64,128]{2,1,0:T(8,128)S(1)}, f32[6,64,128]{2,1,0:T(8,128)S(1)}, u32[]{:S(2)}, u32[]{:S(2)}) %collective-permute-start.1) | collective-permute-done | bytes 196640 | tf_op jit(solution)/shard_map/ppermute | solution.py:770
  19.8 0.7 %shard_map.98 = (f32[9,4,64,128]{3,2,1,0:T(8,128)S(1)}, f32[3,4,40,128]{3,2,1,0:T(8,128)S(1)}, f32[3,4,40,128]{3,2,1,0:T(8,128)S(1)}) custom-call(f32[6,64,128]{2,1,0:T(8,128)S(1)} %collective-permute-done.refs_0_, f32[6,64,128]{2,1,0:T(8,128)S(1)} %collective-permute-done.1.refs_1_, f32[9,4,64,128]{3,2,1,0:T(8,128)S(1)} %get-tuple-element.30.refs_5_.refs_2_, ...), custom_call_target="tpu_custom_call" | custom-call | tf_op jit(solution)/shard_map/pallas_call | solution.py:784
  20.5 0.1 collective-permute-start.5
  20.6 1.5 %collective-permute-done.5.received = f32[3,4,40,128]{3,2,1,0:T(8,128)S(1)} collective-permute-done((f32[3,4,40,128]{3,2,1,0:T(8,128)S(1)}, f32[3,4,40,128]{3,2,1,0:T(8,128)S(1)}, u32[]{:S(2)}, u32[]{:S(2)}) %collective-permute-start.5) | collective-permute-done | bytes 245792 | tf_op jit(solution)/shard_map/ppermute | solution.py:874
  22.1 0.2 shard_map.99
  22.3 1.6 %collective-permute-start.7 = (f32[200,128]{1,0:T(8,128)S(1)}, f32[200,128]{1,0:T(8,128)S(1)}, u32[]{:S(2)}, u32[]{:S(2)}) collective-permute-start(f32[200,128]{1,0:T(8,128)S(1)} %get-tuple-element.47), channel_id=1, source_target_pairs={{0,1},{1,0},{2,3},{3,2},{4,5},{5,4},{6,7},{7,6},{8,9},{9,8},{10,11... | collective-permute-start | bytes 307208 | tf_op jit(solution)/shard_map/ppermute | solution.py:770
  23.9 0.9 %collective-permute-start.6 = (f32[200,128]{1,0:T(8,128)S(1)}, f32[200,128]{1,0:T(8,128)S(1)}, u32[]{:S(2)}, u32[]{:S(2)}) collective-permute-start(f32[200,128]{1,0:T(8,128)S(1)} %get-tuple-element.46), channel_id=1, source_target_pairs={{0,16},{1,2},{2,1},{3,4},{4,3},{5,6},{6,5},{7,8},{8,7},{9,10},{10,... | collective-permute-start | bytes 307208 | tf_op jit(solution)/shard_map/ppermute | solution.py:770
  24.8 1.0 %copy.12 = f32[1,9,4,64,128]{4,3,2,1,0:T(8,128)} copy(f32[1,9,4,64,128]{4,3,2,1,0:T(8,128)S(1)} %bitcast.5) | data formatting | bytes 2359296
  25.8 0.3 shard_map.100
  26.1 1.2 %collective-permute-done.7.refs_0_ = f32[200,128]{1,0:T(8,128)S(1)} collective-permute-done((f32[200,128]{1,0:T(8,128)S(1)}, f32[200,128]{1,0:T(8,128)S(1)}, u32[]{:S(2)}, u32[]{:S(2)}) %collective-permute-start.7) | collective-permute-done | bytes 102432 | tf_op jit(solution)/shard_map/ppermute | solution.py:770
  27.3 0.8 %shard_map.101.refs_1_ = f32[3,4,32,128]{3,2,1,0:T(8,128)} custom-call(f32[200,128]{1,0:T(8,128)S(1)} %collective-permute-done.7.refs_0_, f32[3,4,40,128]{3,2,1,0:T(8,128)S(1)} %get-tuple-element.48.grad.refs_1_.refs_2_, f32[3,4,40,128]{3,2,1,0:T(8,128)S(1)} %get-tuple-element.50.refs_2_.refs_3_, f32[3,2,40,128]{3,2,1,0:T(8,128)S(1)} %get-tuple-element.51.refs_3_.refs_4_, ...), custom_call_target="tpu_custom_call" | custom-call | tf_op jit(solution)/shard_map/pallas_call | solution.py:784
  28.1 2.3 %collective-permute-done.6.refs_0_ = f32[200,128]{1,0:T(8,128)S(1)} collective-permute-done((f32[200,128]{1,0:T(8,128)S(1)}, f32[200,128]{1,0:T(8,128)S(1)}, u32[]{:S(2)}, u32[]{:S(2)}) %collective-permute-start.6) | collective-permute-done | bytes 102432 | tf_op jit(solution)/shard_map/ppermute | solution.py:770
  30.4 0.8 %shard_map.102 = f32[3,4,32,128]{3,2,1,0:T(8,128)} custom-call(f32[200,128]{1,0:T(8,128)S(1)} %collective-permute-done.6.refs_0_, f32[3,4,32,128]{3,2,1,0:T(8,128)} %shard_map.101.refs_1_, f32[3,4,40,128]{3,2,1,0:T(8,128)S(1)} %get-tuple-element.48.grad.refs_1_.refs_2_, ...), custom_call_target="tpu_custom_call", output_to_operand_aliasing={{}: (1, {})} | custom-call | tf_op jit(solution)/shard_map/pallas_call | solution.py:784
  (3 shorter events, 0.0 us)
Async XLA Ops:
  1.9 15.4 %copy-start = (f32[1,9,4,64,128]{4,3,2,1,0:T(8,128)S(1)}, f32[1,9,4,64,128]{4,3,2,1,0:T(8,128)}, u32[]{:S(2)}) copy-start(f32[1,9,4,64,128]{4,3,2,1,0:T(8,128)} %param.8) | copy-start | bytes 3538948
  1.9 15.4 %copy-start.1 = (bf16[1,9,4,64,128]{4,3,2,1,0:T(8,128)(2,1)S(1)}, bf16[1,9,4,64,128]{4,3,2,1,0:T(8,128)(2,1)}, u32[]{:S(2)}) copy-start(bf16[1,9,4,64,128]{4,3,2,1,0:T(8,128)(2,1)} %param.10) | copy-start | bytes 1769476
  1.9 15.4 %copy-start.2 = (s32[1,4,4]{2,1,0:T(4,128)S(1)}, s32[1,4,4]{2,1,0:T(4,128)}, u32[]{:S(2)}) copy-start(s32[1,4,4]{2,1,0:T(4,128)} %refs_3_.1) | copy-start | bytes 196
  1.9 13.9 %collective-permute-start.2 = (f32[320,128]{1,0:T(8,128)S(1)}, f32[320,128]{1,0:T(8,128)S(1)}, u32[]{:S(2)}, u32[]{:S(2)}) collective-permute-start(f32[320,128]{1,0:T(8,128)S(1)} %get-tuple-element.31), channel_id=1, source_target_pairs={{0,1},{1,0},{2,3},{3,2},{4,5},{5,4},{6,7},{7,6},{8,9},{9,8},{10,11... | collective-permute-start | bytes 491528 | tf_op jit(solution)/shard_map/ppermute | solution.py:770
  3.5 12.3 %collective-permute-start.3 = (f32[320,128]{1,0:T(8,128)S(1)}, f32[320,128]{1,0:T(8,128)S(1)}, u32[]{:S(2)}, u32[]{:S(2)}) collective-permute-start(f32[320,128]{1,0:T(8,128)S(1)} %get-tuple-element.32), channel_id=1, source_target_pairs={{0,16},{1,2},{2,1},{3,4},{4,3},{5,6},{6,5},{7,8},{8,7},{9,10},{10,... | collective-permute-start | bytes 491528 | tf_op jit(solution)/shard_map/ppermute | solution.py:770
  7.1 11.7 %collective-permute-start = (f32[6,64,128]{2,1,0:T(8,128)S(1)}, f32[6,64,128]{2,1,0:T(8,128)S(1)}, u32[]{:S(2)}, u32[]{:S(2)}) collective-permute-start(f32[6,64,128]{2,1,0:T(8,128)S(1)} %get-tuple-element.28), channel_id=1, source_target_pairs={{0,16},{1,2},{2,1},{3,4},{4,3},{5,6},{6,5},{7,8},{8,7},{9,10},{10,... | collective-permute-start | bytes 589832 | tf_op jit(solution)/shard_map/ppermute | solution.py:770
  9.6 10.2 %collective-permute-start.1 = (f32[6,64,128]{2,1,0:T(8,128)S(1)}, f32[6,64,128]{2,1,0:T(8,128)S(1)}, u32[]{:S(2)}, u32[]{:S(2)}) collective-permute-start(f32[6,64,128]{2,1,0:T(8,128)S(1)} %get-tuple-element.29), channel_id=1, source_target_pairs={{0,1},{1,0},{2,3},{3,2},{4,5},{5,4},{6,7},{7,6},{8,9},{9,8},{10,11... | collective-permute-start | bytes 589832 | tf_op jit(solution)/shard_map/ppermute | solution.py:770
  15.8 1.4 %collective-permute-start.4 = (f32[264,128]{1,0:T(8,128)S(1)}, f32[264,128]{1,0:T(8,128)S(1)}, u32[]{:S(2)}, u32[]{:S(2)}) collective-permute-start(f32[264,128]{1,0:T(8,128)S(1)} %pad_maximum_fusion), channel_id=1, source_target_pairs={{0,16},{16,0},{1,17},{17,1},{2,18},{18,2},{3,19},{19,3},{4,20},{20... | collective-permute-start | bytes 405512 | tf_op jit(solution)/shard_map/ppermute | solution.py:849
  20.5 1.6 %collective-permute-start.5 = (f32[3,4,40,128]{3,2,1,0:T(8,128)S(1)}, f32[3,4,40,128]{3,2,1,0:T(8,128)S(1)}, u32[]{:S(2)}, u32[]{:S(2)}) collective-permute-start(f32[3,4,40,128]{3,2,1,0:T(8,128)S(1)} %get-tuple-element.44), channel_id=1, source_target_pairs={{0,16},{16,0},{1,17},{17,1},{2,18},{18,2},{3,19},{19,3},{4,20},{20... | collective-permute-start | bytes 737288 | tf_op jit(solution)/shard_map/ppermute | solution.py:874
  22.3 5.0 %collective-permute-start.7 = (f32[200,128]{1,0:T(8,128)S(1)}, f32[200,128]{1,0:T(8,128)S(1)}, u32[]{:S(2)}, u32[]{:S(2)}) collective-permute-start(f32[200,128]{1,0:T(8,128)S(1)} %get-tuple-element.47), channel_id=1, source_target_pairs={{0,1},{1,0},{2,3},{3,2},{4,5},{5,4},{6,7},{7,6},{8,9},{9,8},{10,11... | collective-permute-start | bytes 307208 | tf_op jit(solution)/shard_map/ppermute | solution.py:770
  23.9 6.5 %collective-permute-start.6 = (f32[200,128]{1,0:T(8,128)S(1)}, f32[200,128]{1,0:T(8,128)S(1)}, u32[]{:S(2)}, u32[]{:S(2)}) collective-permute-start(f32[200,128]{1,0:T(8,128)S(1)} %get-tuple-element.46), channel_id=1, source_target_pairs={{0,16},{1,2},{2,1},{3,4},{4,3},{5,6},{6,5},{7,8},{8,7},{9,10},{10,... | collective-permute-start | bytes 307208 | tf_op jit(solution)/shard_map/ppermute | solution.py:770

commit v10 on v9

--- a/solution.py
+++ b/solution.py
@@ -258,7 +258,7 @@
 
 
 def late_kernel(
-    state, source, buoyancy, lame, shear, cells, by_pair, by_next, st, push, coef, v2, s2, up, down
+    state, source, buoyancy, lame, shear, forward, cells, by_pair, by_next, st, push, coef, field, early, v2, s2, up, down
 ):
     width, size_y = state.shape[1], state.shape[2]
     last = width - 1
@@ -270,6 +270,11 @@
         for n, param in enumerate((buoyancy, lame, shear)):
             for x in range(width):
                 coef[n, x, here(row)] = c * param[x, here(row)]
+
+    for row in chunks(size_y):
+        for x in range(width):
+            for n in range(9):
+                field[n, x, here(row)] = forward[n, x, here(row)].astype(jnp.float32)
 
     def coefs(x, row):
         return [coef[n, x, here(row)] for n in range(3)]
@@ -325,6 +330,17 @@
                 value = value + push[2, 0, here(row)]
             down[comp, here(row)] = before
             down[3 + comp, here(row)] = value
+    for row in chunks(size_y):
+        for x in range(1, width):
+            if x < last:
+                moved = {c: one[x][c].at(row, ROWS) for c in range(9)}
+                values = imaged(moved, field, x, row)
+            else:
+                moved = [one[x][c].at(row, ROWS) * field[6 + c, x, here(row)] for c in VEL]
+                values = [None, None, add(moved)]
+            for n, value in enumerate(values):
+                if value is not None:
+                    early[n, x, here(row)] = value
     hand_out(by_pair, by_next, up, down)
 
 
@@ -338,7 +354,7 @@
 
 
 def imaged(moved, forward, x, row):
-    f = [forward[n, x, here(row)].astype(jnp.float32) for n in range(9)]
+    f = [forward[n, x, here(row)] for n in range(9)]
     trace = (moved[XX] + moved[YY] + moved[ZZ]) * (f[0] + f[1] + f[2])
     shear = add([moved[comp] * f[n] for n, comp in enumerate(STRESS)])
     density = add([moved[c] * f[6 + c] for c in VEL]) if VX in moved else None
@@ -357,7 +373,7 @@
     by_pair, by_next, *refs = refs
     if groups == 2:
         swapped, orientation, *refs = refs
-    state, st, coef, cells, push, forward, end, w, third, outer, parts, known, *refs = refs
+    state, st, coef, cells, push, forward, early, end, w, third, outer, parts, known, *refs = refs
     if groups == 2:
         weights, *refs = refs
     low, high, high_v, d_s, d_v, *classes = refs
@@ -475,14 +491,15 @@
     for row in chunks(size_y):
         for x in range(width):
             inner = 1 <= x < last
-            v, t = [one[x]], [one[x]] + [two[x]] * inner
-            if x:
-                v.append(two[x])
+            v = [two[x]] if x else [one[x]]
             if 2 <= x < last:
                 v.append({c: Plane(third, c, x) for c in VEL})
+            t = two[x] if inner else one[x]
             moved = {c: add([k[c].at(row, ROWS) for k in v]) for c in VEL}
-            moved |= {c: add([k[c].at(row, ROWS) for k in t]) for c in STRESS}
+            moved |= {c: t[c].at(row, ROWS) for c in STRESS}
             for n, value in enumerate(imaged(moved, forward, x, row)):
+                if inner or (x and n == 2):
+                    value = value + early[n, x, here(row)]
                 known[n, x, here(row)] = value
     if groups != 2:
         return
@@ -833,10 +850,24 @@
         space=HBM,
     )
     by_pair, by_next = both_ways(by_pair, by_next)
-    late_pair, late_next, st, push, coef = call(
+    late_pair, late_next, st, push, coef, forward, first_images = call(
         late_kernel,
-        [f32(6, *plane), f32(6, *plane), grid, f32(STEPS, width, *plane), f32(3, width, *plane)],
-        [*(in_hbm(a) for a in (state, source, buoyancy, lame_first, shear_modulus)), cells],
+        [
+            f32(6, *plane),
+            f32(6, *plane),
+            grid,
+            f32(STEPS, width, *plane),
+            f32(3, width, *plane),
+            grid,
+            f32(3, width, *plane),
+        ],
+        [
+            *(
+                in_hbm(a)
+                for a in (state, source, buoyancy, lame_first, shear_modulus, forward)
+            ),
+            cells,
+        ],
         [(3, 3, *plane), (6, *plane), (6, *plane), (6, *plane)],
     )
     late_pair, late_next = both_ways(late_pair, late_next)
@@ -855,7 +886,7 @@
     end, w, third, outer, parts, known, *weights = call(
         functools.partial(near_kernel, groups),
         [f32(2, 9, *plane), grid, three, f32(7, *plane), f32(4, 3, *plane), three, *outs],
-        [*args, state, st, coef, cells, push, forward],
+        [*args, state, st, coef, cells, push, forward, first_images],
         scratch,
         scalars,
     )

time: 31.4 us -> 31.4 us (level)
    ppermute x6, waiting for transfers between devices: 10.8 us -> 10.4 us  [both_ways(): out.append(lax.ppermute(array, ('shot', 'tile'), pairs))]
    unnamed x7 -> x5, local copies, waits for them, and re-layouts: 1.03 us -> 1.02 us
  transfers between devices with their start and end apart: 8 -> 8, of which waited for: 6 -> 6; matrix products, arithmetic and copies ran while one was open for 3% -> 3% of each run, Pallas kernels for 15% -> 16%
where the time goes in v10:
time: 31.4 us; the launch traced here: 31.2 us
  waiting for transfers between devices  13.3 us (42%)
  starting transfers between devices  8.08 us (26%)
  Pallas kernels  8.03 us (26%)
  local copies, waits for them, and re-layouts  1.03 us (3%)
  between operations  0.73 us (2%)
    ppermute x6, waiting for transfers between devices, both_ways(): out.append(lax.ppermute(array, ('shot', 'tile'), pairs))  10.4 us
    pallas_call x8, Pallas kernels, call(): pl.pallas_call(kernel, out_shape=outs, in_specs=specs, out_specs=jax.tree...  8.03 us
    ppermute x6, starting transfers between devices, both_ways(): out.append(lax.ppermute(array, ('shot', 'tile'), pairs))  7.94 us
    ppermute x1, waiting for transfers between devices, local(): received = lax.ppermute(give, 'shot', [(0, 1), (1, 0)])  1.5 us
    ppermute x1, waiting for transfers between devices, local(): swapped = lax.ppermute(swapped, 'shot', [(0, 1), (1, 0)])  1.34 us
    unnamed x5, local copies, waits for them, and re-layouts  1.02 us
  transfers between devices with their start and end apart: 8, of which 6 were waited for; matrix products, arithmetic and copies ran while one was open for 3% of the time, Pallas kernels for 16%

profile of v10, /device:TPU:8, one launch (start us, length us, event | category | flops | bytes accessed | tf_op | source)
XLA Modules:
  0.0 31.2 jit_solution(13499940205364633526)
XLA Ops:
  0.6 1.2 %shard_map.95 = (f32[320,128]{1,0:T(8,128)S(1)}, f32[320,128]{1,0:T(8,128)S(1)}, f32[64,128]{1,0:T(8,128)S(1)}, f32[8,128]{1,0:T(8,128)S(1)}) custom-call(s32[1,4,8]{2,1,0:T(4,128)} %bitcast.12, s32[1,4,4]{2,1,0:T(4,128)} %refs_3_.1, f32[9,4,64,128]{3,2,1,0:T(8,128)} %bitcast.6, bf16[3,4,64,128]{3,2,1,0:T(8,128)(2,1)} %bitcast.9, f32[4,64,128]{2,1,0:T(8,128)} %lame.1, ...), custom_call_target="tpu_custom_call" | custom-call | tf_op jit(solution)/shard_map/pallas_call | solution.py:801
  1.9 1.6 %collective-permute-start.2 = (f32[320,128]{1,0:T(8,128)S(1)}, f32[320,128]{1,0:T(8,128)S(1)}, u32[]{:S(2)}, u32[]{:S(2)}) collective-permute-start(f32[320,128]{1,0:T(8,128)S(1)} %get-tuple-element.33), channel_id=1, source_target_pairs={{0,1},{1,0},{2,3},{3,2},{4,5},{5,4},{6,7},{7,6},{8,9},{9,8},{10,11... | collective-permute-start | bytes 491528 | tf_op jit(solution)/shard_map/ppermute | solution.py:787
  3.4 1.4 %collective-permute-start.3 = (f32[320,128]{1,0:T(8,128)S(1)}, f32[320,128]{1,0:T(8,128)S(1)}, u32[]{:S(2)}, u32[]{:S(2)}) collective-permute-start(f32[320,128]{1,0:T(8,128)S(1)} %get-tuple-element.34), channel_id=1, source_target_pairs={{0,16},{1,2},{2,1},{3,4},{4,3},{5,6},{6,5},{7,8},{8,7},{9,10},{10,... | collective-permute-start | bytes 491528 | tf_op jit(solution)/shard_map/ppermute | solution.py:787
  4.8 0.0 copy-start
  4.8 0.0 copy-start.1
  4.8 2.6 %shard_map.96 = (f32[6,64,128]{2,1,0:T(8,128)S(1)}, f32[6,64,128]{2,1,0:T(8,128)S(1)}, f32[9,4,64,128]{3,2,1,0:T(8,128)S(1)}, f32[3,4,64,128]{3,2,1,0:T(8,128)S(...) custom-call(f32[9,4,64,128]{3,2,1,0:T(8,128)} %bitcast.7, ...), custom_call_target="tpu_custom_call" | custom-call | tf_op jit(solution)/shard_map/pallas_call | solution.py:801
  7.4 2.5 %collective-permute-start = (f32[6,64,128]{2,1,0:T(8,128)S(1)}, f32[6,64,128]{2,1,0:T(8,128)S(1)}, u32[]{:S(2)}, u32[]{:S(2)}) collective-permute-start(f32[6,64,128]{2,1,0:T(8,128)S(1)} %get-tuple-element.30), channel_id=1, source_target_pairs={{0,16},{1,2},{2,1},{3,4},{4,3},{5,6},{6,5},{7,8},{8,7},{9,10},{10,... | collective-permute-start | bytes 589832 | tf_op jit(solution)/shard_map/ppermute | solution.py:787
  9.9 0.0 collective-permute-start.1
  9.9 5.7 %collective-permute-done.2.refs_0_ = f32[320,128]{1,0:T(8,128)S(1)} collective-permute-done((f32[320,128]{1,0:T(8,128)S(1)}, f32[320,128]{1,0:T(8,128)S(1)}, u32[]{:S(2)}, u32[]{:S(2)}) %collective-permute-start.2) | collective-permute-done | bytes 163872 | tf_op jit(solution)/shard_map/ppermute | solution.py:787
  15.6 0.0 collective-permute-done.3.refs_1_
  15.7 0.1 collective-permute-start.4
  15.7 1.3 %collective-permute-done.4.refs_2_ = f32[264,128]{1,0:T(8,128)S(1)} collective-permute-done((f32[264,128]{1,0:T(8,128)S(1)}, f32[264,128]{1,0:T(8,128)S(1)}, u32[]{:S(2)}, u32[]{:S(2)}) %collective-permute-start.4) | collective-permute-done | bytes 135200 | tf_op jit(solution)/shard_map/ppermute | solution.py:880
  17.1 0.0 copy-done
  17.1 0.0 copy-done.1
  17.1 1.5 %shard_map.97 = (f32[2,9,64,128]{3,2,1,0:T(8,128)S(1)}, f32[9,4,64,128]{3,2,1,0:T(8,128)S(1)}, f32[3,4,64,128]{3,2,1,0:T(8,128)S(1)}, f32[7,64,128]{2,1,0:T(8,12...) custom-call(f32[320,128]{1,0:T(8,128)S(1)} %collective-permute-done.2.refs_0_, ...), custom_call_target="tpu_custom_call" | custom-call | tf_op jit(solution)/shard_map/pallas_call | solution.py:801
  18.6 0.0 collective-permute-done.refs_0_
  18.6 1.2 %collective-permute-done.1.refs_1_ = f32[6,64,128]{2,1,0:T(8,128)S(1)} collective-permute-done((f32[6,64,128]{2,1,0:T(8,128)S(1)}, f32[6,64,128]{2,1,0:T(8,128)S(1)}, u32[]{:S(2)}, u32[]{:S(2)}) %collective-permute-start.1) | collective-permute-done | bytes 196640 | tf_op jit(solution)/shard_map/ppermute | solution.py:787
  19.8 0.7 %shard_map.98 = (f32[9,4,64,128]{3,2,1,0:T(8,128)S(1)}, f32[3,4,40,128]{3,2,1,0:T(8,128)S(1)}, f32[3,4,40,128]{3,2,1,0:T(8,128)S(1)}) custom-call(f32[6,64,128]{2,1,0:T(8,128)S(1)} %collective-permute-done.refs_0_, f32[6,64,128]{2,1,0:T(8,128)S(1)} %collective-permute-done.1.refs_1_, f32[9,4,64,128]{3,2,1,0:T(8,128)S(1)} %get-tuple-element.32.refs_5_.refs_2_, ...), custom_call_target="tpu_custom_call" | custom-call | tf_op jit(solution)/shard_map/pallas_call | solution.py:801
  20.5 0.1 collective-permute-start.5
  20.6 1.5 %collective-permute-done.5.received = f32[3,4,40,128]{3,2,1,0:T(8,128)S(1)} collective-permute-done((f32[3,4,40,128]{3,2,1,0:T(8,128)S(1)}, f32[3,4,40,128]{3,2,1,0:T(8,128)S(1)}, u32[]{:S(2)}, u32[]{:S(2)}) %collective-permute-start.5) | collective-permute-done | bytes 245792 | tf_op jit(solution)/shard_map/ppermute | solution.py:905
  22.1 0.2 shard_map.99
  22.3 1.6 %collective-permute-start.7 = (f32[200,128]{1,0:T(8,128)S(1)}, f32[200,128]{1,0:T(8,128)S(1)}, u32[]{:S(2)}, u32[]{:S(2)}) collective-permute-start(f32[200,128]{1,0:T(8,128)S(1)} %get-tuple-element.51), channel_id=1, source_target_pairs={{0,1},{1,0},{2,3},{3,2},{4,5},{5,4},{6,7},{7,6},{8,9},{9,8},{10,11... | collective-permute-start | bytes 307208 | tf_op jit(solution)/shard_map/ppermute | solution.py:787
  23.8 0.9 %collective-permute-start.6 = (f32[200,128]{1,0:T(8,128)S(1)}, f32[200,128]{1,0:T(8,128)S(1)}, u32[]{:S(2)}, u32[]{:S(2)}) collective-permute-start(f32[200,128]{1,0:T(8,128)S(1)} %get-tuple-element.50), channel_id=1, source_target_pairs={{0,16},{1,2},{2,1},{3,4},{4,3},{5,6},{6,5},{7,8},{8,7},{9,10},{10,... | collective-permute-start | bytes 307208 | tf_op jit(solution)/shard_map/ppermute | solution.py:787
  24.8 1.0 %copy.12 = f32[1,9,4,64,128]{4,3,2,1,0:T(8,128)} copy(f32[1,9,4,64,128]{4,3,2,1,0:T(8,128)S(1)} %bitcast.5) | data formatting | bytes 2359296
  25.8 0.3 shard_map.100
  26.0 1.2 %collective-permute-done.7.refs_0_ = f32[200,128]{1,0:T(8,128)S(1)} collective-permute-done((f32[200,128]{1,0:T(8,128)S(1)}, f32[200,128]{1,0:T(8,128)S(1)}, u32[]{:S(2)}, u32[]{:S(2)}) %collective-permute-start.7) | collective-permute-done | bytes 102432 | tf_op jit(solution)/shard_map/ppermute | solution.py:787
  27.3 0.8 %shard_map.101.refs_1_ = f32[3,4,32,128]{3,2,1,0:T(8,128)} custom-call(f32[200,128]{1,0:T(8,128)S(1)} %collective-permute-done.7.refs_0_, f32[3,4,40,128]{3,2,1,0:T(8,128)S(1)} %get-tuple-element.52.grad.refs_1_.refs_2_, f32[3,4,40,128]{3,2,1,0:T(8,128)S(1)} %get-tuple-element.54.refs_2_.refs_3_, f32[3,2,40,128]{3,2,1,0:T(8,128)S(1)} %get-tuple-element.55.refs_3_.refs_4_, ...), custom_call_target="tpu_custom_call" | custom-call | tf_op jit(solution)/shard_map/pallas_call | solution.py:801
  28.1 2.3 %collective-permute-done.6.refs_0_ = f32[200,128]{1,0:T(8,128)S(1)} collective-permute-done((f32[200,128]{1,0:T(8,128)S(1)}, f32[200,128]{1,0:T(8,128)S(1)}, u32[]{:S(2)}, u32[]{:S(2)}) %collective-permute-start.6) | collective-permute-done | bytes 102432 | tf_op jit(solution)/shard_map/ppermute | solution.py:787
  30.4 0.8 %shard_map.102 = f32[3,4,32,128]{3,2,1,0:T(8,128)} custom-call(f32[200,128]{1,0:T(8,128)S(1)} %collective-permute-done.6.refs_0_, f32[3,4,32,128]{3,2,1,0:T(8,128)} %shard_map.101.refs_1_, f32[3,4,40,128]{3,2,1,0:T(8,128)S(1)} %get-tuple-element.52.grad.refs_1_.refs_2_, ...), custom_call_target="tpu_custom_call", output_to_operand_aliasing={{}: (1, {})} | custom-call | tf_op jit(solution)/shard_map/pallas_call | solution.py:801
  (3 shorter events, 0.0 us)
Async XLA Ops:
  1.9 13.8 %collective-permute-start.2 = (f32[320,128]{1,0:T(8,128)S(1)}, f32[320,128]{1,0:T(8,128)S(1)}, u32[]{:S(2)}, u32[]{:S(2)}) collective-permute-start(f32[320,128]{1,0:T(8,128)S(1)} %get-tuple-element.33), channel_id=1, source_target_pairs={{0,1},{1,0},{2,3},{3,2},{4,5},{5,4},{6,7},{7,6},{8,9},{9,8},{10,11... | collective-permute-start | bytes 491528 | tf_op jit(solution)/shard_map/ppermute | solution.py:787
  3.4 12.2 %collective-permute-start.3 = (f32[320,128]{1,0:T(8,128)S(1)}, f32[320,128]{1,0:T(8,128)S(1)}, u32[]{:S(2)}, u32[]{:S(2)}) collective-permute-start(f32[320,128]{1,0:T(8,128)S(1)} %get-tuple-element.34), channel_id=1, source_target_pairs={{0,16},{1,2},{2,1},{3,4},{4,3},{5,6},{6,5},{7,8},{8,7},{9,10},{10,... | collective-permute-start | bytes 491528 | tf_op jit(solution)/shard_map/ppermute | solution.py:787
  4.8 12.3 %copy-start = (f32[1,9,4,64,128]{4,3,2,1,0:T(8,128)S(1)}, f32[1,9,4,64,128]{4,3,2,1,0:T(8,128)}, u32[]{:S(2)}) copy-start(f32[1,9,4,64,128]{4,3,2,1,0:T(8,128)} %param.8) | copy-start | bytes 3538948
  4.8 12.3 %copy-start.1 = (s32[1,4,4]{2,1,0:T(4,128)S(1)}, s32[1,4,4]{2,1,0:T(4,128)}, u32[]{:S(2)}) copy-start(s32[1,4,4]{2,1,0:T(4,128)} %refs_3_.1) | copy-start | bytes 196
  7.4 11.2 %collective-permute-start = (f32[6,64,128]{2,1,0:T(8,128)S(1)}, f32[6,64,128]{2,1,0:T(8,128)S(1)}, u32[]{:S(2)}, u32[]{:S(2)}) collective-permute-start(f32[6,64,128]{2,1,0:T(8,128)S(1)} %get-tuple-element.30), channel_id=1, source_target_pairs={{0,16},{1,2},{2,1},{3,4},{4,3},{5,6},{6,5},{7,8},{8,7},{9,10},{10,... | collective-permute-start | bytes 589832 | tf_op jit(solution)/shard_map/ppermute | solution.py:787
  9.9 9.9 %collective-permute-start.1 = (f32[6,64,128]{2,1,0:T(8,128)S(1)}, f32[6,64,128]{2,1,0:T(8,128)S(1)}, u32[]{:S(2)}, u32[]{:S(2)}) collective-permute-start(f32[6,64,128]{2,1,0:T(8,128)S(1)} %get-tuple-element.31), channel_id=1, source_target_pairs={{0,1},{1,0},{2,3},{3,2},{4,5},{5,4},{6,7},{7,6},{8,9},{9,8},{10,11... | collective-permute-start | bytes 589832 | tf_op jit(solution)/shard_map/ppermute | solution.py:787
  15.7 1.4 %collective-permute-start.4 = (f32[264,128]{1,0:T(8,128)S(1)}, f32[264,128]{1,0:T(8,128)S(1)}, u32[]{:S(2)}, u32[]{:S(2)}) collective-permute-start(f32[264,128]{1,0:T(8,128)S(1)} %pad_maximum_fusion), channel_id=1, source_target_pairs={{0,16},{16,0},{1,17},{17,1},{2,18},{18,2},{3,19},{19,3},{4,20},{20... | collective-permute-start | bytes 405512 | tf_op jit(solution)/shard_map/ppermute | solution.py:880
  20.5 1.6 %collective-permute-start.5 = (f32[3,4,40,128]{3,2,1,0:T(8,128)S(1)}, f32[3,4,40,128]{3,2,1,0:T(8,128)S(1)}, u32[]{:S(2)}, u32[]{:S(2)}) collective-permute-start(f32[3,4,40,128]{3,2,1,0:T(8,128)S(1)} %get-tuple-element.48), channel_id=1, source_target_pairs={{0,16},{16,0},{1,17},{17,1},{2,18},{18,2},{3,19},{19,3},{4,20},{20... | collective-permute-start | bytes 737288 | tf_op jit(solution)/shard_map/ppermute | solution.py:905
  22.3 5.0 %collective-permute-start.7 = (f32[200,128]{1,0:T(8,128)S(1)}, f32[200,128]{1,0:T(8,128)S(1)}, u32[]{:S(2)}, u32[]{:S(2)}) collective-permute-start(f32[200,128]{1,0:T(8,128)S(1)} %get-tuple-element.51), channel_id=1, source_target_pairs={{0,1},{1,0},{2,3},{3,2},{4,5},{5,4},{6,7},{7,6},{8,9},{9,8},{10,11... | collective-permute-start | bytes 307208 | tf_op jit(solution)/shard_map/ppermute | solution.py:787
  23.8 6.5 %collective-permute-start.6 = (f32[200,128]{1,0:T(8,128)S(1)}, f32[200,128]{1,0:T(8,128)S(1)}, u32[]{:S(2)}, u32[]{:S(2)}) collective-permute-start(f32[200,128]{1,0:T(8,128)S(1)} %get-tuple-element.50), channel_id=1, source_target_pairs={{0,16},{1,2},{2,1},{3,4},{4,3},{5,6},{6,5},{7,8},{8,7},{9,10},{10,... | collective-permute-start | bytes 307208 | tf_op jit(solution)/shard_map/ppermute | solution.py:787
